TPU v7x, 256 devices: a whole 4x4x8 slice. The times are simulated.
256 devices in a mesh: ha: 32 (over x_lo, z, core), wa: 8 (over x_hi, y).
Axes of the slice: x: 4 (x_hi: 2, x_lo: 2; x = x_hi * 2 + x_lo), y: 4, z: 8, core: 2. Of those that a mesh axis runs over, the one named last changes fastest.
Arguments:
- features: bfloat16 [256, 262144], P('ha', 'wa'), may hold values from -6 to 6
- grad_out: bfloat16 [256, 262144], P('ha', 'wa'), may hold values from -6 to 6
- dw_weight: float32 [49, 256], replicated, may hold values from -0.875 to 0.875
- dw_bias: float32 [256], replicated, may hold values from -3 to 3
- ln_gain: float32 [256], replicated, may hold values from 0.5 to 1.5
- ln_bias: float32 [256], replicated, may hold values from -3 to 3
- w_in: bfloat16 [256, 1024], replicated, may hold values from -0.375 to 0.375
- b_in: float32 [1024], replicated, may hold values from -3 to 3
- w_out: bfloat16 [1024, 256], replicated, may hold values from -0.1875 to 0.1875
- b_out: float32 [256], replicated, may hold values from -3 to 3
- scale: float32 [256], replicated, may hold values from 0.3 to 1.5
Outputs:
- grad_features: bfloat16 [256, 262144], P('ha', 'wa')
- clip_dw_weight: float32 [49, 256], replicated
- clip_dw_bias: float32 [256], replicated
- clip_ln_gain: float32 [256], replicated
- clip_ln_bias: float32 [256], replicated
- clip_w_in: float32 [256, 1024], replicated
- clip_b_in: float32 [1024], replicated
- clip_w_out: float32 [1024, 256], replicated
- clip_b_out: float32 [256], replicated
- clip_scale: float32 [256], replicated
All inputs are finite; a program needn't handle non-finite values.
Results may differ from a plain program's by a relative error of at most 0.0075.
Values may be sent and summed in bfloat16 or wider, within the bound.
No kernel may reach another device: no remote copies, remote signals or barrier semaphores. Data moves between devices by JAX's collectives and lax.ppermute only.
A program may use at most 64 MiB of HBM per device.

v0:
```python
import math

import jax
import jax.numpy as jnp
from jax import lax
from jax.sharding import PartitionSpec as P

eps_norm = 1e-06
clip_bound = 500.0


def with_halo(x, sides, width):
    for axis, dim in sides:
        devices, length = (lax.axis_size(axis), x.shape[dim])
        up = [(i, (i + 1) % devices) for i in range(devices - 1)]
        down = [(j, i) for i, j in up]
        last = lax.slice_in_dim(x, length - width, length, axis=dim)
        leading = lax.slice_in_dim(x, 0, width, axis=dim)
        before = lax.ppermute(last, axis, up)
        after = lax.ppermute(leading, axis, down)
        x = jnp.concatenate([before, x, after], axis=dim)
    return x


def gelu_parts(pre):
    cdf = 0.5 * (1.0 + jax.scipy.special.erf(pre / math.sqrt(2.0)))
    pdf = jnp.exp(-0.5 * pre * pre) / math.sqrt(2.0 * math.pi)
    return (pre * cdf, cdf + pre * pdf)


def conv_rows(padded, weight, rows, cols, flip):
    total = jnp.zeros((rows, cols, padded.shape[2]), jnp.float32)
    for first in range(7):
        for second in range(7):
            if flip:
                window = padded[6 - first : 6 - first + rows, 6 - second : 6 - second + cols]
            else:
                window = padded[first : first + rows, second : second + cols]
            total = total + window.astype(jnp.float32) * weight[first * 7 + second]
    return total


def contract_rows(left, right):
    return lax.dot_general(
        left, right, (((0,), (0,)), ((), ())), preferred_element_type=jnp.float32
    )


def block_backward(
    padded, grad, dw_weight, dw_bias, ln_gain, ln_bias, w_in, b_in, w_out, b_out, scale
):
    rows, cols, chans = grad.shape
    conv = conv_rows(padded, dw_weight, rows, cols, False) + dw_bias
    center = conv - jnp.mean(conv, axis=-1, keepdims=True)
    inverse = lax.rsqrt(jnp.mean(center * center, axis=-1, keepdims=True) + eps_norm)
    normed = (center * inverse).reshape(rows * cols, chans)
    inverse = inverse.reshape(rows * cols, 1)
    lnout = (normed * ln_gain + ln_bias).astype(jnp.bfloat16)
    pre = jnp.dot(lnout, w_in, preferred_element_type=jnp.float32) + b_in
    act_full, slope = gelu_parts(pre)
    act = act_full.astype(jnp.bfloat16)
    branch = jnp.dot(act, w_out, preferred_element_type=jnp.float32) + b_out
    gflat = grad.reshape(rows * cols, chans).astype(jnp.float32)
    g_scale = jnp.sum(gflat * branch, axis=0)
    dbranch = (gflat * scale).astype(jnp.bfloat16)
    g_wout = contract_rows(act, dbranch)
    g_bout = jnp.sum(dbranch.astype(jnp.float32), axis=0)
    dact = lax.dot_general(
        dbranch, w_out, (((1,), (1,)), ((), ())), preferred_element_type=jnp.float32
    )
    dpre = (dact * slope).astype(jnp.bfloat16)
    g_win_t = contract_rows(dpre, lnout)
    g_bin = jnp.sum(dpre.astype(jnp.float32), axis=0)
    dln = lax.dot_general(dpre, w_in, (((1,), (1,)), ((), ())), preferred_element_type=jnp.float32)
    g_gain = jnp.sum(dln * normed, axis=0)
    g_lnb = jnp.sum(dln, axis=0)
    dnorm = dln * ln_gain
    dconv_flat = (
        dnorm
        - jnp.mean(dnorm, axis=-1, keepdims=True)
        - normed * jnp.mean(dnorm * normed, axis=-1, keepdims=True)
    ) * inverse
    dconv = dconv_flat.astype(jnp.bfloat16).reshape(rows, cols, chans)
    dconv_wide = dconv.astype(jnp.float32)
    g_dwb = jnp.sum(dconv_wide, axis=(0, 1))
    kernel_terms = []
    for first in range(7):
        for second in range(7):
            window = padded[first : first + rows, second : second + cols].astype(jnp.float32)
            kernel_terms.append(jnp.sum(dconv_wide * window, axis=(0, 1)))
    g_dw = jnp.stack(kernel_terms)
    return (dconv, (g_dw, g_dwb, g_gain, g_lnb, g_win_t, g_bin, g_wout, g_bout, g_scale))


def on_device(
    features, grad_out, dw_weight, dw_bias, ln_gain, ln_bias, w_in, b_in, w_out, b_out, scale
):
    chans = dw_weight.shape[1]
    rows = features.shape[0]
    cols = features.shape[1] // chans
    image = features.reshape(rows, cols, chans)
    grads3 = grad_out.reshape(rows, cols, chans)
    padded = with_halo(image, (("ha", 0), ("wa", 1)), 3)
    dconv, terms = block_backward(
        padded, grads3, dw_weight, dw_bias, ln_gain, ln_bias, w_in, b_in, w_out, b_out, scale
    )
    dpad = with_halo(dconv, (("ha", 0), ("wa", 1)), 3)
    result = conv_rows(dpad, dw_weight, rows, cols, True) + grads3.astype(jnp.float32)
    grad_features = result.astype(jnp.bfloat16).reshape(rows, cols * chans)
    g_dw, g_dwb, g_gain, g_lnb, g_win_t, g_bin, g_wout, g_bout, g_scale = terms
    summed = lax.psum(
        (g_dw, g_dwb, g_gain, g_lnb, g_bin, g_bout, g_scale, g_win_t, g_wout), ("ha", "wa")
    )
    squares = sum((jnp.sum(t * t) for t in summed))
    factor = jnp.minimum(1.0, clip_bound / jnp.sqrt(squares))
    s_dw, s_dwb, s_gain, s_lnb, s_bin, s_bout, s_scale, s_win_t, s_wout = summed
    full_win_t = factor * s_win_t
    full_wout = factor * s_wout
    return (
        grad_features,
        factor * s_dw,
        factor * s_dwb,
        factor * s_gain,
        factor * s_lnb,
        full_win_t.T,
        factor * s_bin,
        full_wout,
        factor * s_bout,
        factor * s_scale,
    )


def solution(mesh):
    return jax.shard_map(
        on_device,
        mesh=mesh,
        in_specs=(P("ha", "wa"), P("ha", "wa"), P(), P(), P(), P(), P(), P(), P(), P(), P()),
        out_specs=(P("ha", "wa"), P(), P(), P(), P(), P(), P(), P(), P(), P()),
        check_vma=False,
    )
```

profile of v0, /device:TPU:1, one launch (start us, length us, event | category | flops | bytes accessed | tf_op | source)
XLA Modules:
  0.0 459.0 jit_solution(16799210369752203266)
XLA Ops:
  7.3 1.5 fusion.190
  8.8 4.9 %collective-permute-start = (bf16[3,128,256]{2,1,0:T(8,128)(2,1)S(1)}, bf16[3,128,256]{2,1,0:T(8,128)(2,1)S(1)}, u32[]{:S(2)}, u32[]{:S(2)}) collective-permute-start(bf16[3,128,256]{2,1,0:T(8,128)(2,1)S(1)} %bitcast.207), channel_id=1, source_target_pairs={{0,8},{8,16},{16,24},{24,32},{32,40},{40,48},{48,56},{56,64},{64,7... | collective-permute-start | bytes 589832 | tf_op jit(solution)/shard_map/ppermute | solution.py:19
  13.7 0.7 copy.42
  14.4 1.9 collective-permute-start.1
  16.3 1.7 fusion.191
  18.0 1.3 reshape.136
  19.3 2.1 convert_reduce_fusion.2
  21.4 0.7 fusion.192
  22.4 1.0 constant_dynamic-update-slice_fusion.3
  23.3 0.6 fusion.188
  24.0 3.2 collective-permute-start.2
  27.2 1.3 collective-permute-start.3
  28.5 0.6 fusion.193
  29.1 1.2 reshape.138
  30.3 2.1 convert_element_type.503
  32.4 13.2 %fusion.186 = (f32[8,128]{1,0:T(8,128)S(1)}, f32[8,128,256]{2,1,0:T(8,128)S(1)}) fusion(f32[256]{0:T(256)} %param.14, f32[256]{0:T(256)} %bitcast.304, bf16[14,3,256]{2,1,0:T(4,128)(2,1)S(1)} %collective-permute-done.3, bf16[14,128,256]{2,1,0:T(8,128)(2,1)S(1)} %get-tuple-element.110, f32[256]{0:T(256)} %bitcast.306, f32[256]{0:T(256)} %bitcast.212, ...), kind=kLoop, calls=%fused_computation.387 | loop fusion | flops 71826432 | bytes 5734400 | tf_op jit(solution)/shard_map/reduce_sum | solution.py:54
  46.5 1.7 multiply_convert_fusion
  48.2 3.1 convert_reduce_fusion
  51.3 1.7 fusion.194
  53.1 1.5 fusion.136
  54.6 2.2 fusion.122
  56.7 1.1 fusion.126
  57.9 0.7 fusion.189
  58.6 1.7 fusion.195
  60.3 1.4 convert_reduce_fusion.1
  61.7 3.0 fusion.7
  64.7 1.2 fusion.127
  66.0 1.0 fusion.123
  67.0 1.4 fusion.128
  68.4 1.1 fusion.124
  69.5 1.3 fusion.129
  71.2 1.8 fusion.125
  73.0 4.1 stack.199
  77.1 84.3 %all-reduce = (f32[49,256]{1,0:T(8,128)S(1)}, f32[256]{0:T(256)S(1)}, f32[256]{0:T(256)S(1)}, f32[256]{0:T(256)S(1)}, f32[1024]{0:T(1024)S(1)}, /*index=5*/f32[256]{0:T(256)S(1)}, f32[256]{0:T(256)S(1)}) all-reduce(f32[49,256]{1,0:T(8,128)S(1)} %stack.199, ...), channel_id=1, replica_groups=mesh['ha'=32,'wa'=8] {'ha','wa'}, use_global_device_ids=true, to_apply=%region_53.0 | all-reduce | flops 14848 | bytes 118784 | tf_op jit(solution)/shard_map/psum | solution.py:111
  163.2 0.6 multiply_reduce_fusion.5
  163.9 3.4 collective-permute-start.4
  167.3 1.9 collective-permute-start.5
  169.2 0.7 multiply_reduce_fusion.7
  170.5 3.8 collective-permute-done.5
  174.3 1.3 collective-permute-start.6
  175.6 4.0 collective-permute-start.7
  185.6 11.2 %fusion.183 = bf16[1,8,128,256]{3,2,1,0:T(8,128)(2,1)S(1)} fusion(f32[8,128,256]{2,0,1:T(8,128)S(1)} %bitcast.203, f32[256]{0:T(256)} %bitcast.305, bf16[14,131,256]{2,1,0:T(8,128)(2,1)S(1)} %get-tuple-element.95, f32[256]{0:T(256)} %bitcast.307, f32[256]{0:T(256)S(1)} %bitcast.213, f32[256]{0:T(256)S(1)} %bitcast.215, ...), kind=kLoop, calls=%fused_computation.355 | loop fusion | flops 40370176 | bytes 24560640
  196.9 1.1 copy.29
  198.0 242.6 %all-reduce.4.cloned.1.call-done = (f32[1024,256]{1,0:T(8,128)}, f32[1024,256]{1,0:T(8,128)}) async-done(((f32[1024,256]{1,0:T(8,128)}, f32[1024,256]{1,0:T(8,128)}), (f32[1024,256]{1,0:T(8,128)}, f32[1024,256]{1,0:T(8,128)})) %all-reduce.4.cloned.1.call-update) | async-done | bytes 2097168 | tf_op jit(solution)/shard_map/psum | solution.py:111
  440.6 2.5 multiply_reduce_fusion
  445.6 2.3 broadcast_multiply_fusion
  450.2 0.6 broadcast_multiply_fusion.1
  450.9 1.3 copy.26
  (138 shorter events, 8.4 us)
Async XLA Ops:
  7.2 433.4 %all-reduce.4.cloned.1.call-start = ((), (), s32[]{:S(2)}) async-start(), calls=%async_computation | async-start | bytes 4194304 | tf_op jit(solution)/shard_map/psum | solution.py:111
  8.8 13.3 %collective-permute-start = (bf16[3,128,256]{2,1,0:T(8,128)(2,1)S(1)}, bf16[3,128,256]{2,1,0:T(8,128)(2,1)S(1)}, u32[]{:S(2)}, u32[]{:S(2)}) collective-permute-start(bf16[3,128,256]{2,1,0:T(8,128)(2,1)S(1)} %bitcast.207), channel_id=1, source_target_pairs={{0,8},{8,16},{16,24},{24,32},{32,40},{40,48},{48,56},{56,64},{64,7... | collective-permute-start | bytes 589832 | tf_op jit(solution)/shard_map/ppermute | solution.py:19
  14.4 8.0 %collective-permute-start.1 = (bf16[3,128,256]{2,1,0:T(8,128)(2,1)}, bf16[3,128,256]{2,1,0:T(8,128)(2,1)}, u32[]{:S(2)}, u32[]{:S(2)}) collective-permute-start(bf16[3,128,256]{2,1,0:T(8,128)(2,1)} %bitcast.196), channel_id=1, source_target_pairs={{8,0},{16,8},{24,16},{32,24},{40,32},{48,40},{56,48},{64,56},{72,6... | collective-permute-start | bytes 589832 | tf_op jit(solution)/shard_map/ppermute | solution.py:20
  24.0 8.4 %collective-permute-start.2 = (bf16[14,3,256]{2,1,0:T(4,128)(2,1)}, bf16[14,3,256]{2,1,0:T(4,128)(2,1)S(1)}, u32[]{:S(2)}, u32[]{:S(2)}) collective-permute-start(bf16[14,3,256]{2,1,0:T(4,128)(2,1)} %get-tuple-element.98), channel_id=1, source_target_pairs={{0,1},{1,2},{2,3},{3,4},{4,5},{5,6},{6,7},{8,9},{9,10},{10,11},{11... | collective-permute-start | bytes 64520 | tf_op jit(solution)/shard_map/ppermute | solution.py:19
  27.2 5.2 %collective-permute-start.3 = (bf16[14,3,256]{2,1,0:T(4,128)(2,1)S(1)}, bf16[14,3,256]{2,1,0:T(4,128)(2,1)S(1)}, u32[]{:S(2)}, u32[]{:S(2)}) collective-permute-start(bf16[14,3,256]{2,1,0:T(4,128)(2,1)S(1)} %get-tuple-element.99), channel_id=1, source_target_pairs={{1,0},{2,1},{3,2},{4,3},{5,4},{6,5},{7,6},{9,8},{10,9},{11,10},{12... | collective-permute-start | bytes 64520 | tf_op jit(solution)/shard_map/ppermute | solution.py:20
  70.8 114.4 %copy-start.5 = (f32[8,32768]{1,0:T(8,128)S(1)}, f32[8,32768]{1,0:T(8,128)}, u32[]{:S(2)}) copy-start(f32[8,32768]{1,0:T(8,128)} %convert_element_type.503) | copy-start | bytes 3145732
  70.8 114.4 %copy-start.9 = (f32[1,256]{1,0:T(1,128)S(1)}, f32[1,256]{1,0:T(1,128)}, u32[]{:S(2)}) copy-start(f32[1,256]{1,0:T(1,128)} %get-tuple-element.112) | copy-start | bytes 3076
  70.8 114.4 %copy-start.10 = (f32[1,256]{1,0:T(1,128)S(1)}, f32[1,256]{1,0:T(1,128)}, u32[]{:S(2)}) copy-start(f32[1,256]{1,0:T(1,128)} %get-tuple-element.113) | copy-start | bytes 3076
  70.8 114.4 %copy-start.11 = (f32[1,256]{1,0:T(1,128)S(1)}, f32[1,256]{1,0:T(1,128)}, u32[]{:S(2)}) copy-start(f32[1,256]{1,0:T(1,128)} %get-tuple-element.114) | copy-start | bytes 3076
  70.8 114.4 %copy-start.12 = (f32[1,256]{1,0:T(1,128)S(1)}, f32[1,256]{1,0:T(1,128)}, u32[]{:S(2)}) copy-start(f32[1,256]{1,0:T(1,128)} %get-tuple-element.115) | copy-start | bytes 3076
  70.9 114.4 %copy-start.13 = (f32[1,256]{1,0:T(1,128)S(1)}, f32[1,256]{1,0:T(1,128)}, u32[]{:S(2)}) copy-start(f32[1,256]{1,0:T(1,128)} %get-tuple-element.116) | copy-start | bytes 3076
  70.9 114.4 %copy-start.14 = (f32[1,256]{1,0:T(1,128)S(1)}, f32[1,256]{1,0:T(1,128)}, u32[]{:S(2)}) copy-start(f32[1,256]{1,0:T(1,128)} %get-tuple-element.117) | copy-start | bytes 3076
  70.9 114.4 %copy-start.15 = (f32[1,256]{1,0:T(1,128)S(1)}, f32[1,256]{1,0:T(1,128)}, u32[]{:S(2)}) copy-start(f32[1,256]{1,0:T(1,128)} %get-tuple-element.118) | copy-start | bytes 3076
  70.9 114.4 %copy-start.16 = (f32[1,256]{1,0:T(1,128)S(1)}, f32[1,256]{1,0:T(1,128)}, u32[]{:S(2)}) copy-start(f32[1,256]{1,0:T(1,128)} %get-tuple-element.119) | copy-start | bytes 3076
  70.9 114.4 %copy-start.17 = (f32[1,256]{1,0:T(1,128)S(1)}, f32[1,256]{1,0:T(1,128)}, u32[]{:S(2)}) copy-start(f32[1,256]{1,0:T(1,128)} %get-tuple-element.120) | copy-start | bytes 3076
  70.9 114.4 %copy-start.18 = (f32[1,256]{1,0:T(1,128)S(1)}, f32[1,256]{1,0:T(1,128)}, u32[]{:S(2)}) copy-start(f32[1,256]{1,0:T(1,128)} %get-tuple-element.121) | copy-start | bytes 3076
  70.9 114.4 %copy-start.19 = (f32[1,256]{1,0:T(1,128)S(1)}, f32[1,256]{1,0:T(1,128)}, u32[]{:S(2)}) copy-start(f32[1,256]{1,0:T(1,128)} %get-tuple-element.122) | copy-start | bytes 3076
  70.9 114.4 %copy-start.20 = (f32[1,256]{1,0:T(1,128)S(1)}, f32[1,256]{1,0:T(1,128)}, u32[]{:S(2)}) copy-start(f32[1,256]{1,0:T(1,128)} %get-tuple-element.123) | copy-start | bytes 3076
  70.9 114.4 %copy-start.21 = (f32[1,256]{1,0:T(1,128)S(1)}, f32[1,256]{1,0:T(1,128)}, u32[]{:S(2)}) copy-start(f32[1,256]{1,0:T(1,128)} %get-tuple-element.124) | copy-start | bytes 3076
  70.9 114.4 %copy-start.22 = (f32[1,256]{1,0:T(1,128)S(1)}, f32[1,256]{1,0:T(1,128)}, u32[]{:S(2)}) copy-start(f32[1,256]{1,0:T(1,128)} %get-tuple-element.125) | copy-start | bytes 3076
  71.0 114.4 %copy-start.23 = (f32[1,256]{1,0:T(1,128)S(1)}, f32[1,256]{1,0:T(1,128)}, u32[]{:S(2)}) copy-start(f32[1,256]{1,0:T(1,128)} %get-tuple-element.126) | copy-start | bytes 3076
  71.0 114.4 %copy-start.24 = (f32[1,256]{1,0:T(1,128)S(1)}, f32[1,256]{1,0:T(1,128)}, u32[]{:S(2)}) copy-start(f32[1,256]{1,0:T(1,128)} %get-tuple-element.127) | copy-start | bytes 3076
  71.0 114.4 %copy-start.25 = (f32[1,256]{1,0:T(1,128)S(1)}, f32[1,256]{1,0:T(1,128)}, u32[]{:S(2)}) copy-start(f32[1,256]{1,0:T(1,128)} %get-tuple-element.128) | copy-start | bytes 3076
  71.0 114.4 %copy-start.26 = (f32[1,256]{1,0:T(1,128)S(1)}, f32[1,256]{1,0:T(1,128)}, u32[]{:S(2)}) copy-start(f32[1,256]{1,0:T(1,128)} %get-tuple-element.129) | copy-start | bytes 3076
  71.0 114.4 %copy-start.27 = (f32[1,256]{1,0:T(1,128)S(1)}, f32[1,256]{1,0:T(1,128)}, u32[]{:S(2)}) copy-start(f32[1,256]{1,0:T(1,128)} %get-tuple-element.130) | copy-start | bytes 3076
  71.0 114.4 %copy-start.28 = (f32[1,256]{1,0:T(1,128)S(1)}, f32[1,256]{1,0:T(1,128)}, u32[]{:S(2)}) copy-start(f32[1,256]{1,0:T(1,128)} %get-tuple-element.131) | copy-start | bytes 3076
  71.0 114.4 %copy-start.29 = (f32[1,256]{1,0:T(1,128)S(1)}, f32[1,256]{1,0:T(1,128)}, u32[]{:S(2)}) copy-start(f32[1,256]{1,0:T(1,128)} %get-tuple-element.132) | copy-start | bytes 3076
  71.0 114.4 %copy-start.30 = (f32[1,256]{1,0:T(1,128)S(1)}, f32[1,256]{1,0:T(1,128)}, u32[]{:S(2)}) copy-start(f32[1,256]{1,0:T(1,128)} %get-tuple-element.133) | copy-start | bytes 3076
  71.0 114.4 %copy-start.31 = (f32[1,256]{1,0:T(1,128)S(1)}, f32[1,256]{1,0:T(1,128)}, u32[]{:S(2)}) copy-start(f32[1,256]{1,0:T(1,128)} %get-tuple-element.134) | copy-start | bytes 3076
  71.0 114.4 %copy-start.32 = (f32[1,256]{1,0:T(1,128)S(1)}, f32[1,256]{1,0:T(1,128)}, u32[]{:S(2)}) copy-start(f32[1,256]{1,0:T(1,128)} %get-tuple-element.135) | copy-start | bytes 3076
  71.1 114.4 %copy-start.33 = (f32[1,256]{1,0:T(1,128)S(1)}, f32[1,256]{1,0:T(1,128)}, u32[]{:S(2)}) copy-start(f32[1,256]{1,0:T(1,128)} %get-tuple-element.136) | copy-start | bytes 3076
  71.1 114.4 %copy-start.34 = (f32[1,256]{1,0:T(1,128)S(1)}, f32[1,256]{1,0:T(1,128)}, u32[]{:S(2)}) copy-start(f32[1,256]{1,0:T(1,128)} %get-tuple-element.137) | copy-start | bytes 3076
  71.1 114.4 %copy-start.35 = (f32[1,256]{1,0:T(1,128)S(1)}, f32[1,256]{1,0:T(1,128)}, u32[]{:S(2)}) copy-start(f32[1,256]{1,0:T(1,128)} %get-tuple-element.138) | copy-start | bytes 3076
  71.1 114.4 %copy-start.36 = (f32[1,256]{1,0:T(1,128)S(1)}, f32[1,256]{1,0:T(1,128)}, u32[]{:S(2)}) copy-start(f32[1,256]{1,0:T(1,128)} %get-tuple-element.139) | copy-start | bytes 3076
  71.1 114.4 %copy-start.37 = (f32[1,256]{1,0:T(1,128)S(1)}, f32[1,256]{1,0:T(1,128)}, u32[]{:S(2)}) copy-start(f32[1,256]{1,0:T(1,128)} %get-tuple-element.140) | copy-start | bytes 3076
  71.1 114.4 %copy-start.38 = (f32[1,256]{1,0:T(1,128)S(1)}, f32[1,256]{1,0:T(1,128)}, u32[]{:S(2)}) copy-start(f32[1,256]{1,0:T(1,128)} %get-tuple-element.141) | copy-start | bytes 3076
  71.1 114.4 %copy-start.39 = (f32[1,256]{1,0:T(1,128)S(1)}, f32[1,256]{1,0:T(1,128)}, u32[]{:S(2)}) copy-start(f32[1,256]{1,0:T(1,128)} %get-tuple-element.142) | copy-start | bytes 3076
  71.1 114.4 %copy-start.40 = (f32[1,256]{1,0:T(1,128)S(1)}, f32[1,256]{1,0:T(1,128)}, u32[]{:S(2)}) copy-start(f32[1,256]{1,0:T(1,128)} %get-tuple-element.143) | copy-start | bytes 3076
  71.1 114.4 %copy-start.41 = (f32[1,256]{1,0:T(1,128)S(1)}, f32[1,256]{1,0:T(1,128)}, u32[]{:S(2)}) copy-start(f32[1,256]{1,0:T(1,128)} %get-tuple-element.144) | copy-start | bytes 3076
  71.1 114.4 %copy-start.42 = (f32[1,256]{1,0:T(1,128)S(1)}, f32[1,256]{1,0:T(1,128)}, u32[]{:S(2)}) copy-start(f32[1,256]{1,0:T(1,128)} %get-tuple-element.145) | copy-start | bytes 3076
  71.2 114.4 %copy-start.43 = (f32[1,256]{1,0:T(1,128)S(1)}, f32[1,256]{1,0:T(1,128)}, u32[]{:S(2)}) copy-start(f32[1,256]{1,0:T(1,128)} %get-tuple-element.146) | copy-start | bytes 3076
  71.2 114.4 %copy-start.44 = (f32[1,256]{1,0:T(1,128)S(1)}, f32[1,256]{1,0:T(1,128)}, u32[]{:S(2)}) copy-start(f32[1,256]{1,0:T(1,128)} %get-tuple-element.147) | copy-start | bytes 3076
  71.2 114.4 %copy-start.45 = (f32[1,256]{1,0:T(1,128)S(1)}, f32[1,256]{1,0:T(1,128)}, u32[]{:S(2)}) copy-start(f32[1,256]{1,0:T(1,128)} %get-tuple-element.148) | copy-start | bytes 3076
  71.2 114.4 %copy-start.46 = (f32[1,256]{1,0:T(1,128)S(1)}, f32[1,256]{1,0:T(1,128)}, u32[]{:S(2)}) copy-start(f32[1,256]{1,0:T(1,128)} %get-tuple-element.149) | copy-start | bytes 3076
  163.9 6.6 %collective-permute-start.4 = (bf16[3,128,256]{2,1,0:T(8,128)(2,1)}, bf16[3,128,256]{2,1,0:T(8,128)(2,1)S(1)}, u32[]{:S(2)}, u32[]{:S(2)}) collective-permute-start(bf16[3,128,256]{2,1,0:T(8,128)(2,1)} %bitcast.209), channel_id=1, source_target_pairs={{0,8},{8,16},{16,24},{24,32},{32,40},{40,48},{48,56},{56,64},{64,7... | collective-permute-start | bytes 589832 | tf_op jit(solution)/shard_map/ppermute | solution.py:19
  167.3 7.0 %collective-permute-start.5 = (bf16[3,128,256]{2,1,0:T(8,128)(2,1)S(1)}, bf16[3,128,256]{2,1,0:T(8,128)(2,1)S(1)}, u32[]{:S(2)}, u32[]{:S(2)}) collective-permute-start(bf16[3,128,256]{2,1,0:T(8,128)(2,1)S(1)} %bitcast.208), channel_id=1, source_target_pairs={{8,0},{16,8},{24,16},{32,24},{40,32},{48,40},{56,48},{64,56},{72,6... | collective-permute-start | bytes 589832 | tf_op jit(solution)/shard_map/ppermute | solution.py:20
  174.3 10.4 %collective-permute-start.6 = (bf16[14,3,256]{2,1,0:T(4,128)(2,1)S(1)}, bf16[14,3,256]{2,1,0:T(4,128)(2,1)S(1)}, u32[]{:S(2)}, u32[]{:S(2)}) collective-permute-start(bf16[14,3,256]{2,1,0:T(4,128)(2,1)S(1)} %get-tuple-element.96), channel_id=1, source_target_pairs={{1,0},{2,1},{3,2},{4,3},{5,4},{6,5},{7,6},{9,8},{10,9},{11,10},{12... | collective-permute-start | bytes 64520 | tf_op jit(solution)/shard_map/ppermute | solution.py:20
  175.6 9.1 %collective-permute-start.7 = (bf16[14,3,256]{2,1,0:T(4,128)(2,1)S(1)}, bf16[14,3,256]{2,1,0:T(4,128)(2,1)S(1)}, u32[]{:S(2)}, u32[]{:S(2)}) collective-permute-start(bf16[14,3,256]{2,1,0:T(4,128)(2,1)S(1)} %get-tuple-element.97), channel_id=1, source_target_pairs={{0,1},{1,2},{2,3},{3,4},{4,5},{5,6},{6,7},{8,9},{9,10},{10,11},{11... | collective-permute-start | bytes 64520 | tf_op jit(solution)/shard_map/ppermute | solution.py:19
  (14 other events, 257.4 us)
Sparse Core Ops, SparseCore 0:
  180.3 260.2 all-reduce.3
where the time goes:
time: 461 us; the launch traced here: 459 us
  waiting for transfers between devices  246 us (53%)
  blocking collectives  84.3 us (18%)
  other arithmetic  55.8 us (12%)
  starting transfers between devices  22 us (5%)
  between operations  20.9 us (5%)
  local copies, waits for them, and re-layouts  16.9 us (4%)
  matrix products  12.7 us (3%)
    psum x1, waiting for transfers between devices, on_device(): lax.psum((g_dw, g_dwb, g_gain, g_lnb, g_bin, g_bout, g_scale, g_win_t, g_...  243 us
    psum x1, blocking collectives, on_device(): lax.psum((g_dw, g_dwb, g_gain, g_lnb, g_bin, g_bout, g_scale, g_win_t, g_...  84.3 us
    ppermute x4, starting transfers between devices, with_halo(): before = lax.ppermute(last, axis, up)  15.5 us
    reduce_sum x1, other arithmetic, block_backward(): center = conv - jnp.mean(conv, axis=-1, keepdims=True)  13.2 us
    unnamed x1, other arithmetic  11.2 us
    reduce_sum x8, other arithmetic, block_backward(): kernel_terms.append(jnp.sum(dconv_wide * window, axis=(0, 1)))  11.2 us
  transfers between devices with their start and end apart: 9, of which 2 were waited for; matrix products, arithmetic and copies ran while one was open for 6% of the time, Pallas kernels for 0%

commit v1 on v0

v1 whole, which is shorter than its diff:
```python
import math

import jax
import jax.numpy as jnp
from jax import lax
from jax.experimental import pallas as pl
from jax.experimental.pallas import tpu as pltpu
from jax.sharding import PartitionSpec as P

eps_norm = 1e-06
clip_bound = 500.0
F32, BF16 = jnp.float32, jnp.bfloat16
ROWS, COLS, C, HID = 8, 128, 256, 1024
PIX = ROWS * COLS
WIDE = COLS + 6
JB = 8
LIMIT = 60 * 1024 * 1024


def shift_rows(own, left, right, top, bottom, tall, shifted):
    def place(j, mid, at):
        tall[j, 8:16, :] = mid.astype(F32)
        tall[j, 5:8, :] = top[:, pl.ds(at, C)].astype(F32)
        tall[j, 16:19, :] = bottom[:, pl.ds(at, C)].astype(F32)
        for a in range(7):
            shifted[a, j] = tall[j, 5 + a : 13 + a, :]

    for k in range(3):
        place(k, left[:, k * C : (k + 1) * C], k * C)
        place(COLS + 3 + k, right[:, k * C : (k + 1) * C], (COLS + 3 + k) * C)

    def step(j, carry):
        mid = own[:, pl.ds(pl.multiple_of(j * C, C), C)]
        place(j + 3, mid, pl.multiple_of((j + 3) * C, C))
        return carry

    lax.fori_loop(0, COLS, step, 0, unroll=4)


def spread_weights(w_ref, spread):
    for k in range(49):
        spread[k] = jnp.broadcast_to(w_ref[k : k + 1, :], (8, C))


def conv_block(shifted, spread, first, lane):
    lanes = slice(lane * 128, lane * 128 + 128)
    acc = [None] * JB
    for a in range(7):
        taps = [spread[a * 7 + b, :, lanes] for b in range(7)]
        for t in range(JB + 6):
            x = shifted[a, first + t, :, lanes]
            for b in range(7):
                o = t - b
                if 0 <= o < JB:
                    term = x * taps[b]
                    acc[o] = term if acc[o] is None else acc[o] + term
    return acc


def fold(x):
    return jnp.sum(x.reshape(-1, 8, C), axis=0)


def main_kernel(
    own, left, right, top, bottom, grad, dww, dwb, gain, lnb, w_in, w_in_t, b_in, w_out_t, b_out, scale,
    dconv_out, pay,
    tall, shifted, spread, conv, normed, inv, lnout, lnout_t, grad_flat, grad_t, pre, dact, act, dpre, dcw, small,
    big,
):
    shift_rows(own, left, right, top, bottom, tall, shifted)
    spread_weights(dww, spread)

    def forward(n, carry):
        first = n * JB
        for lane in range(2):
            lanes = slice(lane * 128, lane * 128 + 128)
            for o, acc in enumerate(conv_block(shifted, spread, first, lane)):
                conv[first + o, :, lanes] = acc
        block = conv[pl.ds(first, JB)].reshape(JB * 8, C) + dwb[...]
        center = block - jnp.mean(block, axis=-1, keepdims=True)
        inverse = lax.rsqrt(jnp.mean(center * center, axis=-1, keepdims=True) + eps_norm)
        norm = center * inverse
        rows = pl.ds(pl.multiple_of(first * 8, 64), JB * 8)
        normed[rows, :] = norm
        inv[rows, :] = inverse
        lnout[rows, :] = (norm * gain[...] + lnb[...]).astype(BF16)
        for o in range(JB):
            at = pl.multiple_of((first + o) * C, C)
            g = grad[:, pl.ds(at, C)].astype(F32)
            grad_flat[pl.ds(pl.multiple_of((first + o) * 8, 8), 8), :] = g
        return carry

    lax.fori_loop(0, COLS // JB, forward, 0)

    CH = 256

    def mlp(n, carry):
        s_gain, s_lnb, s_g, s_dwb = carry
        rows = pl.ds(pl.multiple_of(n * CH, CH), CH)
        ln = lnout[rows, :]
        lnout_t[n, 0:C, :] = ln.astype(F32).T.astype(BF16)
        g = grad_flat[rows, :]
        grad_t[n] = g.T.astype(BF16)
        pre[...] = jnp.dot(ln, w_in[...], preferred_element_type=F32) + b_in[...]
        dbr = (g * scale[...]).astype(BF16)
        dact[...] = jnp.dot(dbr, w_out_t[...], preferred_element_type=F32)
        s_g = s_g + fold(g)

        def gelu(m, c):
            sub = pl.ds(pl.multiple_of(m * 16, 16), 16)
            out = pl.ds(pl.multiple_of(n * CH + m * 16, 16), 16)
            for q in range(4):
                lanes = slice(q * 256, q * 256 + 256)
                v = pre[sub, lanes]
                e = jnp.exp(v * v * -0.5)
                t = 1.0 / (1.0 + (0.3275911 / math.sqrt(2.0)) * jnp.abs(v))
                poly = 0.5 * 1.061405429 * t - 0.5 * 1.453152027
                poly = poly * t + 0.5 * 1.421413741
                poly = poly * t - 0.5 * 0.284496736
                poly = poly * t + 0.5 * 0.254829592
                tail = poly * t * e
                cdf = jnp.where(v < 0.0, tail, 1.0 - tail)
                act[out, lanes] = (v * cdf).astype(BF16)
                slope = cdf + v * (e * (1.0 / math.sqrt(2.0 * math.pi)))
                dpre[out, lanes] = (dact[sub, lanes] * slope).astype(BF16)
            return c

        lax.fori_loop(0, CH // 16, gelu, 0)
        dact[:, 0:C] = jnp.dot(dpre[rows, :], w_in_t[...], preferred_element_type=F32)

        def back(m, c):
            s_gain, s_lnb, s_dwb = c
            sub = pl.ds(pl.multiple_of(m * 64, 64), 64)
            out = pl.ds(pl.multiple_of(n * CH + m * 64, 64), 64)
            dln = dact[sub, 0:C]
            norm = normed[out, :]
            prod = dln * norm
            s_gain = s_gain + fold(prod)
            s_lnb = s_lnb + fold(dln)
            dn = dln * gain[...]
            m1 = jnp.mean(dn, axis=-1, keepdims=True)
            m2 = jnp.mean(dn * norm, axis=-1, keepdims=True)
            dc = ((dn - m1 - norm * m2) * inv[out, :]).astype(BF16)
            wide = dc.astype(F32)
            s_dwb = s_dwb + fold(wide)
            wide = wide.reshape(8, 8, C)
            j0 = n * (CH // 8) + m * 8
            dcw[pl.ds(j0, 8)] = wide
            for o in range(8):
                dconv_out[:, pl.ds(pl.multiple_of((j0 + o) * C, C), C)] = wide[o].astype(BF16)
            return s_gain, s_lnb, s_dwb

        s_gain, s_lnb, s_dwb = lax.fori_loop(0, CH // 64, back, (s_gain, s_lnb, s_dwb))
        return s_gain, s_lnb, s_g, s_dwb

    for n in range(PIX // CH):
        lnout_t[n, C:, :] = jnp.ones((16, CH), BF16)
    zero = jnp.zeros((8, C), F32)
    s_gain, s_lnb, s_g, s_dwb = lax.fori_loop(0, PIX // CH, mlp, (zero, zero, zero, zero))

    small[...] = jnp.zeros_like(small)
    down = lambda v: jnp.sum(v, axis=0, keepdims=True)
    sum_g = down(s_g)
    small[49:50, :] = down(s_dwb)
    small[50:51, :] = down(s_gain)
    small[51:52, :] = down(s_lnb)
    small[52:53, :] = sum_g * scale[...]

    pay[:, :, :, C:] = jnp.zeros((2, 128, 8, 128), BF16)
    s_scale = jnp.zeros((C, 1), F32)
    for q in range(4):
        lanes = slice(q * 256, q * 256 + 256)
        total = jnp.zeros((C + 16, 256), F32)
        for n in range(PIX // CH):
            part = slice(n * CH, (n + 1) * CH)
            total = total + jnp.dot(lnout_t[n], dpre[part, lanes], preferred_element_type=F32)
        small[54 + q : 55 + q, :] = total[C : C + 1]
        pay[0, q * 32 : q * 32 + 32, :, 0:C] = total[0:C].reshape(32, 8, C).astype(BF16)
    for q in range(4):
        lanes = slice(q * 256, q * 256 + 256)
        total = jnp.zeros((C, 256), F32)
        for n in range(PIX // CH):
            part = slice(n * CH, (n + 1) * CH)
            total = total + jnp.dot(grad_t[n], act[part, lanes], preferred_element_type=F32)
        big[...] = total
        s_scale = s_scale + jnp.sum(total * w_out_t[:, lanes].astype(F32), axis=1, keepdims=True)
        pay[1, q * 32 : q * 32 + 32, :, 0:C] = (
            (total.T * scale[...]).reshape(32, 8, C).astype(BF16)
        )
    wide_scale = jnp.broadcast_to(s_scale, (C, 128)).T
    small[53:54, :] = wide_scale[0:1, :] + b_out[...] * sum_g

    for lane in range(2):
        lanes = slice(lane * 128, lane * 128 + 128)
        for group in ((0, 1), (2, 3), (4, 5), (6,)):

            def taps(n, acc, group=group, lanes=lanes):
                first = n * JB
                d = [dcw[first + o, :, lanes] for o in range(JB)]
                acc = list(acc)
                for p, a in enumerate(group):
                    for t in range(JB + 6):
                        x = shifted[a, first + t, :, lanes]
                        for b in range(7):
                            o = t - b
                            if 0 <= o < JB:
                                acc[p * 7 + b] = acc[p * 7 + b] + d[o] * x
                return tuple(acc)

            none = jnp.zeros((8, 128), F32)
            acc = lax.fori_loop(0, COLS // JB, taps, (none,) * (7 * len(group)))
            for p, a in enumerate(group):
                for b in range(7):
                    k = a * 7 + b
                    small[k : k + 1, lanes] = down(acc[p * 7 + b])

    for k in range(8):
        for lane in range(2):
            part = small[k * 8 : k * 8 + 8, lane * 128 : lane * 128 + 128]
            pay[0, k * 2 + lane, :, C:] = part.astype(BF16)


def transposed_kernel(
    own, left, right, top, bottom, grad, dww, out, tall, shifted, spread
):
    shift_rows(own, left, right, top, bottom, tall, shifted)
    spread_weights(dww, spread)

    def step(n, carry):
        first = n * JB
        for lane in range(2):
            for o, acc in enumerate(conv_block(shifted, spread, first, lane)):
                at = pl.ds(pl.multiple_of((first + o) * C + lane * 128, 128), 128)
                out[:, at] = (acc + grad[:, at].astype(F32)).astype(BF16)
        return carry

    lax.fori_loop(0, COLS // JB, step, 0)


def finish_kernel(
    core, mine, other, o_dw, o_dwb, o_gain, o_lnb, o_win, o_bin, o_wout, o_bout, o_scale, small, win, wout
):
    even = core[0] == 0
    total = jnp.zeros((8, 256), F32)
    for q in range(4):
        for part in range(4):
            at = slice(q * 32 + part * 8, q * 32 + part * 8 + 8)
            a = mine[at, :, 0:C].astype(F32)
            b = other[at, :, 0:C].astype(F32)
            first = jnp.where(even, a, b)
            second = jnp.where(even, b, a)
            total = total + jnp.sum(first * first + second * second, axis=0)
            win[part * 64 : part * 64 + 64, q * 256 : q * 256 + 256] = first.reshape(64, C)
            row = q * 256 + part * 64
            wout[row : row + 64, :] = second.reshape(64, C)
    for k in range(8):
        for lane in range(2):
            a = mine[k * 2 + lane, :, C:].astype(F32)
            b = other[k * 2 + lane, :, C:].astype(F32)
            small[k * 8 : k * 8 + 8, lane * 128 : lane * 128 + 128] = jnp.where(even, a, b)
    rest = small[...]
    total = total + jnp.sum((rest * rest).reshape(8, 8, C), axis=0)
    squares = jnp.sum(jnp.sum(total, axis=1, keepdims=True), axis=0, keepdims=True)
    factor = jnp.minimum(1.0, clip_bound / jnp.sqrt(squares))
    o_win[...] = win[...] * factor
    o_wout[...] = wout[...] * factor
    o_dw[...] = small[0:49, :] * factor
    o_dwb[...] = small[49:50, :] * factor
    o_gain[...] = small[50:51, :] * factor
    o_lnb[...] = small[51:52, :] * factor
    o_bout[...] = small[52:53, :] * factor
    o_scale[...] = small[53:54, :] * factor
    for q in range(4):
        o_bin[:, q * 256 : q * 256 + 256] = small[54 + q : 55 + q, :] * factor


PARAMS = pltpu.CompilerParams(vmem_limit_bytes=LIMIT)
CONV_SCRATCH = (
    pltpu.VMEM((WIDE, 24, C), F32),
    pltpu.VMEM((7, WIDE, 8, C), F32),
    pltpu.VMEM((49, 8, C), F32),
)


def run_main(*operands):
    return pl.pallas_call(
        main_kernel,
        out_shape=(
            jax.ShapeDtypeStruct((ROWS, COLS * C), BF16),
            jax.ShapeDtypeStruct((2, 128, 8, 384), BF16),
        ),
        scratch_shapes=CONV_SCRATCH
        + (
            pltpu.VMEM((COLS, 8, C), F32),
            pltpu.VMEM((PIX, C), F32),
            pltpu.VMEM((PIX, 1), F32),
            pltpu.VMEM((PIX, C), BF16),
            pltpu.VMEM((4, C + 16, 256), BF16),
            pltpu.VMEM((PIX, C), F32),
            pltpu.VMEM((4, C, 256), BF16),
            pltpu.VMEM((256, HID), F32),
            pltpu.VMEM((256, HID), F32),
            pltpu.VMEM((PIX, HID), BF16),
            pltpu.VMEM((PIX, HID), BF16),
            pltpu.VMEM((COLS, 8, C), F32),
            pltpu.VMEM((64, C), F32),
            pltpu.VMEM((C, 256), F32),
        ),
        compiler_params=PARAMS,
        name="block_backward",
    )(*operands)


def run_transposed(*operands):
    return pl.pallas_call(
        transposed_kernel,
        out_shape=jax.ShapeDtypeStruct((ROWS, COLS * C), BF16),
        scratch_shapes=CONV_SCRATCH,
        compiler_params=PARAMS,
        name="transposed_conv",
    )(*operands)


def run_finish(core, mine, other):
    vec = jax.ShapeDtypeStruct((1, C), F32)
    vmem = pl.BlockSpec(memory_space=pltpu.VMEM)
    return pl.pallas_call(
        finish_kernel,
        in_specs=[pl.BlockSpec(memory_space=pltpu.SMEM), vmem, vmem],
        out_shape=(
            jax.ShapeDtypeStruct((49, C), F32), vec, vec, vec, jax.ShapeDtypeStruct((C, HID), F32),
            jax.ShapeDtypeStruct((1, HID), F32), jax.ShapeDtypeStruct((HID, C), F32), vec, vec,
        ),
        scratch_shapes=(
            pltpu.VMEM((64, C), F32), pltpu.VMEM((C, HID), F32), pltpu.VMEM((HID, C), F32),
        ),
        compiler_params=PARAMS,
        name="clip",
    )(core, mine, other)


def halo(x):
    up_w = [(i, i + 1) for i in range(lax.axis_size("wa") - 1)]
    up_h = [(i, i + 1) for i in range(lax.axis_size("ha") - 1)]
    left = lax.ppermute(x[:, -3 * C :], "wa", up_w)
    right = lax.ppermute(x[:, : 3 * C], "wa", [(j, i) for i, j in up_w])
    last = jnp.concatenate([left[5:], x[5:], right[5:]], axis=1)
    lead = jnp.concatenate([left[:3], x[:3], right[:3]], axis=1)
    top = lax.ppermute(last, "ha", up_h)
    bottom = lax.ppermute(lead, "ha", [(j, i) for i, j in up_h])
    return left, right, top, bottom


def sum_over_devices(pay):
    both = ("ha", "wa")
    pairs, wide = lax.axis_size("ha") // 2, lax.axis_size("wa")
    core = lax.rem(lax.axis_index("ha"), 2)
    swap = [(i, i ^ 1) for i in range(2 * pairs)]
    groups = [[(2 * i + c) * wide + w for i in range(pairs) for w in range(wide)] for c in range(2)]

    def exchange(x):
        return lax.all_to_all(x, both, 0, 0, axis_index_groups=groups, tiled=True)

    send = lax.dynamic_index_in_dim(pay, 1 - core, 0, keepdims=False)
    keep = lax.dynamic_index_in_dim(pay, core, 0, keepdims=False)
    half = (keep.astype(F32) + lax.ppermute(send, "ha", swap).astype(F32)).astype(BF16)
    total = jnp.sum(exchange(half).astype(F32), axis=0).astype(BF16)
    mine = exchange(jnp.broadcast_to(total[None], half.shape))
    return core, mine, lax.ppermute(mine, "ha", swap)


def on_device(
    features, grad_out, dw_weight, dw_bias, ln_gain, ln_bias, w_in, b_in, w_out, b_out, scale
):
    row = lambda v: v.reshape(1, -1)
    dconv, pay = run_main(
        features, *halo(features), grad_out, dw_weight, row(dw_bias), row(ln_gain), row(ln_bias),
        w_in, w_in.T, row(b_in), w_out.T, row(b_out), row(scale),
    )
    core, mine, other = sum_over_devices(pay)
    grad_features = run_transposed(dconv, *halo(dconv), grad_out, dw_weight[::-1])
    o_dw, o_dwb, o_gain, o_lnb, o_win, o_bin, o_wout, o_bout, o_scale = run_finish(
        core.reshape(1).astype(jnp.int32), mine, other
    )
    flat = lambda v: v.reshape(-1)
    return (
        grad_features, o_dw, flat(o_dwb), flat(o_gain), flat(o_lnb), o_win, flat(o_bin), o_wout,
        flat(o_bout), flat(o_scale),
    )


def solution(mesh):
    return jax.shard_map(
        on_device,
        mesh=mesh,
        in_specs=(P("ha", "wa"), P("ha", "wa"), P(), P(), P(), P(), P(), P(), P(), P(), P()),
        out_specs=(P("ha", "wa"), P(), P(), P(), P(), P(), P(), P(), P(), P()),
        check_vma=False,
    )
```

time: 461 us -> 159 us (0.34)
  waiting for transfers between devices: 246 us -> 46.5 us
  blocking collectives: 84.3 us -> 0 us
  other arithmetic: 55.8 us -> 2.85 us
  Pallas kernels: 0 us -> 39.8 us
  starting transfers between devices: 22 us -> 58.7 us
  between operations: 20.9 us -> 0.94 us
  matrix products: 12.7 us -> 0 us
  local copies, waits for them, and re-layouts: 16.9 us -> 9.68 us
    psum x1 -> x0, waiting for transfers between devices: 243 us -> none  [on_device(): lax.psum((g_dw, g_dwb, g_gain, g_lnb, g_bin, g_bout, g_scale, g_win_t, g_...]
    psum x1 -> x0, blocking collectives: 84.3 us -> none  [on_device(): lax.psum((g_dw, g_dwb, g_gain, g_lnb, g_bin, g_bout, g_scale, g_win_t, g_...]
    pallas_call x0 -> x3, Pallas kernels: none -> 39.8 us  [the longest x1 28.5 us: run_main(): pl.pallas_call(main_kernel, out_shape=(jax.ShapeDtypeStruct((ROWS, COLS *...]
    all_to_all x0 -> x2, waiting for transfers between devices: none -> 35.7 us  [exchange(): return lax.all_to_all(x, both, 0, 0, axis_index_groups=groups, tiled=True)]
    reduce_sum x20 -> x1, other arithmetic: 35.1 us -> 0.16 us  [sum_over_devices(): total = jnp.sum(exchange(half).astype(F32), axis=0).astype(BF16)]
    all_to_all x0 -> x2, starting transfers between devices: none -> 29 us  [exchange(): return lax.all_to_all(x, both, 0, 0, axis_index_groups=groups, tiled=True)]
    dot_general x6 -> x0, matrix products: 12.7 us -> none  [the longest x2 3.45 us: contract_rows(): lax.dot_general(left, right, (((0,), (0,)), ((), ())), preferred_element_...]
    unnamed x1 -> x0, other arithmetic: 11.2 us -> none
  transfers between devices with their start and end apart: 9 -> 12, of which waited for: 2 -> 6; matrix products, arithmetic and copies ran while one was open for 6% -> 4% of each run, Pallas kernels for 0% -> 5%
where the time goes in v1:
time: 159 us; the launch traced here: 158 us
  starting transfers between devices  58.7 us (37%)
  waiting for transfers between devices  46.5 us (29%)
  Pallas kernels  39.8 us (25%)
  local copies, waits for them, and re-layouts  9.68 us (6%)
  other arithmetic  2.85 us (2%)
    all_to_all x2, waiting for transfers between devices, exchange(): return lax.all_to_all(x, both, 0, 0, axis_index_groups=groups, tiled=True)  35.7 us
    all_to_all x2, starting transfers between devices, exchange(): return lax.all_to_all(x, both, 0, 0, axis_index_groups=groups, tiled=True)  29 us
    pallas_call x1, Pallas kernels, run_main(): pl.pallas_call(main_kernel, out_shape=(jax.ShapeDtypeStruct((ROWS, COLS *...  28.5 us
    ppermute x2, starting transfers between devices, halo(): top = lax.ppermute(last, 'ha', up_h)  9.45 us
    ppermute x2, waiting for transfers between devices, halo(): bottom = lax.ppermute(lead, 'ha', [(j, i) for i, j in up_h])  9.05 us
    pallas_call x1, Pallas kernels, run_transposed(): pl.pallas_call(transposed_kernel, out_shape=jax.ShapeDtypeStruct((ROWS, C...  8.1 us
    ppermute x2, starting transfers between devices, halo(): left = lax.ppermute(x[:, -3 * C:], 'wa', up_w)  7.27 us
    ppermute x1, starting transfers between devices, sum_over_devices(): return (core, mine, lax.ppermute(mine, 'ha', swap))  6.42 us
  transfers between devices with their start and end apart: 12, of which 6 were waited for; matrix products, arithmetic and copies ran while one was open for 4% of the time, Pallas kernels for 5%

profile of v1, /device:TPU:1, one launch (start us, length us, event | category | flops | bytes accessed | tf_op | source)
XLA Modules:
  0.0 158.4 jit_solution(10948498775509594319)
XLA Ops:
  0.7 0.8 fusion.4
  1.4 1.3 collective-permute-start.1
  2.7 0.0 copy-start.2
  2.7 4.8 %collective-permute-start = (bf16[8,768]{1,0:T(8,128)(2,1)S(1)}, bf16[8,768]{1,0:T(8,128)(2,1)S(1)}, u32[]{:S(2)}, u32[]{:S(2)}) collective-permute-start(bf16[8,768]{1,0:T(8,128)(2,1)S(1)} %get-tuple-element.39), channel_id=1, source_target_pairs={{0,1},{1,2},{2,3},{3,4},{4,5},{5,6},{6,7},{8,9},{9,10},{10,11},{11... | collective-permute-start | bytes 36872 | tf_op jit(solution)/shard_map/ppermute | solution.py:345
  7.5 1.4 fusion.3
  8.9 0.0 collective-permute-done.1.right
  9.0 0.0 copy-start.11
  9.0 0.0 collective-permute-done.left
  9.0 0.0 copy-start.12
  9.0 0.1 pad_maximum_fusion
  9.2 4.8 %collective-permute-start.2 = (bf16[3,34304]{1,0:T(4,128)(2,1)S(1)}, bf16[3,34304]{1,0:T(4,128)(2,1)S(1)}, u32[]{:S(2)}, u32[]{:S(2)}) collective-permute-start(bf16[3,34304]{1,0:T(4,128)(2,1)S(1)} %pad_maximum_fusion), channel_id=1, source_target_pairs={{0,8},{8,16},{16,24},{24,32},{32,40},{40,48},{48,56},{56,64},{64,7... | collective-permute-start | bytes 617480 | tf_op jit(solution)/shard_map/ppermute | solution.py:349
  14.0 0.1 pad_maximum_fusion.1
  14.1 1.9 %collective-permute-start.3 = (bf16[3,34304]{1,0:T(4,128)(2,1)S(1)}, bf16[3,34304]{1,0:T(4,128)(2,1)S(1)}, u32[]{:S(2)}, u32[]{:S(2)}) collective-permute-start(bf16[3,34304]{1,0:T(4,128)(2,1)S(1)} %pad_maximum_fusion.1), channel_id=1, source_target_pairs={{8,0},{16,8},{24,16},{32,24},{40,32},{48,40},{56,48},{64,56},{72,6... | collective-permute-start | bytes 617480 | tf_op jit(solution)/shard_map/ppermute | solution.py:350
  16.1 1.0 copy.22
  17.1 1.0 copy.21
  18.1 0.0 copy-done.12
  18.1 0.0 collective-permute-done.2.top
  18.1 3.9 %collective-permute-done.3.bottom = bf16[3,34304]{1,0:T(4,128)(2,1)S(1)} collective-permute-done((bf16[3,34304]{1,0:T(4,128)(2,1)S(1)}, bf16[3,34304]{1,0:T(4,128)(2,1)S(1)}, u32[]{:S(2)}, u32[]{:S(2)}) %collective-permute-start.3) | collective-permute-done | bytes 205856 | tf_op jit(solution)/shard_map/ppermute | solution.py:350
  21.9 0.7 copy-done.6
  22.6 28.5 %block_backward.1 = (bf16[8,32768]{1,0:T(8,128)(2,1)}, bf16[2,128,8,384]{3,2,1,0:T(8,128)(2,1)}) custom-call(bf16[8,32768]{1,0:T(8,128)(2,1)} %own.1, bf16[8,768]{1,0:T(8,128)(2,1)} %copy-done.12, bf16[8,768]{1,0:T(8,128)(2,1)} %copy-done.11, bf16[3,34304]{1,0:T(4,128)(2,1)} %copy-done.5, bf16[3,34304]{1,0:T(4,128)(2,1)} %copy-done.6, ...), custom_call_target="tpu_custom_call" | custom-call | tf_op jit(solution)/shard_map/block_backward/pallas_call | solution.py:286
  51.2 1.3 dynamic-slice_bitcast_fusion
  52.4 0.1 collective-permute-start.8
  52.6 1.3 collective-permute-start.5
  53.9 0.9 collective-permute-done.8
  54.8 2.2 %fusion = bf16[128,8,384]{2,1,0:T(8,128)(2,1)} fusion(bf16[128,8,384]{2,1,0:T(8,128)(2,1)S(1)} %collective-permute-done.8, bf16[2,128,8,384]{3,2,1,0:T(8,128)(2,1)} %get-tuple-element.22, s32[]{:T(128)S(6)} %select_n.7), kind=kLoop, calls=%fused_computation.1 | loop fusion | flops 1572864 | bytes 2359300 | tf_op jit(solution)/shard_map/convert_element_type | solution.py:366
  57.0 21.0 %all-to-all-start = ((bf16[128,8,384]{2,1,0:T(8,128)(2,1)}), bf16[128,8,384]{2,1,0:T(8,128)(2,1)S(1)}, u32[]{:S(2)}, u32[]{:S(2)}) async-start(bf16[128,8,384]{2,1,0:T(8,128)(2,1)} %fusion), calls=%async_computation | async-start | bytes 1572864 | tf_op jit(solution)/shard_map/all_to_all | solution.py:362
  78.0 0.2 fusion.1
  78.2 2.5 %collective-permute-start.4 = (bf16[8,768]{1,0:T(8,128)(2,1)S(1)}, bf16[8,768]{1,0:T(8,128)(2,1)S(1)}, u32[]{:S(2)}, u32[]{:S(2)}) collective-permute-start(bf16[8,768]{1,0:T(8,128)(2,1)S(1)} %get-tuple-element.35), channel_id=1, source_target_pairs={{0,1},{1,2},{2,3},{3,4},{4,5},{5,6},{6,7},{8,9},{9,10},{10,11},{11... | collective-permute-start | bytes 36872 | tf_op jit(solution)/shard_map/ppermute | solution.py:345
  80.7 0.0 collective-permute-done.5.right
  80.7 0.8 collective-permute-done.4.left
  81.5 19.5 %all-to-all-done = bf16[128,8,384]{2,1,0:T(8,128)(2,1)S(1)} async-done(((bf16[128,8,384]{2,1,0:T(8,128)(2,1)}), bf16[128,8,384]{2,1,0:T(8,128)(2,1)S(1)}, u32[]{:S(2)}, u32[]{:S(2)}) %all-to-all-start) | async-done | bytes 786464 | tf_op jit(solution)/shard_map/all_to_all | solution.py:362
  101.0 0.2 reduce_sum.12
  101.2 0.9 broadcast_in_dim.2
  102.1 8.0 %all-to-all-start.1 = ((bf16[128,8,384]{2,1,0:T(8,128)(2,1)}), bf16[128,8,384]{2,1,0:T(8,128)(2,1)S(1)}, u32[]{:S(2)}, u32[]{:S(2)}) async-start(bf16[128,8,384]{2,1,0:T(8,128)(2,1)} %broadcast_in_dim.2), calls=%async_computation.1 | async-start | bytes 1572864 | tf_op jit(solution)/shard_map/all_to_all | solution.py:362
  110.2 0.1 pad_maximum_fusion.2
  110.3 4.6 %collective-permute-start.6 = (bf16[3,34304]{1,0:T(4,128)(2,1)S(1)}, bf16[3,34304]{1,0:T(4,128)(2,1)S(1)}, u32[]{:S(2)}, u32[]{:S(2)}) collective-permute-start(bf16[3,34304]{1,0:T(4,128)(2,1)S(1)} %pad_maximum_fusion.2), channel_id=1, source_target_pairs={{0,8},{8,16},{16,24},{24,32},{32,40},{40,48},{48,56},{56,64},{64,7... | collective-permute-start | bytes 617480 | tf_op jit(solution)/shard_map/ppermute | solution.py:349
  115.0 16.2 %all-to-all-done.1.mine = bf16[128,8,384]{2,1,0:T(8,128)(2,1)S(1)} async-done(((bf16[128,8,384]{2,1,0:T(8,128)(2,1)}), bf16[128,8,384]{2,1,0:T(8,128)(2,1)S(1)}, u32[]{:S(2)}, u32[]{:S(2)}) %all-to-all-start.1) | async-done | bytes 786464 | tf_op jit(solution)/shard_map/all_to_all | solution.py:362
  131.2 6.4 %collective-permute-start.9 = (bf16[128,8,384]{2,1,0:T(8,128)(2,1)S(1)}, bf16[128,8,384]{2,1,0:T(8,128)(2,1)S(1)}, u32[]{:S(2)}, u32[]{:S(2)}) collective-permute-start(bf16[128,8,384]{2,1,0:T(8,128)(2,1)S(1)} %all-to-all-done.1.mine), channel_id=1, source_target_pairs={{0,8},{8,0},{16,24},{24,16},{32,40},{40,32},{48,56},{56,48},{64,72... | collective-permute-start | bytes 2359304 | tf_op jit(solution)/shard_map/ppermute | solution.py:369
  137.6 0.1 pad_maximum_fusion.3
  137.7 1.9 %collective-permute-start.7 = (bf16[3,34304]{1,0:T(4,128)(2,1)S(1)}, bf16[3,34304]{1,0:T(4,128)(2,1)S(1)}, u32[]{:S(2)}, u32[]{:S(2)}) collective-permute-start(bf16[3,34304]{1,0:T(4,128)(2,1)S(1)} %pad_maximum_fusion.3), channel_id=1, source_target_pairs={{8,0},{16,8},{24,16},{32,24},{40,32},{48,40},{56,48},{64,56},{72,6... | collective-permute-start | bytes 617480 | tf_op jit(solution)/shard_map/ppermute | solution.py:350
  139.6 0.7 rev.3.dww
  140.3 0.0 collective-permute-done.6.top
  140.3 5.2 %collective-permute-done.7.bottom = bf16[3,34304]{1,0:T(4,128)(2,1)S(1)} collective-permute-done((bf16[3,34304]{1,0:T(4,128)(2,1)S(1)}, bf16[3,34304]{1,0:T(4,128)(2,1)S(1)}, u32[]{:S(2)}, u32[]{:S(2)}) %collective-permute-start.7) | collective-permute-done | bytes 205856 | tf_op jit(solution)/shard_map/ppermute | solution.py:350
  145.5 0.7 copy-done.8
  146.2 8.1 %transposed_conv.1 = bf16[8,32768]{1,0:T(8,128)(2,1)} custom-call(bf16[8,32768]{1,0:T(8,128)(2,1)} %get-tuple-element.21.own, bf16[8,768]{1,0:T(8,128)(2,1)} %copy-done.13, bf16[8,768]{1,0:T(8,128)(2,1)} %copy-done.10, bf16[3,34304]{1,0:T(4,128)(2,1)} %copy-done.7, bf16[3,34304]{1,0:T(4,128)(2,1)} %copy-done.8, bf16[8,32768]{1,0:T(8,128)(2,1)} %grad.3, ...), custom_call_target="tpu_custom_call" | custom-call | tf_op jit(solution)/shard_map/transposed_conv/pallas_call | solution.py:315
  154.4 0.0 collective-permute-done.9.other
  154.4 0.9 copy-done.3
  155.3 3.2 %clip.1 = (f32[49,256]{1,0:T(8,128)}, f32[1,256]{1,0:T(1,128)}, f32[1,256]{1,0:T(1,128)}, f32[1,256]{1,0:T(1,128)}, f32[256,1024]{1,0:T(8,128)}, /*index=5*/f32[...) custom-call(s32[1]{0:T(128)} %bitcast.8.core, bf16[128,8,384]{2,1,0:T(8,128)(2,1)} %copy-done, ...), custom_call_target="tpu_custom_call" | custom-call | tf_op jit(solution)/shard_map/clip/pallas_call | solution.py:327
  (26 shorter events, 0.1 us)
Async XLA Ops:
  0.6 15.4 %copy-start.4 = (bf16[1024,256]{1,0:T(8,128)(2,1)S(1)}, bf16[1024,256]{1,0:T(8,128)(2,1)}, u32[]{:S(2)}) copy-start(bf16[1024,256]{1,0:T(8,128)(2,1)} %param.19) | copy-start | bytes 1572868
  1.4 7.5 %collective-permute-start.1 = (bf16[8,768]{1,0:T(8,128)(2,1)S(1)}, bf16[8,768]{1,0:T(8,128)(2,1)S(1)}, u32[]{:S(2)}, u32[]{:S(2)}) collective-permute-start(bf16[8,768]{1,0:T(8,128)(2,1)S(1)} %get-tuple-element.38), channel_id=1, source_target_pairs={{1,0},{2,1},{3,2},{4,3},{5,4},{6,5},{7,6},{9,8},{10,9},{11,10},{12... | collective-permute-start | bytes 36872 | tf_op jit(solution)/shard_map/ppermute | solution.py:346
  2.7 14.3 %copy-start.2 = (bf16[256,1024]{1,0:T(8,128)(2,1)S(1)}, bf16[256,1024]{1,0:T(8,128)(2,1)}, u32[]{:S(2)}) copy-start(bf16[256,1024]{1,0:T(8,128)(2,1)} %w_in.1) | copy-start | bytes 1572868
  2.7 6.2 %collective-permute-start = (bf16[8,768]{1,0:T(8,128)(2,1)S(1)}, bf16[8,768]{1,0:T(8,128)(2,1)S(1)}, u32[]{:S(2)}, u32[]{:S(2)}) collective-permute-start(bf16[8,768]{1,0:T(8,128)(2,1)S(1)} %get-tuple-element.39), channel_id=1, source_target_pairs={{0,1},{1,2},{2,3},{3,4},{4,5},{5,6},{6,7},{8,9},{9,10},{10,11},{11... | collective-permute-start | bytes 36872 | tf_op jit(solution)/shard_map/ppermute | solution.py:345
  9.0 9.1 %copy-start.11 = (bf16[8,768]{1,0:T(8,128)(2,1)}, bf16[8,768]{1,0:T(8,128)(2,1)S(1)}, u32[]{:S(2)}) copy-start(bf16[8,768]{1,0:T(8,128)(2,1)S(1)} %collective-permute-done.1.right) | copy-start | bytes 36868
  9.0 9.1 %copy-start.12 = (bf16[8,768]{1,0:T(8,128)(2,1)}, bf16[8,768]{1,0:T(8,128)(2,1)S(1)}, u32[]{:S(2)}) copy-start(bf16[8,768]{1,0:T(8,128)(2,1)S(1)} %collective-permute-done.left) | copy-start | bytes 36868
  9.2 8.9 %collective-permute-start.2 = (bf16[3,34304]{1,0:T(4,128)(2,1)S(1)}, bf16[3,34304]{1,0:T(4,128)(2,1)S(1)}, u32[]{:S(2)}, u32[]{:S(2)}) collective-permute-start(bf16[3,34304]{1,0:T(4,128)(2,1)S(1)} %pad_maximum_fusion), channel_id=1, source_target_pairs={{0,8},{8,16},{16,24},{24,32},{32,40},{40,48},{48,56},{56,64},{64,7... | collective-permute-start | bytes 617480 | tf_op jit(solution)/shard_map/ppermute | solution.py:349
  14.1 7.8 %collective-permute-start.3 = (bf16[3,34304]{1,0:T(4,128)(2,1)S(1)}, bf16[3,34304]{1,0:T(4,128)(2,1)S(1)}, u32[]{:S(2)}, u32[]{:S(2)}) collective-permute-start(bf16[3,34304]{1,0:T(4,128)(2,1)S(1)} %pad_maximum_fusion.1), channel_id=1, source_target_pairs={{8,0},{16,8},{24,16},{32,24},{40,32},{48,40},{56,48},{64,56},{72,6... | collective-permute-start | bytes 617480 | tf_op jit(solution)/shard_map/ppermute | solution.py:350
  18.1 3.9 %copy-start.5 = (bf16[3,34304]{1,0:T(4,128)(2,1)}, bf16[3,34304]{1,0:T(4,128)(2,1)S(1)}, u32[]{:S(2)}) copy-start(bf16[3,34304]{1,0:T(4,128)(2,1)S(1)} %collective-permute-done.2.top) | copy-start | bytes 617476
  21.9 0.7 copy-start.6
  51.2 1.4 copy-start.1
  52.4 2.4 %collective-permute-start.8 = (bf16[128,8,384]{2,1,0:T(8,128)(2,1)S(1)}, bf16[128,8,384]{2,1,0:T(8,128)(2,1)S(1)}, u32[]{:S(2)}, u32[]{:S(2)}) collective-permute-start(bf16[128,8,384]{2,1,0:T(8,128)(2,1)S(1)} %dynamic-slice_bitcast_fusion), channel_id=1, source_target_pairs={{0,8},{8,0},{16,24},{24,16},{32,40},{40,32},{48,56},{56,48},{64,72... | collective-permute-start | bytes 2359304 | tf_op jit(solution)/shard_map/ppermute | solution.py:366
  52.6 28.1 %collective-permute-start.5 = (bf16[8,768]{1,0:T(8,128)(2,1)S(1)}, bf16[8,768]{1,0:T(8,128)(2,1)S(1)}, u32[]{:S(2)}, u32[]{:S(2)}) collective-permute-start(bf16[8,768]{1,0:T(8,128)(2,1)S(1)} %get-tuple-element.34), channel_id=1, source_target_pairs={{1,0},{2,1},{3,2},{4,3},{5,4},{6,5},{7,6},{9,8},{10,9},{11,10},{12... | collective-permute-start | bytes 36872 | tf_op jit(solution)/shard_map/ppermute | solution.py:346
  57.0 44.0 %all-to-all-start = ((bf16[128,8,384]{2,1,0:T(8,128)(2,1)}), bf16[128,8,384]{2,1,0:T(8,128)(2,1)S(1)}, u32[]{:S(2)}, u32[]{:S(2)}) async-start(bf16[128,8,384]{2,1,0:T(8,128)(2,1)} %fusion), calls=%async_computation | async-start | bytes 1572864 | tf_op jit(solution)/shard_map/all_to_all | solution.py:362
  78.2 3.3 %collective-permute-start.4 = (bf16[8,768]{1,0:T(8,128)(2,1)S(1)}, bf16[8,768]{1,0:T(8,128)(2,1)S(1)}, u32[]{:S(2)}, u32[]{:S(2)}) collective-permute-start(bf16[8,768]{1,0:T(8,128)(2,1)S(1)} %get-tuple-element.35), channel_id=1, source_target_pairs={{0,1},{1,2},{2,3},{3,4},{4,5},{5,6},{6,7},{8,9},{9,10},{10,11},{11... | collective-permute-start | bytes 36872 | tf_op jit(solution)/shard_map/ppermute | solution.py:345
  80.7 21.4 %copy-start.10 = (bf16[8,768]{1,0:T(8,128)(2,1)}, bf16[8,768]{1,0:T(8,128)(2,1)S(1)}, u32[]{:S(2)}) copy-start(bf16[8,768]{1,0:T(8,128)(2,1)S(1)} %collective-permute-done.5.right) | copy-start | bytes 36868
  81.5 20.6 %copy-start.13 = (bf16[8,768]{1,0:T(8,128)(2,1)}, bf16[8,768]{1,0:T(8,128)(2,1)S(1)}, u32[]{:S(2)}) copy-start(bf16[8,768]{1,0:T(8,128)(2,1)S(1)} %collective-permute-done.4.left) | copy-start | bytes 36868
  101.2 38.5 %copy-start.9 = (f32[49,256]{1,0:T(8,128)S(1)}, f32[49,256]{1,0:T(8,128)}, u32[]{:S(2)}) copy-start(f32[49,256]{1,0:T(8,128)} %dww.1) | copy-start | bytes 150532
  102.1 29.0 %all-to-all-start.1 = ((bf16[128,8,384]{2,1,0:T(8,128)(2,1)}), bf16[128,8,384]{2,1,0:T(8,128)(2,1)S(1)}, u32[]{:S(2)}, u32[]{:S(2)}) async-start(bf16[128,8,384]{2,1,0:T(8,128)(2,1)} %broadcast_in_dim.2), calls=%async_computation.1 | async-start | bytes 1572864 | tf_op jit(solution)/shard_map/all_to_all | solution.py:362
  110.3 30.0 %collective-permute-start.6 = (bf16[3,34304]{1,0:T(4,128)(2,1)S(1)}, bf16[3,34304]{1,0:T(4,128)(2,1)S(1)}, u32[]{:S(2)}, u32[]{:S(2)}) collective-permute-start(bf16[3,34304]{1,0:T(4,128)(2,1)S(1)} %pad_maximum_fusion.2), channel_id=1, source_target_pairs={{0,8},{8,16},{16,24},{24,32},{32,40},{40,48},{48,56},{56,64},{64,7... | collective-permute-start | bytes 617480 | tf_op jit(solution)/shard_map/ppermute | solution.py:349
  131.2 23.2 %copy-start = (bf16[128,8,384]{2,1,0:T(8,128)(2,1)}, bf16[128,8,384]{2,1,0:T(8,128)(2,1)S(1)}, u32[]{:S(2)}) copy-start(bf16[128,8,384]{2,1,0:T(8,128)(2,1)S(1)} %all-to-all-done.1.mine) | copy-start | bytes 2359300
  131.2 23.2 %collective-permute-start.9 = (bf16[128,8,384]{2,1,0:T(8,128)(2,1)S(1)}, bf16[128,8,384]{2,1,0:T(8,128)(2,1)S(1)}, u32[]{:S(2)}, u32[]{:S(2)}) collective-permute-start(bf16[128,8,384]{2,1,0:T(8,128)(2,1)S(1)} %all-to-all-done.1.mine), channel_id=1, source_target_pairs={{0,8},{8,0},{16,24},{24,16},{32,40},{40,32},{48,56},{56,48},{64,72... | collective-permute-start | bytes 2359304 | tf_op jit(solution)/shard_map/ppermute | solution.py:369
  137.7 7.8 %collective-permute-start.7 = (bf16[3,34304]{1,0:T(4,128)(2,1)S(1)}, bf16[3,34304]{1,0:T(4,128)(2,1)S(1)}, u32[]{:S(2)}, u32[]{:S(2)}) collective-permute-start(bf16[3,34304]{1,0:T(4,128)(2,1)S(1)} %pad_maximum_fusion.3), channel_id=1, source_target_pairs={{8,0},{16,8},{24,16},{32,24},{40,32},{48,40},{56,48},{64,56},{72,6... | collective-permute-start | bytes 617480 | tf_op jit(solution)/shard_map/ppermute | solution.py:350
  140.3 5.2 %copy-start.7 = (bf16[3,34304]{1,0:T(4,128)(2,1)}, bf16[3,34304]{1,0:T(4,128)(2,1)S(1)}, u32[]{:S(2)}) copy-start(bf16[3,34304]{1,0:T(4,128)(2,1)S(1)} %collective-permute-done.6.top) | copy-start | bytes 617476
  145.5 0.7 copy-start.8
  154.4 0.9 copy-start.3

commit v2 on v1

--- a/solution.py
+++ b/solution.py
@@ -62,10 +62,10 @@
 
 
 def main_kernel(
-    own, left, right, top, bottom, grad, dww, dwb, gain, lnb, w_in, w_in_t, b_in, w_out_t, b_out, scale,
-    dconv_out, pay,
+    core, own, left, right, top, bottom, grad, dww, dwb, gain, lnb, w_in, w_in_t, b_in, w_out_t, b_out, scale,
+    dconv_out, keep, send,
     tall, shifted, spread, conv, normed, inv, lnout, lnout_t, grad_flat, grad_t, pre, dact, act, dpre, dcw, small,
-    big,
+    pay,
 ):
     shift_rows(own, left, right, top, bottom, tall, shifted)
     spread_weights(dww, spread)
@@ -182,7 +182,6 @@
         for n in range(PIX // CH):
             part = slice(n * CH, (n + 1) * CH)
             total = total + jnp.dot(grad_t[n], act[part, lanes], preferred_element_type=F32)
-        big[...] = total
         s_scale = s_scale + jnp.sum(total * w_out_t[:, lanes].astype(F32), axis=1, keepdims=True)
         pay[1, q * 32 : q * 32 + 32, :, 0:C] = (
             (total.T * scale[...]).reshape(32, 8, C).astype(BF16)
@@ -218,6 +217,8 @@
         for lane in range(2):
             part = small[k * 8 : k * 8 + 8, lane * 128 : lane * 128 + 128]
             pay[0, k * 2 + lane, :, C:] = part.astype(BF16)
+    keep[...] = pay[core[0]]
+    send[...] = pay[1 - core[0]]
 
 
 def transposed_kernel(
@@ -287,8 +288,11 @@
         main_kernel,
         out_shape=(
             jax.ShapeDtypeStruct((ROWS, COLS * C), BF16),
-            jax.ShapeDtypeStruct((2, 128, 8, 384), BF16),
+            jax.ShapeDtypeStruct((128, 8, 384), BF16),
+            jax.ShapeDtypeStruct((128, 8, 384), BF16),
         ),
+        in_specs=[pl.BlockSpec(memory_space=pltpu.SMEM)]
+        + [pl.BlockSpec(memory_space=pltpu.VMEM)] * (len(operands) - 1),
         scratch_shapes=CONV_SCRATCH
         + (
             pltpu.VMEM((COLS, 8, C), F32),
@@ -304,7 +308,7 @@
             pltpu.VMEM((PIX, HID), BF16),
             pltpu.VMEM((COLS, 8, C), F32),
             pltpu.VMEM((64, C), F32),
-            pltpu.VMEM((C, 256), F32),
+            pltpu.VMEM((2, 128, 8, 384), BF16),
         ),
         compiler_params=PARAMS,
         name="block_backward",
@@ -351,36 +355,32 @@
     return left, right, top, bottom
 
 
-def sum_over_devices(pay):
-    both = ("ha", "wa")
-    pairs, wide = lax.axis_size("ha") // 2, lax.axis_size("wa")
-    core = lax.rem(lax.axis_index("ha"), 2)
-    swap = [(i, i ^ 1) for i in range(2 * pairs)]
-    groups = [[(2 * i + c) * wide + w for i in range(pairs) for w in range(wide)] for c in range(2)]
-
-    def exchange(x):
-        return lax.all_to_all(x, both, 0, 0, axis_index_groups=groups, tiled=True)
-
-    send = lax.dynamic_index_in_dim(pay, 1 - core, 0, keepdims=False)
-    keep = lax.dynamic_index_in_dim(pay, core, 0, keepdims=False)
-    half = (keep.astype(F32) + lax.ppermute(send, "ha", swap).astype(F32)).astype(BF16)
-    total = jnp.sum(exchange(half).astype(F32), axis=0).astype(BF16)
-    mine = exchange(jnp.broadcast_to(total[None], half.shape))
-    return core, mine, lax.ppermute(mine, "ha", swap)
-
-
 def on_device(
     features, grad_out, dw_weight, dw_bias, ln_gain, ln_bias, w_in, b_in, w_out, b_out, scale
 ):
     row = lambda v: v.reshape(1, -1)
-    dconv, pay = run_main(
-        features, *halo(features), grad_out, dw_weight, row(dw_bias), row(ln_gain), row(ln_bias),
-        w_in, w_in.T, row(b_in), w_out.T, row(b_out), row(scale),
+    both = ("ha", "wa")
+    pairs, wide = lax.axis_size("ha") // 2, lax.axis_size("wa")
+    core = lax.rem(lax.axis_index("ha"), 2).reshape(1).astype(jnp.int32)
+    swap = [(i, i ^ 1) for i in range(2 * pairs)]
+    groups = [[(2 * i + c) * wide + w for i in range(pairs) for w in range(wide)] for c in range(2)]
+
+    def exchange(x):
+        return lax.all_to_all(x, both, 0, 0, axis_index_groups=groups, tiled=True)
+
+    dconv, keep, send = run_main(
+        core, features, *halo(features), grad_out, dw_weight, row(dw_bias), row(ln_gain),
+        row(ln_bias), w_in, w_in.T, row(b_in), w_out.T, row(b_out), row(scale),
     )
-    core, mine, other = sum_over_devices(pay)
+    half = (keep.astype(F32) + lax.ppermute(send, "ha", swap).astype(F32)).astype(BF16)
+    terms = exchange(half)
     grad_features = run_transposed(dconv, *halo(dconv), grad_out, dw_weight[::-1])
+    terms, grad_features = lax.optimization_barrier((terms, grad_features))
+    total = jnp.sum(terms.astype(F32), axis=0).astype(BF16)
+    mine = exchange(jnp.broadcast_to(total[None], half.shape))
+    other = lax.ppermute(mine, "ha", swap)
     o_dw, o_dwb, o_gain, o_lnb, o_win, o_bin, o_wout, o_bout, o_scale = run_finish(
-        core.reshape(1).astype(jnp.int32), mine, other
+        core, mine, other
     )
     flat = lambda v: v.reshape(-1)
     return (

time: 159 us -> 163 us (1.025)
  blocking collectives: 0 us -> 36.9 us
  waiting for transfers between devices: 46.5 us -> 24.5 us
  starting transfers between devices: 58.7 us -> 48.6 us
    all_to_all x0 -> x1, blocking collectives: none -> 36.9 us  [exchange(): return lax.all_to_all(x, both, 0, 0, axis_index_groups=groups, tiled=True)]
    all_to_all x2 -> x1, waiting for transfers between devices: 35.7 us -> 0.01 us  [exchange(): return lax.all_to_all(x, both, 0, 0, axis_index_groups=groups, tiled=True)]
    ppermute x2, waiting for transfers between devices: 9.05 us -> 21.9 us  [halo(): bottom = lax.ppermute(lead, 'ha', [(j, i) for i, j in up_h])]
    all_to_all x2 -> x1, starting transfers between devices: 29 us -> 23.3 us  [exchange(): return lax.all_to_all(x, both, 0, 0, axis_index_groups=groups, tiled=True)]
    ppermute x2, starting transfers between devices: 6.51 us -> 1.29 us  [the longest x1 1.2 us: on_device(): other = lax.ppermute(mine, 'ha', swap)]
    ppermute x2, starting transfers between devices: 7.27 us -> 9.25 us  [halo(): left = lax.ppermute(x[:, -3 * C:], 'wa', up_w)]
  transfers between devices with their start and end apart: 12 -> 11, of which waited for: 6 -> 4; matrix products, arithmetic and copies ran while one was open for 4% -> 4% of each run, Pallas kernels for 5% -> 5%
where the time goes in v2:
time: 163 us; the launch traced here: 162 us
  starting transfers between devices  48.6 us (30%)
  Pallas kernels  39.8 us (24%)
  blocking collectives  36.9 us (23%)
  waiting for transfers between devices  24.5 us (15%)
  local copies, waits for them, and re-layouts  9.55 us (6%)
  other arithmetic  1.72 us (1%)
    all_to_all x1, blocking collectives, exchange(): return lax.all_to_all(x, both, 0, 0, axis_index_groups=groups, tiled=True)  36.9 us
    pallas_call x1, Pallas kernels, run_main(): pl.pallas_call(main_kernel, out_shape=(jax.ShapeDtypeStruct((ROWS, COLS *...  28.5 us
    all_to_all x1, starting transfers between devices, exchange(): return lax.all_to_all(x, both, 0, 0, axis_index_groups=groups, tiled=True)  23.3 us
    ppermute x2, waiting for transfers between devices, halo(): bottom = lax.ppermute(lead, 'ha', [(j, i) for i, j in up_h])  21.9 us
    ppermute x2, starting transfers between devices, halo(): left = lax.ppermute(x[:, -3 * C:], 'wa', up_w)  9.25 us
    ppermute x2, starting transfers between devices, halo(): top = lax.ppermute(last, 'ha', up_h)  8.21 us
    pallas_call x1, Pallas kernels, run_transposed(): pl.pallas_call(transposed_kernel, out_shape=jax.ShapeDtypeStruct((ROWS, C...  8.1 us
    unnamed x30, local copies, waits for them, and re-layouts  4.42 us
  transfers between devices with their start and end apart: 11, of which 4 were waited for; matrix products, arithmetic and copies ran while one was open for 4% of the time, Pallas kernels for 5%

profile of v2, /device:TPU:1, one launch (start us, length us, event | category | flops | bytes accessed | tf_op | source)
XLA Modules:
  0.0 161.9 jit_solution(5483056158546361732)
XLA Ops:
  0.6 0.7 fusion.3
  1.4 1.3 collective-permute-start.1
  2.7 0.0 copy-start.4
  2.7 4.8 %collective-permute-start = (bf16[8,768]{1,0:T(8,128)(2,1)S(1)}, bf16[8,768]{1,0:T(8,128)(2,1)S(1)}, u32[]{:S(2)}, u32[]{:S(2)}) collective-permute-start(bf16[8,768]{1,0:T(8,128)(2,1)S(1)} %get-tuple-element.45), channel_id=1, source_target_pairs={{0,1},{1,2},{2,3},{3,4},{4,5},{5,6},{6,7},{8,9},{9,10},{10,11},{11... | collective-permute-start | bytes 36872 | tf_op jit(solution)/shard_map/ppermute | solution.py:349
  7.5 1.4 fusion.2
  8.9 0.0 collective-permute-done.1.right
  8.9 0.0 copy-start.10
  8.9 0.0 collective-permute-done.left
  8.9 0.0 copy-start.11
  9.0 0.0 copy-start.1
  9.0 0.1 pad_maximum_fusion
  9.1 5.0 %collective-permute-start.2 = (bf16[3,34304]{1,0:T(4,128)(2,1)S(1)}, bf16[3,34304]{1,0:T(4,128)(2,1)S(1)}, u32[]{:S(2)}, u32[]{:S(2)}) collective-permute-start(bf16[3,34304]{1,0:T(4,128)(2,1)S(1)} %pad_maximum_fusion), channel_id=1, source_target_pairs={{0,8},{8,16},{16,24},{24,32},{32,40},{40,48},{48,56},{56,64},{64,7... | collective-permute-start | bytes 617480 | tf_op jit(solution)/shard_map/ppermute | solution.py:353
  14.1 0.1 pad_maximum_fusion.1
  14.2 1.9 %collective-permute-start.3 = (bf16[3,34304]{1,0:T(4,128)(2,1)S(1)}, bf16[3,34304]{1,0:T(4,128)(2,1)S(1)}, u32[]{:S(2)}, u32[]{:S(2)}) collective-permute-start(bf16[3,34304]{1,0:T(4,128)(2,1)S(1)} %pad_maximum_fusion.1), channel_id=1, source_target_pairs={{8,0},{16,8},{24,16},{32,24},{40,32},{48,40},{56,48},{64,56},{72,6... | collective-permute-start | bytes 617480 | tf_op jit(solution)/shard_map/ppermute | solution.py:354
  16.1 1.0 copy.22
  17.2 1.0 copy.21
  18.2 0.0 collective-permute-done.2.top
  18.2 3.8 %collective-permute-done.3.bottom = bf16[3,34304]{1,0:T(4,128)(2,1)S(1)} collective-permute-done((bf16[3,34304]{1,0:T(4,128)(2,1)S(1)}, bf16[3,34304]{1,0:T(4,128)(2,1)S(1)}, u32[]{:S(2)}, u32[]{:S(2)}) %collective-permute-start.3) | collective-permute-done | bytes 205856 | tf_op jit(solution)/shard_map/ppermute | solution.py:354
  22.0 0.7 copy-done.6
  22.7 28.5 %block_backward.1 = (bf16[8,32768]{1,0:T(8,128)(2,1)}, bf16[128,8,384]{2,1,0:T(8,128)(2,1)}, bf16[128,8,384]{2,1,0:T(8,128)(2,1)}) custom-call(s32[1]{0:T(128)} %bitcast.core, bf16[8,32768]{1,0:T(8,128)(2,1)} %own.1, bf16[8,768]{1,0:T(8,128)(2,1)} %copy-done.11, bf16[8,768]{1,0:T(8,128)(2,1)} %copy-done.10, bf16[3,34304]{1,0:T(4,128)(2,1)} %copy-done.5, ...), custom_call_target="tpu_custom_call" | custom-call | tf_op jit(solution)/shard_map/block_backward/pallas_call | solution.py:287
  51.2 0.8 fusion.1
  52.0 1.3 collective-permute-start.6
  53.3 1.4 fusion
  54.7 4.5 %collective-permute-start.5 = (bf16[8,768]{1,0:T(8,128)(2,1)S(1)}, bf16[8,768]{1,0:T(8,128)(2,1)S(1)}, u32[]{:S(2)}, u32[]{:S(2)}) collective-permute-start(bf16[8,768]{1,0:T(8,128)(2,1)S(1)} %get-tuple-element.41), channel_id=1, source_target_pairs={{0,1},{1,2},{2,3},{3,4},{4,5},{5,6},{6,7},{8,9},{9,10},{10,11},{11... | collective-permute-start | bytes 36872 | tf_op jit(solution)/shard_map/ppermute | solution.py:349
  59.2 0.1 collective-permute-start.4
  59.3 0.0 collective-permute-done.6.right
  59.3 0.7 collective-permute-done.5.left
  60.0 0.1 pad_maximum_fusion.2
  60.1 3.3 %collective-permute-start.7 = (bf16[3,34304]{1,0:T(4,128)(2,1)S(1)}, bf16[3,34304]{1,0:T(4,128)(2,1)S(1)}, u32[]{:S(2)}, u32[]{:S(2)}) collective-permute-start(bf16[3,34304]{1,0:T(4,128)(2,1)S(1)} %pad_maximum_fusion.2), channel_id=1, source_target_pairs={{0,8},{8,16},{16,24},{24,32},{32,40},{40,48},{48,56},{56,64},{64,7... | collective-permute-start | bytes 617480 | tf_op jit(solution)/shard_map/ppermute | solution.py:353
  63.4 0.0 collective-permute-done.4
  63.4 1.1 add_convert_fusion
  64.5 0.0 copy-done.13
  64.5 23.3 %all-to-all-start = ((bf16[128,8,384]{2,1,0:T(8,128)(2,1)}), bf16[128,8,384]{2,1,0:T(8,128)(2,1)S(1)}, u32[]{:S(2)}, u32[]{:S(2)}) async-start(bf16[128,8,384]{2,1,0:T(8,128)(2,1)} %add_convert_fusion), calls=%async_computation | async-start | bytes 1572864 | tf_op jit(solution)/shard_map/all_to_all | solution.py:369
  87.8 0.1 pad_maximum_fusion.3
  87.9 2.0 %collective-permute-start.8 = (bf16[3,34304]{1,0:T(4,128)(2,1)S(1)}, bf16[3,34304]{1,0:T(4,128)(2,1)S(1)}, u32[]{:S(2)}, u32[]{:S(2)}) collective-permute-start(bf16[3,34304]{1,0:T(4,128)(2,1)S(1)} %pad_maximum_fusion.3), channel_id=1, source_target_pairs={{8,0},{16,8},{24,16},{32,24},{40,32},{48,40},{56,48},{64,56},{72,6... | collective-permute-start | bytes 617480 | tf_op jit(solution)/shard_map/ppermute | solution.py:354
  90.0 0.7 rev.3.dww
  90.6 0.0 collective-permute-done.7.top
  90.7 18.1 %collective-permute-done.8.bottom = bf16[3,34304]{1,0:T(4,128)(2,1)S(1)} collective-permute-done((bf16[3,34304]{1,0:T(4,128)(2,1)S(1)}, bf16[3,34304]{1,0:T(4,128)(2,1)S(1)}, u32[]{:S(2)}, u32[]{:S(2)}) %collective-permute-start.8) | collective-permute-done | bytes 205856 | tf_op jit(solution)/shard_map/ppermute | solution.py:354
  108.7 0.7 copy-done.8
  109.5 8.1 %transposed_conv.1 = bf16[8,32768]{1,0:T(8,128)(2,1)} custom-call(bf16[8,32768]{1,0:T(8,128)(2,1)} %get-tuple-element.26.own, bf16[8,768]{1,0:T(8,128)(2,1)} %copy-done.13, bf16[8,768]{1,0:T(8,128)(2,1)} %copy-done.12, bf16[3,34304]{1,0:T(4,128)(2,1)} %copy-done.7, bf16[3,34304]{1,0:T(4,128)(2,1)} %copy-done.8, bf16[8,32768]{1,0:T(8,128)(2,1)} %grad.3, ...), custom_call_target="tpu_custom_call" | custom-call | tf_op jit(solution)/shard_map/transposed_conv/pallas_call | solution.py:319
  117.6 0.0 all-to-all-done
  117.6 0.2 reduce_sum.12
  117.7 0.1 broadcast_in_dim.2
  117.8 36.9 %all_to_all.10.mine = bf16[128,8,384]{2,1,0:T(8,128)(2,1)S(1)} all-to-all(bf16[128,8,384]{2,1,0:T(8,128)(2,1)S(1)} %broadcast_in_dim.2), channel_id=1, replica_groups={{0,1,2,3,4,5,6,7,16,17,18,19,20,21,22,23,32,33,34,35,36,37,38,39,48,49,..., dimensions={0} | all-to-all | bytes 1572864 | tf_op jit(solution)/shard_map/all_to_all | solution.py:369
  154.7 1.2 collective-permute-start.9
  155.9 1.9 %collective-permute-done.9.other = bf16[128,8,384]{2,1,0:T(8,128)(2,1)S(1)} collective-permute-done((bf16[128,8,384]{2,1,0:T(8,128)(2,1)S(1)}, bf16[128,8,384]{2,1,0:T(8,128)(2,1)S(1)}, u32[]{:S(2)}, u32[]{:S(2)}) %collective-permute-start.9) | collective-permute-done | bytes 786464 | tf_op jit(solution)/shard_map/ppermute | solution.py:381
  157.8 0.9 copy-done.2
  158.7 3.2 %clip.1 = (f32[49,256]{1,0:T(8,128)}, f32[1,256]{1,0:T(1,128)}, f32[1,256]{1,0:T(1,128)}, f32[1,256]{1,0:T(1,128)}, f32[256,1024]{1,0:T(8,128)}, /*index=5*/f32[...) custom-call(s32[1]{0:T(128)} %bitcast.core, bf16[128,8,384]{2,1,0:T(8,128)(2,1)} %copy-done, ...), custom_call_target="tpu_custom_call" | custom-call | tf_op jit(solution)/shard_map/clip/pallas_call | solution.py:331
  (24 shorter events, 0.1 us)
Async XLA Ops:
  1.4 7.5 %collective-permute-start.1 = (bf16[8,768]{1,0:T(8,128)(2,1)S(1)}, bf16[8,768]{1,0:T(8,128)(2,1)S(1)}, u32[]{:S(2)}, u32[]{:S(2)}) collective-permute-start(bf16[8,768]{1,0:T(8,128)(2,1)S(1)} %get-tuple-element.44), channel_id=1, source_target_pairs={{1,0},{2,1},{3,2},{4,3},{5,4},{6,5},{7,6},{9,8},{10,9},{11,10},{12... | collective-permute-start | bytes 36872 | tf_op jit(solution)/shard_map/ppermute | solution.py:350
  2.7 13.5 %copy-start.4 = (bf16[1024,256]{1,0:T(8,128)(2,1)S(1)}, bf16[1024,256]{1,0:T(8,128)(2,1)}, u32[]{:S(2)}) copy-start(bf16[1024,256]{1,0:T(8,128)(2,1)} %param.19) | copy-start | bytes 1572868
  2.7 6.2 %collective-permute-start = (bf16[8,768]{1,0:T(8,128)(2,1)S(1)}, bf16[8,768]{1,0:T(8,128)(2,1)S(1)}, u32[]{:S(2)}, u32[]{:S(2)}) collective-permute-start(bf16[8,768]{1,0:T(8,128)(2,1)S(1)} %get-tuple-element.45), channel_id=1, source_target_pairs={{0,1},{1,2},{2,3},{3,4},{4,5},{5,6},{6,7},{8,9},{9,10},{10,11},{11... | collective-permute-start | bytes 36872 | tf_op jit(solution)/shard_map/ppermute | solution.py:349
  8.9 8.3 %copy-start.10 = (bf16[8,768]{1,0:T(8,128)(2,1)}, bf16[8,768]{1,0:T(8,128)(2,1)S(1)}, u32[]{:S(2)}) copy-start(bf16[8,768]{1,0:T(8,128)(2,1)S(1)} %collective-permute-done.1.right) | copy-start | bytes 36868
  8.9 8.2 %copy-start.11 = (bf16[8,768]{1,0:T(8,128)(2,1)}, bf16[8,768]{1,0:T(8,128)(2,1)S(1)}, u32[]{:S(2)}) copy-start(bf16[8,768]{1,0:T(8,128)(2,1)S(1)} %collective-permute-done.left) | copy-start | bytes 36868
  9.0 8.2 %copy-start.1 = (bf16[256,1024]{1,0:T(8,128)(2,1)S(1)}, bf16[256,1024]{1,0:T(8,128)(2,1)}, u32[]{:S(2)}) copy-start(bf16[256,1024]{1,0:T(8,128)(2,1)} %w_in.1) | copy-start | bytes 1572868
  9.1 9.1 %collective-permute-start.2 = (bf16[3,34304]{1,0:T(4,128)(2,1)S(1)}, bf16[3,34304]{1,0:T(4,128)(2,1)S(1)}, u32[]{:S(2)}, u32[]{:S(2)}) collective-permute-start(bf16[3,34304]{1,0:T(4,128)(2,1)S(1)} %pad_maximum_fusion), channel_id=1, source_target_pairs={{0,8},{8,16},{16,24},{24,32},{32,40},{40,48},{48,56},{56,64},{64,7... | collective-permute-start | bytes 617480 | tf_op jit(solution)/shard_map/ppermute | solution.py:353
  14.2 7.8 %collective-permute-start.3 = (bf16[3,34304]{1,0:T(4,128)(2,1)S(1)}, bf16[3,34304]{1,0:T(4,128)(2,1)S(1)}, u32[]{:S(2)}, u32[]{:S(2)}) collective-permute-start(bf16[3,34304]{1,0:T(4,128)(2,1)S(1)} %pad_maximum_fusion.1), channel_id=1, source_target_pairs={{8,0},{16,8},{24,16},{32,24},{40,32},{48,40},{56,48},{64,56},{72,6... | collective-permute-start | bytes 617480 | tf_op jit(solution)/shard_map/ppermute | solution.py:354
  18.2 3.9 %copy-start.5 = (bf16[3,34304]{1,0:T(4,128)(2,1)}, bf16[3,34304]{1,0:T(4,128)(2,1)S(1)}, u32[]{:S(2)}) copy-start(bf16[3,34304]{1,0:T(4,128)(2,1)S(1)} %collective-permute-done.2.top) | copy-start | bytes 617476
  22.0 0.7 copy-start.6
  51.2 12.2 %copy-start.3 = (bf16[128,8,384]{2,1,0:T(8,128)(2,1)S(1)}, bf16[128,8,384]{2,1,0:T(8,128)(2,1)}, u32[]{:S(2)}) copy-start(bf16[128,8,384]{2,1,0:T(8,128)(2,1)} %get-tuple-element.24) | copy-start | bytes 2359300
  52.0 7.3 %collective-permute-start.6 = (bf16[8,768]{1,0:T(8,128)(2,1)S(1)}, bf16[8,768]{1,0:T(8,128)(2,1)S(1)}, u32[]{:S(2)}, u32[]{:S(2)}) collective-permute-start(bf16[8,768]{1,0:T(8,128)(2,1)S(1)} %get-tuple-element.40), channel_id=1, source_target_pairs={{1,0},{2,1},{3,2},{4,3},{5,4},{6,5},{7,6},{9,8},{10,9},{11,10},{12... | collective-permute-start | bytes 36872 | tf_op jit(solution)/shard_map/ppermute | solution.py:350
  54.7 5.3 %collective-permute-start.5 = (bf16[8,768]{1,0:T(8,128)(2,1)S(1)}, bf16[8,768]{1,0:T(8,128)(2,1)S(1)}, u32[]{:S(2)}, u32[]{:S(2)}) collective-permute-start(bf16[8,768]{1,0:T(8,128)(2,1)S(1)} %get-tuple-element.41), channel_id=1, source_target_pairs={{0,1},{1,2},{2,3},{3,4},{4,5},{5,6},{6,7},{8,9},{9,10},{10,11},{11... | collective-permute-start | bytes 36872 | tf_op jit(solution)/shard_map/ppermute | solution.py:349
  59.2 4.2 %collective-permute-start.4 = (bf16[128,8,384]{2,1,0:T(8,128)(2,1)}, bf16[128,8,384]{2,1,0:T(8,128)(2,1)S(1)}, u32[]{:S(2)}, u32[]{:S(2)}) collective-permute-start(bf16[128,8,384]{2,1,0:T(8,128)(2,1)} %get-tuple-element.25), channel_id=1, source_target_pairs={{0,8},{8,0},{16,24},{24,16},{32,40},{40,32},{48,56},{56,48},{64,72... | collective-permute-start | bytes 2359304 | tf_op jit(solution)/shard_map/ppermute | solution.py:375
  59.3 5.2 %copy-start.12 = (bf16[8,768]{1,0:T(8,128)(2,1)}, bf16[8,768]{1,0:T(8,128)(2,1)S(1)}, u32[]{:S(2)}) copy-start(bf16[8,768]{1,0:T(8,128)(2,1)S(1)} %collective-permute-done.6.right) | copy-start | bytes 36868
  60.0 4.5 %copy-start.13 = (bf16[8,768]{1,0:T(8,128)(2,1)}, bf16[8,768]{1,0:T(8,128)(2,1)S(1)}, u32[]{:S(2)}) copy-start(bf16[8,768]{1,0:T(8,128)(2,1)S(1)} %collective-permute-done.5.left) | copy-start | bytes 36868
  60.1 30.5 %collective-permute-start.7 = (bf16[3,34304]{1,0:T(4,128)(2,1)S(1)}, bf16[3,34304]{1,0:T(4,128)(2,1)S(1)}, u32[]{:S(2)}, u32[]{:S(2)}) collective-permute-start(bf16[3,34304]{1,0:T(4,128)(2,1)S(1)} %pad_maximum_fusion.2), channel_id=1, source_target_pairs={{0,8},{8,16},{16,24},{24,32},{32,40},{40,48},{48,56},{56,64},{64,7... | collective-permute-start | bytes 617480 | tf_op jit(solution)/shard_map/ppermute | solution.py:353
  64.5 25.5 %copy-start.9 = (f32[49,256]{1,0:T(8,128)S(1)}, f32[49,256]{1,0:T(8,128)}, u32[]{:S(2)}) copy-start(f32[49,256]{1,0:T(8,128)} %dww.1) | copy-start | bytes 150532
  64.5 53.1 %all-to-all-start = ((bf16[128,8,384]{2,1,0:T(8,128)(2,1)}), bf16[128,8,384]{2,1,0:T(8,128)(2,1)S(1)}, u32[]{:S(2)}, u32[]{:S(2)}) async-start(bf16[128,8,384]{2,1,0:T(8,128)(2,1)} %add_convert_fusion), calls=%async_computation | async-start | bytes 1572864 | tf_op jit(solution)/shard_map/all_to_all | solution.py:369
  87.9 20.8 %collective-permute-start.8 = (bf16[3,34304]{1,0:T(4,128)(2,1)S(1)}, bf16[3,34304]{1,0:T(4,128)(2,1)S(1)}, u32[]{:S(2)}, u32[]{:S(2)}) collective-permute-start(bf16[3,34304]{1,0:T(4,128)(2,1)S(1)} %pad_maximum_fusion.3), channel_id=1, source_target_pairs={{8,0},{16,8},{24,16},{32,24},{40,32},{48,40},{56,48},{64,56},{72,6... | collective-permute-start | bytes 617480 | tf_op jit(solution)/shard_map/ppermute | solution.py:354
  90.6 18.1 %copy-start.7 = (bf16[3,34304]{1,0:T(4,128)(2,1)}, bf16[3,34304]{1,0:T(4,128)(2,1)S(1)}, u32[]{:S(2)}) copy-start(bf16[3,34304]{1,0:T(4,128)(2,1)S(1)} %collective-permute-done.7.top) | copy-start | bytes 617476
  108.7 0.7 copy-start.8
  154.7 3.1 %copy-start = (bf16[128,8,384]{2,1,0:T(8,128)(2,1)}, bf16[128,8,384]{2,1,0:T(8,128)(2,1)S(1)}, u32[]{:S(2)}) copy-start(bf16[128,8,384]{2,1,0:T(8,128)(2,1)S(1)} %all_to_all.10.mine) | copy-start | bytes 2359300
  154.7 3.1 %collective-permute-start.9 = (bf16[128,8,384]{2,1,0:T(8,128)(2,1)S(1)}, bf16[128,8,384]{2,1,0:T(8,128)(2,1)S(1)}, u32[]{:S(2)}, u32[]{:S(2)}) collective-permute-start(bf16[128,8,384]{2,1,0:T(8,128)(2,1)S(1)} %all_to_all.10.mine), channel_id=1, source_target_pairs={{0,8},{8,0},{16,24},{24,16},{32,40},{40,32},{48,56},{56,48},{64,72... | collective-permute-start | bytes 2359304 | tf_op jit(solution)/shard_map/ppermute | solution.py:381
  157.8 0.9 copy-start.2

commit v3 on v2

--- a/solution.py
+++ b/solution.py
@@ -14,7 +14,7 @@
 PIX = ROWS * COLS
 WIDE = COLS + 6
 JB = 8
-LIMIT = 60 * 1024 * 1024
+MIB = 1024 * 1024
 
 
 def shift_rows(own, left, right, top, bottom, tall, shifted):
@@ -275,7 +275,6 @@
         o_bin[:, q * 256 : q * 256 + 256] = small[54 + q : 55 + q, :] * factor
 
 
-PARAMS = pltpu.CompilerParams(vmem_limit_bytes=LIMIT)
 CONV_SCRATCH = (
     pltpu.VMEM((WIDE, 24, C), F32),
     pltpu.VMEM((7, WIDE, 8, C), F32),
@@ -310,7 +309,7 @@
             pltpu.VMEM((64, C), F32),
             pltpu.VMEM((2, 128, 8, 384), BF16),
         ),
-        compiler_params=PARAMS,
+        compiler_params=pltpu.CompilerParams(vmem_limit_bytes=40 * MIB),
         name="block_backward",
     )(*operands)
 
@@ -320,7 +319,8 @@
         transposed_kernel,
         out_shape=jax.ShapeDtypeStruct((ROWS, COLS * C), BF16),
         scratch_shapes=CONV_SCRATCH,
-        compiler_params=PARAMS,
+        compiler_params=pltpu.CompilerParams(vmem_limit_bytes=20 * MIB),
+        cost_estimate=pl.CostEstimate(flops=200_000_000, bytes_accessed=40 * MIB, transcendentals=0),
         name="transposed_conv",
     )(*operands)
 
@@ -338,7 +338,7 @@
         scratch_shapes=(
             pltpu.VMEM((64, C), F32), pltpu.VMEM((C, HID), F32), pltpu.VMEM((HID, C), F32),
         ),
-        compiler_params=PARAMS,
+        compiler_params=pltpu.CompilerParams(vmem_limit_bytes=16 * MIB),
         name="clip",
     )(core, mine, other)
 
@@ -374,10 +374,12 @@
     )
     half = (keep.astype(F32) + lax.ppermute(send, "ha", swap).astype(F32)).astype(BF16)
     terms = exchange(half)
-    grad_features = run_transposed(dconv, *halo(dconv), grad_out, dw_weight[::-1])
-    terms, grad_features = lax.optimization_barrier((terms, grad_features))
+    edges = halo(dconv)
     total = jnp.sum(terms.astype(F32), axis=0).astype(BF16)
+    total, edges = lax.optimization_barrier((total, edges))
     mine = exchange(jnp.broadcast_to(total[None], half.shape))
+    grad_features = run_transposed(dconv, *edges, grad_out, dw_weight[::-1])
+    mine, grad_features = lax.optimization_barrier((mine, grad_features))
     other = lax.ppermute(mine, "ha", swap)
     o_dw, o_dwb, o_gain, o_lnb, o_win, o_bin, o_wout, o_bout, o_scale = run_finish(
         core, mine, other

time: 163 us -> 151 us (0.926)
  blocking collectives: 36.9 us -> 0 us
  waiting for transfers between devices: 24.5 us -> 47.3 us
  starting transfers between devices: 48.6 us -> 57.4 us
  Pallas kernels: 39.8 us -> 33.9 us
  local copies, waits for them, and re-layouts: 9.55 us -> 7.25 us
  other arithmetic: 1.72 us -> 3.86 us
    all_to_all x1 -> x2, waiting for transfers between devices: 0.01 us -> 39.8 us  [exchange(): return lax.all_to_all(x, both, 0, 0, axis_index_groups=groups, tiled=True)]
    all_to_all x1 -> x0, blocking collectives: 36.9 us -> none  [exchange(): return lax.all_to_all(x, both, 0, 0, axis_index_groups=groups, tiled=True)]
    ppermute x2, waiting for transfers between devices: 21.9 us -> 4.41 us  [halo(): bottom = lax.ppermute(lead, 'ha', [(j, i) for i, j in up_h])]
    all_to_all x1 -> x2, starting transfers between devices: 23.3 us -> 32.3 us  [exchange(): return lax.all_to_all(x, both, 0, 0, axis_index_groups=groups, tiled=True)]
    pallas_call x1, Pallas kernels: 28.5 us -> 25.4 us  [run_main(): pl.pallas_call(main_kernel, out_shape=(jax.ShapeDtypeStruct((ROWS, COLS *...]
    unnamed x30 -> x32, local copies, waits for them, and re-layouts: 4.42 us -> 3.79 us
  transfers between devices with their start and end apart: 11 -> 12, of which waited for: 4 -> 6; matrix products, arithmetic and copies ran while one was open for 4% -> 3% of each run, Pallas kernels for 5% -> 4%
where the time goes in v3:
time: 151 us
  starting transfers between devices  57.4 us (38%)
  waiting for transfers between devices  47.3 us (31%)
  Pallas kernels  33.9 us (22%)
  local copies, waits for them, and re-layouts  7.25 us (5%)
  other arithmetic  3.86 us (3%)
    all_to_all x2, waiting for transfers between devices, exchange(): return lax.all_to_all(x, both, 0, 0, axis_index_groups=groups, tiled=True)  39.8 us
    all_to_all x2, starting transfers between devices, exchange(): return lax.all_to_all(x, both, 0, 0, axis_index_groups=groups, tiled=True)  32.3 us
    pallas_call x1, Pallas kernels, run_main(): pl.pallas_call(main_kernel, out_shape=(jax.ShapeDtypeStruct((ROWS, COLS *...  25.4 us
    ppermute x2, starting transfers between devices, halo(): left = lax.ppermute(x[:, -3 * C:], 'wa', up_w)  9.2 us
    ppermute x2, starting transfers between devices, halo(): top = lax.ppermute(last, 'ha', up_h)  8.05 us
    pallas_call x1, Pallas kernels, run_transposed(): pl.pallas_call(transposed_kernel, out_shape=jax.ShapeDtypeStruct((ROWS, C...  6.69 us
    ppermute x2, waiting for transfers between devices, halo(): bottom = lax.ppermute(lead, 'ha', [(j, i) for i, j in up_h])  4.41 us
    ppermute x2, starting transfers between devices, halo(): bottom = lax.ppermute(lead, 'ha', [(j, i) for i, j in up_h])  3.94 us
  transfers between devices with their start and end apart: 12, of which 6 were waited for; matrix products, arithmetic and copies ran while one was open for 3% of the time, Pallas kernels for 4%

profile of v3, /device:TPU:1, one launch (start us, length us, event | category | flops | bytes accessed | tf_op | source)
XLA Modules:
  0.0 150.7 jit_solution(17141122858754875668)
XLA Ops:
  0.6 0.7 fusion.3
  1.4 1.3 collective-permute-start.1
  2.7 0.0 copy-start.14
  2.7 4.8 %collective-permute-start = (bf16[8,768]{1,0:T(8,128)(2,1)S(1)}, bf16[8,768]{1,0:T(8,128)(2,1)S(1)}, u32[]{:S(2)}, u32[]{:S(2)}) collective-permute-start(bf16[8,768]{1,0:T(8,128)(2,1)S(1)} %get-tuple-element.55), channel_id=1, source_target_pairs={{0,1},{1,2},{2,3},{3,4},{4,5},{5,6},{6,7},{8,9},{9,10},{10,11},{11... | collective-permute-start | bytes 36872 | tf_op jit(solution)/shard_map/ppermute | solution.py:349
  7.5 1.5 fusion.2
  9.0 0.0 copy-start.1
  9.0 0.8 pad_maximum_fusion
  9.8 4.8 %collective-permute-start.2 = (bf16[3,34304]{1,0:T(4,128)(2,1)}, bf16[3,34304]{1,0:T(4,128)(2,1)S(1)}, u32[]{:S(2)}, u32[]{:S(2)}) collective-permute-start(bf16[3,34304]{1,0:T(4,128)(2,1)} %pad_maximum_fusion), channel_id=1, source_target_pairs={{0,8},{8,16},{16,24},{24,32},{32,40},{40,48},{48,56},{56,64},{64,7... | collective-permute-start | bytes 617480 | tf_op jit(solution)/shard_map/ppermute | solution.py:353
  14.7 0.8 pad_maximum_fusion.1
  15.5 1.9 %collective-permute-start.3 = (bf16[3,34304]{1,0:T(4,128)(2,1)}, bf16[3,34304]{1,0:T(4,128)(2,1)S(1)}, u32[]{:S(2)}, u32[]{:S(2)}) collective-permute-start(bf16[3,34304]{1,0:T(4,128)(2,1)} %pad_maximum_fusion.1), channel_id=1, source_target_pairs={{8,0},{16,8},{24,16},{32,24},{40,32},{48,40},{56,48},{64,56},{72,6... | collective-permute-start | bytes 617480 | tf_op jit(solution)/shard_map/ppermute | solution.py:354
  17.4 0.0 copy-start
  17.4 0.0 copy-start.2
  17.5 0.0 copy-start.7
  17.5 0.0 copy-start.8
  17.5 0.0 copy-start.9
  17.5 0.0 copy-start.10
  17.5 0.0 copy-start.11
  17.5 0.0 copy-start.12
  17.5 0.2 copy.22
  17.8 0.2 copy.21
  18.0 0.4 collective-permute-done.2.top
  18.4 0.7 copy-done.3
  19.1 4.4 %collective-permute-done.3.bottom = bf16[3,34304]{1,0:T(4,128)(2,1)S(1)} collective-permute-done((bf16[3,34304]{1,0:T(4,128)(2,1)}, bf16[3,34304]{1,0:T(4,128)(2,1)S(1)}, u32[]{:S(2)}, u32[]{:S(2)}) %collective-permute-start.3) | collective-permute-done | bytes 205856 | tf_op jit(solution)/shard_map/ppermute | solution.py:354
  23.5 0.7 copy-done.5
  24.3 0.9 copy-done.4
  25.2 1.0 copy-done.6
  26.2 25.4 %block_backward.1 = (bf16[8,32768]{1,0:T(8,128)(2,1)S(1)}, bf16[128,8,384]{2,1,0:T(8,128)(2,1)S(1)}, bf16[128,8,384]{2,1,0:T(8,128)(2,1)S(1)}) custom-call(s32[1]{0:T(128)} %bitcast.core, bf16[8,32768]{1,0:T(8,128)(2,1)S(1)} %copy-done, bf16[8,768]{1,0:T(8,128)(2,1)S(1)} %collective-permute-done.left, bf16[8,768]{1,0:T(8,128)(2,1)S(1)} %collective-permute-done.1.right, ...), custom_call_target="tpu_custom_call" | custom-call | tf_op jit(solution)/shard_map/block_backward/pallas_call | solution.py:286
  51.6 1.3 collective-permute-start.6
  52.9 0.2 fusion
  53.1 4.4 %collective-permute-start.5 = (bf16[8,768]{1,0:T(8,128)(2,1)S(1)}, bf16[8,768]{1,0:T(8,128)(2,1)S(1)}, u32[]{:S(2)}, u32[]{:S(2)}) collective-permute-start(bf16[8,768]{1,0:T(8,128)(2,1)S(1)} %get-tuple-element.51), channel_id=1, source_target_pairs={{0,1},{1,2},{2,3},{3,4},{4,5},{5,6},{6,7},{8,9},{9,10},{10,11},{11... | collective-permute-start | bytes 36872 | tf_op jit(solution)/shard_map/ppermute | solution.py:349
  57.5 0.1 collective-permute-start.4
  57.6 0.7 collective-permute-done.5.left
  58.3 0.8 pad_maximum_fusion.2
  59.2 3.2 %collective-permute-start.7 = (bf16[3,34304]{1,0:T(4,128)(2,1)}, bf16[3,34304]{1,0:T(4,128)(2,1)S(1)}, u32[]{:S(2)}, u32[]{:S(2)}) collective-permute-start(bf16[3,34304]{1,0:T(4,128)(2,1)} %pad_maximum_fusion.2), channel_id=1, source_target_pairs={{0,8},{8,16},{16,24},{24,32},{32,40},{40,48},{48,56},{56,64},{64,7... | collective-permute-start | bytes 617480 | tf_op jit(solution)/shard_map/ppermute | solution.py:353
  62.4 1.1 add_convert_fusion
  63.5 23.3 %all-to-all-start = ((bf16[128,8,384]{2,1,0:T(8,128)(2,1)}), bf16[128,8,384]{2,1,0:T(8,128)(2,1)S(1)}, u32[]{:S(2)}, u32[]{:S(2)}) async-start(bf16[128,8,384]{2,1,0:T(8,128)(2,1)} %add_convert_fusion), calls=%async_computation | async-start | bytes 1572864 | tf_op jit(solution)/shard_map/all_to_all | solution.py:369
  86.8 0.1 pad_maximum_fusion.3
  86.9 2.0 %collective-permute-start.8 = (bf16[3,34304]{1,0:T(4,128)(2,1)S(1)}, bf16[3,34304]{1,0:T(4,128)(2,1)S(1)}, u32[]{:S(2)}, u32[]{:S(2)}) collective-permute-start(bf16[3,34304]{1,0:T(4,128)(2,1)S(1)} %pad_maximum_fusion.3), channel_id=1, source_target_pairs={{8,0},{16,8},{24,16},{32,24},{40,32},{48,40},{56,48},{64,56},{72,6... | collective-permute-start | bytes 617480 | tf_op jit(solution)/shard_map/ppermute | solution.py:354
  88.9 22.1 %all-to-all-done = bf16[128,8,384]{2,1,0:T(8,128)(2,1)S(1)} async-done(((bf16[128,8,384]{2,1,0:T(8,128)(2,1)}), bf16[128,8,384]{2,1,0:T(8,128)(2,1)S(1)}, u32[]{:S(2)}, u32[]{:S(2)}) %all-to-all-start) | async-done | bytes 786464 | tf_op jit(solution)/shard_map/all_to_all | solution.py:369
  111.0 0.2 reduce_sum.12
  111.2 0.9 broadcast_in_dim.2
  112.2 9.1 %all-to-all-start.1 = ((bf16[128,8,384]{2,1,0:T(8,128)(2,1)}), bf16[128,8,384]{2,1,0:T(8,128)(2,1)S(1)}, u32[]{:S(2)}, u32[]{:S(2)}) async-start(bf16[128,8,384]{2,1,0:T(8,128)(2,1)} %broadcast_in_dim.2), calls=%async_computation.1 | async-start | bytes 1572864 | tf_op jit(solution)/shard_map/all_to_all | solution.py:369
  121.2 0.1 rev.3.dww
  121.3 6.7 %transposed_conv.1 = bf16[8,32768]{1,0:T(8,128)(2,1)} custom-call(bf16[8,32768]{1,0:T(8,128)(2,1)S(1)} %get-tuple-element.31.own, bf16[8,768]{1,0:T(8,128)(2,1)S(1)} %collective-permute-done.5.left, bf16[8,768]{1,0:T(8,128)(2,1)S(1)} %collective-permute-done.6.right, bf16[3,34304]{1,0:T(4,128)(2,1)S(1)} %collective-permute-done.7.top, ...), custom_call_target="tpu_custom_call" | custom-call | flops 200000000 | bytes 41943040 | tf_op jit(solution)/shard_map/transposed_conv/pallas_call | solution.py:318
  128.0 17.8 %all-to-all-done.1.mine = bf16[128,8,384]{2,1,0:T(8,128)(2,1)S(1)} async-done(((bf16[128,8,384]{2,1,0:T(8,128)(2,1)}), bf16[128,8,384]{2,1,0:T(8,128)(2,1)S(1)}, u32[]{:S(2)}, u32[]{:S(2)}) %all-to-all-start.1) | async-done | bytes 786464 | tf_op jit(solution)/shard_map/all_to_all | solution.py:369
  145.8 1.2 collective-permute-start.9
  147.0 1.9 %collective-permute-done.9.other = bf16[128,8,384]{2,1,0:T(8,128)(2,1)S(1)} collective-permute-done((bf16[128,8,384]{2,1,0:T(8,128)(2,1)S(1)}, bf16[128,8,384]{2,1,0:T(8,128)(2,1)S(1)}, u32[]{:S(2)}, u32[]{:S(2)}) %collective-permute-start.9) | collective-permute-done | bytes 786464 | tf_op jit(solution)/shard_map/ppermute | solution.py:383
  148.9 1.8 %clip.1 = (f32[49,256]{1,0:T(8,128)}, f32[1,256]{1,0:T(1,128)}, f32[1,256]{1,0:T(1,128)}, f32[1,256]{1,0:T(1,128)}, f32[256,1024]{1,0:T(8,128)}, /*index=5*/f32[...) custom-call(s32[1]{0:T(128)} %bitcast.core, bf16[128,8,384]{2,1,0:T(8,128)(2,1)S(1)} %all-to-all-done.1.mine, ...), custom_call_target="tpu_custom_call" | custom-call | tf_op jit(solution)/shard_map/clip/pallas_call | solution.py:331
  (27 shorter events, 0.1 us)
Async XLA Ops:
  1.4 7.6 %collective-permute-start.1 = (bf16[8,768]{1,0:T(8,128)(2,1)S(1)}, bf16[8,768]{1,0:T(8,128)(2,1)S(1)}, u32[]{:S(2)}, u32[]{:S(2)}) collective-permute-start(bf16[8,768]{1,0:T(8,128)(2,1)S(1)} %get-tuple-element.54), channel_id=1, source_target_pairs={{1,0},{2,1},{3,2},{4,3},{5,4},{6,5},{7,6},{9,8},{10,9},{11,10},{12... | collective-permute-start | bytes 36872 | tf_op jit(solution)/shard_map/ppermute | solution.py:350
  2.7 14.8 %copy-start.14 = (bf16[1024,256]{1,0:T(8,128)(2,1)S(1)}, bf16[1024,256]{1,0:T(8,128)(2,1)}, u32[]{:S(2)}) copy-start(bf16[1024,256]{1,0:T(8,128)(2,1)} %param.19) | copy-start | bytes 1572868
  2.7 6.3 %collective-permute-start = (bf16[8,768]{1,0:T(8,128)(2,1)S(1)}, bf16[8,768]{1,0:T(8,128)(2,1)S(1)}, u32[]{:S(2)}, u32[]{:S(2)}) collective-permute-start(bf16[8,768]{1,0:T(8,128)(2,1)S(1)} %get-tuple-element.55), channel_id=1, source_target_pairs={{0,1},{1,2},{2,3},{3,4},{4,5},{5,6},{6,7},{8,9},{9,10},{10,11},{11... | collective-permute-start | bytes 36872 | tf_op jit(solution)/shard_map/ppermute | solution.py:349
  9.0 8.8 %copy-start.1 = (bf16[256,1024]{1,0:T(8,128)(2,1)S(1)}, bf16[256,1024]{1,0:T(8,128)(2,1)}, u32[]{:S(2)}) copy-start(bf16[256,1024]{1,0:T(8,128)(2,1)} %w_in.1) | copy-start | bytes 1572868
  9.8 8.6 %collective-permute-start.2 = (bf16[3,34304]{1,0:T(4,128)(2,1)}, bf16[3,34304]{1,0:T(4,128)(2,1)S(1)}, u32[]{:S(2)}, u32[]{:S(2)}) collective-permute-start(bf16[3,34304]{1,0:T(4,128)(2,1)} %pad_maximum_fusion), channel_id=1, source_target_pairs={{0,8},{8,16},{16,24},{24,32},{32,40},{40,48},{48,56},{56,64},{64,7... | collective-permute-start | bytes 617480 | tf_op jit(solution)/shard_map/ppermute | solution.py:353
  15.5 8.0 %collective-permute-start.3 = (bf16[3,34304]{1,0:T(4,128)(2,1)}, bf16[3,34304]{1,0:T(4,128)(2,1)S(1)}, u32[]{:S(2)}, u32[]{:S(2)}) collective-permute-start(bf16[3,34304]{1,0:T(4,128)(2,1)} %pad_maximum_fusion.1), channel_id=1, source_target_pairs={{8,0},{16,8},{24,16},{32,24},{40,32},{48,40},{56,48},{64,56},{72,6... | collective-permute-start | bytes 617480 | tf_op jit(solution)/shard_map/ppermute | solution.py:354
  17.4 6.8 %copy-start = (bf16[8,32768]{1,0:T(8,128)(2,1)S(1)}, bf16[8,32768]{1,0:T(8,128)(2,1)}, u32[]{:S(2)}) copy-start(bf16[8,32768]{1,0:T(8,128)(2,1)} %own.1) | copy-start | bytes 1572868
  17.4 6.8 %copy-start.2 = (bf16[8,32768]{1,0:T(8,128)(2,1)S(1)}, bf16[8,32768]{1,0:T(8,128)(2,1)}, u32[]{:S(2)}) copy-start(bf16[8,32768]{1,0:T(8,128)(2,1)} %grad.3) | copy-start | bytes 1572868
  17.5 6.8 %copy-start.7 = (f32[49,256]{1,0:T(8,128)S(1)}, f32[49,256]{1,0:T(8,128)}, u32[]{:S(2)}) copy-start(f32[49,256]{1,0:T(8,128)} %dww.1) | copy-start | bytes 150532
  17.5 6.8 %copy-start.8 = (f32[1024]{0:T(1024)S(1)}, f32[1024]{0:T(1024)}, u32[]{:S(2)}) copy-start(f32[1024]{0:T(1024)} %param.18) | copy-start | bytes 12292
  17.5 6.8 %copy-start.9 = (f32[256]{0:T(256)S(1)}, f32[256]{0:T(256)}, u32[]{:S(2)}) copy-start(f32[256]{0:T(256)} %param.14) | copy-start | bytes 3076
  17.5 6.8 %copy-start.10 = (f32[256]{0:T(256)S(1)}, f32[256]{0:T(256)}, u32[]{:S(2)}) copy-start(f32[256]{0:T(256)} %param.15) | copy-start | bytes 3076
  17.5 6.8 %copy-start.11 = (f32[256]{0:T(256)S(1)}, f32[256]{0:T(256)}, u32[]{:S(2)}) copy-start(f32[256]{0:T(256)} %param.16) | copy-start | bytes 3076
  17.5 6.8 %copy-start.12 = (f32[256]{0:T(256)S(1)}, f32[256]{0:T(256)}, u32[]{:S(2)}) copy-start(f32[256]{0:T(256)} %param.20) | copy-start | bytes 3076
  17.5 6.8 %copy-start.13 = (f32[256]{0:T(256)S(1)}, f32[256]{0:T(256)}, u32[]{:S(2)}) copy-start(f32[256]{0:T(256)} %param.21) | copy-start | bytes 3076
  18.4 0.7 copy-start.3
  23.5 0.7 copy-start.5
  24.3 1.0 copy-start.4
  25.2 1.0 copy-start.6
  51.6 6.0 %collective-permute-start.6 = (bf16[8,768]{1,0:T(8,128)(2,1)S(1)}, bf16[8,768]{1,0:T(8,128)(2,1)S(1)}, u32[]{:S(2)}, u32[]{:S(2)}) collective-permute-start(bf16[8,768]{1,0:T(8,128)(2,1)S(1)} %get-tuple-element.50), channel_id=1, source_target_pairs={{1,0},{2,1},{3,2},{4,3},{5,4},{6,5},{7,6},{9,8},{10,9},{11,10},{12... | collective-permute-start | bytes 36872 | tf_op jit(solution)/shard_map/ppermute | solution.py:350
  53.1 5.2 %collective-permute-start.5 = (bf16[8,768]{1,0:T(8,128)(2,1)S(1)}, bf16[8,768]{1,0:T(8,128)(2,1)S(1)}, u32[]{:S(2)}, u32[]{:S(2)}) collective-permute-start(bf16[8,768]{1,0:T(8,128)(2,1)S(1)} %get-tuple-element.51), channel_id=1, source_target_pairs={{0,1},{1,2},{2,3},{3,4},{4,5},{5,6},{6,7},{8,9},{9,10},{10,11},{11... | collective-permute-start | bytes 36872 | tf_op jit(solution)/shard_map/ppermute | solution.py:349
  57.5 4.9 %collective-permute-start.4 = (bf16[128,8,384]{2,1,0:T(8,128)(2,1)S(1)}, bf16[128,8,384]{2,1,0:T(8,128)(2,1)S(1)}, u32[]{:S(2)}, u32[]{:S(2)}) collective-permute-start(bf16[128,8,384]{2,1,0:T(8,128)(2,1)S(1)} %get-tuple-element.30), channel_id=1, source_target_pairs={{0,8},{8,0},{16,24},{24,16},{32,40},{40,32},{48,56},{56,48},{64,72... | collective-permute-start | bytes 2359304 | tf_op jit(solution)/shard_map/ppermute | solution.py:375
  59.2 52.0 %collective-permute-start.7 = (bf16[3,34304]{1,0:T(4,128)(2,1)}, bf16[3,34304]{1,0:T(4,128)(2,1)S(1)}, u32[]{:S(2)}, u32[]{:S(2)}) collective-permute-start(bf16[3,34304]{1,0:T(4,128)(2,1)} %pad_maximum_fusion.2), channel_id=1, source_target_pairs={{0,8},{8,16},{16,24},{24,32},{32,40},{40,48},{48,56},{56,64},{64,7... | collective-permute-start | bytes 617480 | tf_op jit(solution)/shard_map/ppermute | solution.py:353
  63.5 47.5 %all-to-all-start = ((bf16[128,8,384]{2,1,0:T(8,128)(2,1)}), bf16[128,8,384]{2,1,0:T(8,128)(2,1)S(1)}, u32[]{:S(2)}, u32[]{:S(2)}) async-start(bf16[128,8,384]{2,1,0:T(8,128)(2,1)} %add_convert_fusion), calls=%async_computation | async-start | bytes 1572864 | tf_op jit(solution)/shard_map/all_to_all | solution.py:369
  86.9 24.3 %collective-permute-start.8 = (bf16[3,34304]{1,0:T(4,128)(2,1)S(1)}, bf16[3,34304]{1,0:T(4,128)(2,1)S(1)}, u32[]{:S(2)}, u32[]{:S(2)}) collective-permute-start(bf16[3,34304]{1,0:T(4,128)(2,1)S(1)} %pad_maximum_fusion.3), channel_id=1, source_target_pairs={{8,0},{16,8},{24,16},{32,24},{40,32},{48,40},{56,48},{64,56},{72,6... | collective-permute-start | bytes 617480 | tf_op jit(solution)/shard_map/ppermute | solution.py:354
  112.2 33.6 %all-to-all-start.1 = ((bf16[128,8,384]{2,1,0:T(8,128)(2,1)}), bf16[128,8,384]{2,1,0:T(8,128)(2,1)S(1)}, u32[]{:S(2)}, u32[]{:S(2)}) async-start(bf16[128,8,384]{2,1,0:T(8,128)(2,1)} %broadcast_in_dim.2), calls=%async_computation.1 | async-start | bytes 1572864 | tf_op jit(solution)/shard_map/all_to_all | solution.py:369
  145.8 3.1 %collective-permute-start.9 = (bf16[128,8,384]{2,1,0:T(8,128)(2,1)S(1)}, bf16[128,8,384]{2,1,0:T(8,128)(2,1)S(1)}, u32[]{:S(2)}, u32[]{:S(2)}) collective-permute-start(bf16[128,8,384]{2,1,0:T(8,128)(2,1)S(1)} %all-to-all-done.1.mine), channel_id=1, source_target_pairs={{0,8},{8,0},{16,24},{24,16},{32,40},{40,32},{48,56},{56,48},{64,72... | collective-permute-start | bytes 2359304 | tf_op jit(solution)/shard_map/ppermute | solution.py:383

commit v4 on v3

--- a/solution.py
+++ b/solution.py
@@ -17,11 +17,15 @@
 MIB = 1024 * 1024
 
 
-def shift_rows(own, left, right, top, bottom, tall, shifted):
+def shift_rows(core, own, left, right, swapped, crossed, tall, shifted):
+    even = core[0] == 0
+
     def place(j, mid, at):
+        inner = swapped[:, pl.ds(at, C)].astype(F32)
+        outer = crossed[:, pl.ds(at, C)].astype(F32)
         tall[j, 8:16, :] = mid.astype(F32)
-        tall[j, 5:8, :] = top[:, pl.ds(at, C)].astype(F32)
-        tall[j, 16:19, :] = bottom[:, pl.ds(at, C)].astype(F32)
+        tall[j, 5:8, :] = jnp.where(even, outer, inner)
+        tall[j, 16:19, :] = jnp.where(even, inner, outer)
         for a in range(7):
             shifted[a, j] = tall[j, 5 + a : 13 + a, :]
 
@@ -62,12 +66,12 @@
 
 
 def main_kernel(
-    core, own, left, right, top, bottom, grad, dww, dwb, gain, lnb, w_in, w_in_t, b_in, w_out_t, b_out, scale,
+    core, own, left, right, swapped, crossed, grad, dww, dwb, gain, lnb, w_in, w_in_t, b_in, w_out_t, b_out, scale,
     dconv_out, keep, send,
     tall, shifted, spread, conv, normed, inv, lnout, lnout_t, grad_flat, grad_t, pre, dact, act, dpre, dcw, small,
     pay,
 ):
-    shift_rows(own, left, right, top, bottom, tall, shifted)
+    shift_rows(core, own, left, right, swapped, crossed, tall, shifted)
     spread_weights(dww, spread)
 
     def forward(n, carry):
@@ -222,9 +226,9 @@
 
 
 def transposed_kernel(
-    own, left, right, top, bottom, grad, dww, out, tall, shifted, spread
+    core, own, left, right, swapped, crossed, grad, dww, out, tall, shifted, spread
 ):
-    shift_rows(own, left, right, top, bottom, tall, shifted)
+    shift_rows(core, own, left, right, swapped, crossed, tall, shifted)
     spread_weights(dww, spread)
 
     def step(n, carry):
@@ -318,6 +322,8 @@
     return pl.pallas_call(
         transposed_kernel,
         out_shape=jax.ShapeDtypeStruct((ROWS, COLS * C), BF16),
+        in_specs=[pl.BlockSpec(memory_space=pltpu.SMEM)]
+        + [pl.BlockSpec(memory_space=pltpu.VMEM)] * (len(operands) - 1),
         scratch_shapes=CONV_SCRATCH,
         compiler_params=pltpu.CompilerParams(vmem_limit_bytes=20 * MIB),
         cost_estimate=pl.CostEstimate(flops=200_000_000, bytes_accessed=40 * MIB, transcendentals=0),
@@ -343,42 +349,71 @@
     )(core, mine, other)
 
 
-def halo(x):
-    up_w = [(i, i + 1) for i in range(lax.axis_size("wa") - 1)]
-    up_h = [(i, i + 1) for i in range(lax.axis_size("ha") - 1)]
-    left = lax.ppermute(x[:, -3 * C :], "wa", up_w)
-    right = lax.ppermute(x[:, : 3 * C], "wa", [(j, i) for i, j in up_w])
+def pair_swaps(n):
+    inner = [(i, i ^ 1) for i in range(n)]
+    outer = [(i, i + 1 if i % 2 else i - 1) for i in range(1, n - 1)]
+    return inner, outer
+
+
+def halo(x, core):
+    inner, outer = pair_swaps(lax.axis_size("wa"))
+    even = lax.rem(lax.axis_index("wa"), 2) == 0
+    first, last = x[:, : 3 * C], x[:, -3 * C :]
+    near = lax.ppermute(jnp.where(even, last, first), "wa", inner)
+    far = lax.ppermute(jnp.where(even, first, last), "wa", outer)
+    left, right = jnp.where(even, far, near), jnp.where(even, near, far)
+    inner, outer = pair_swaps(lax.axis_size("ha"))
+    even = core[0] == 0
     last = jnp.concatenate([left[5:], x[5:], right[5:]], axis=1)
     lead = jnp.concatenate([left[:3], x[:3], right[:3]], axis=1)
-    top = lax.ppermute(last, "ha", up_h)
-    bottom = lax.ppermute(lead, "ha", [(j, i) for i, j in up_h])
-    return left, right, top, bottom
+    crossed = lax.ppermute(jnp.where(even, lead, last), "ha", outer)
+    swapped = lax.ppermute(jnp.where(even, last, lead), "ha", inner)
+    return left, right, swapped, crossed
+
+
+def plane_and_line():
+    wide, pairs = lax.axis_size("wa"), lax.axis_size("ha") // 2
+    depth = pairs // 2
+    at = lambda x, z, c, w: ((x * depth + z) * 2 + c) * wide + w
+    plane = [
+        [at(x, z, c, w) for x in range(2) for w in range(wide)]
+        for z in range(depth)
+        for c in range(2)
+    ]
+    line = [
+        [at(x, z, c, w) for z in range(depth)]
+        for x in range(2)
+        for w in range(wide)
+        for c in range(2)
+    ]
+    return plane, line
 
 
 def on_device(
     features, grad_out, dw_weight, dw_bias, ln_gain, ln_bias, w_in, b_in, w_out, b_out, scale
 ):
     row = lambda v: v.reshape(1, -1)
-    both = ("ha", "wa")
-    pairs, wide = lax.axis_size("ha") // 2, lax.axis_size("wa")
     core = lax.rem(lax.axis_index("ha"), 2).reshape(1).astype(jnp.int32)
-    swap = [(i, i ^ 1) for i in range(2 * pairs)]
-    groups = [[(2 * i + c) * wide + w for i in range(pairs) for w in range(wide)] for c in range(2)]
-
-    def exchange(x):
-        return lax.all_to_all(x, both, 0, 0, axis_index_groups=groups, tiled=True)
+    swap, _ = pair_swaps(lax.axis_size("ha"))
+    plane, line = plane_and_line()
+
+    def exchange(x, groups):
+        return lax.all_to_all(x, ("ha", "wa"), 0, 0, axis_index_groups=groups, tiled=True)
 
     dconv, keep, send = run_main(
-        core, features, *halo(features), grad_out, dw_weight, row(dw_bias), row(ln_gain),
+        core, features, *halo(features, core), grad_out, dw_weight, row(dw_bias), row(ln_gain),
         row(ln_bias), w_in, w_in.T, row(b_in), w_out.T, row(b_out), row(scale),
     )
     half = (keep.astype(F32) + lax.ppermute(send, "ha", swap).astype(F32)).astype(BF16)
-    terms = exchange(half)
-    edges = halo(dconv)
-    total = jnp.sum(terms.astype(F32), axis=0).astype(BF16)
+    terms = exchange(half, plane)
+    edges = halo(dconv, core)
+    sums = jnp.sum(terms.reshape(len(plane[0]), -1, 8, 384).astype(F32), axis=0)
+    total = jnp.sum(exchange(sums, line), axis=0).astype(BF16)
     total, edges = lax.optimization_barrier((total, edges))
-    mine = exchange(jnp.broadcast_to(total[None], half.shape))
-    grad_features = run_transposed(dconv, *edges, grad_out, dw_weight[::-1])
+    mine = exchange(jnp.broadcast_to(total[None], sums.shape), line)
+    mine = jnp.broadcast_to(mine[None], (len(plane[0]),) + mine.shape).reshape(half.shape)
+    mine = exchange(mine, plane)
+    grad_features = run_transposed(core, dconv, *edges, grad_out, dw_weight[::-1])
     mine, grad_features = lax.optimization_barrier((mine, grad_features))
     other = lax.ppermute(mine, "ha", swap)
     o_dw, o_dwb, o_gain, o_lnb, o_win, o_bin, o_wout, o_bout, o_scale = run_finish(

time: 151 us -> 129 us (0.85)
  waiting for transfers between devices: 47.3 us -> 18 us
  blocking collectives: 0 us -> 24.1 us
  starting transfers between devices: 57.4 us -> 41.4 us
    all_to_all x2, waiting for transfers between devices: 39.8 us -> 10.3 us  [exchange(): lax.all_to_all(x, ('ha', 'wa'), 0, 0, axis_index_groups=groups, tiled=True)]
    all_to_all x0 -> x2, blocking collectives: none -> 24.1 us  [exchange(): lax.all_to_all(x, ('ha', 'wa'), 0, 0, axis_index_groups=groups, tiled=True)]
    all_to_all x2, starting transfers between devices: 32.3 us -> 19.2 us  [exchange(): lax.all_to_all(x, ('ha', 'wa'), 0, 0, axis_index_groups=groups, tiled=True)]
    ppermute x8, starting transfers between devices: 23.8 us -> 15.7 us  [the longest x2 7.86 us: halo(): crossed = lax.ppermute(jnp.where(even, lead, last), 'ha', outer)]
    ppermute x1, starting transfers between devices: 1.2 us -> 6.41 us  [on_device(): other = lax.ppermute(mine, 'ha', swap)]
    concatenate x4 -> x0, other arithmetic: 2.62 us -> none  [the longest x2 1.67 us: halo(): last = jnp.concatenate([left[5:], x[5:], right[5:]], axis=1)]
    select_n x0 -> x6, other arithmetic: none -> 2.13 us  [the longest x2 1.38 us: halo(): crossed = lax.ppermute(jnp.where(even, lead, last), 'ha', outer)]
    ppermute x1, waiting for transfers between devices: 0.01 us -> 1.9 us  [on_device(): lax.ppermute(send, 'ha', swap).astype(F32)]
  transfers between devices with their start and end apart: 12 -> 12, of which waited for: 6 -> 6; matrix products, arithmetic and copies ran while one was open for 3% -> 2% of each run, Pallas kernels for 4% -> 5%
where the time goes in v4:
time: 129 us; the launch traced here: 128 us
  starting transfers between devices  41.4 us (32%)
  Pallas kernels  34 us (26%)
  blocking collectives  24.1 us (19%)
  waiting for transfers between devices  18 us (14%)
  local copies, waits for them, and re-layouts  6.55 us (5%)
  other arithmetic  3.33 us (3%)
    pallas_call x1, Pallas kernels, run_main(): pl.pallas_call(main_kernel, out_shape=(jax.ShapeDtypeStruct((ROWS, COLS *...  25.5 us
    all_to_all x2, blocking collectives, exchange(): lax.all_to_all(x, ('ha', 'wa'), 0, 0, axis_index_groups=groups, tiled=True)  24.1 us
    all_to_all x2, starting transfers between devices, exchange(): lax.all_to_all(x, ('ha', 'wa'), 0, 0, axis_index_groups=groups, tiled=True)  19.2 us
    all_to_all x2, waiting for transfers between devices, exchange(): lax.all_to_all(x, ('ha', 'wa'), 0, 0, axis_index_groups=groups, tiled=True)  10.3 us
    ppermute x2, starting transfers between devices, halo(): crossed = lax.ppermute(jnp.where(even, lead, last), 'ha', outer)  7.86 us
    pallas_call x1, Pallas kernels, run_transposed(): pl.pallas_call(transposed_kernel, out_shape=jax.ShapeDtypeStruct((ROWS, C...  6.77 us
    ppermute x1, starting transfers between devices, on_device(): other = lax.ppermute(mine, 'ha', swap)  6.41 us
    ppermute x2, starting transfers between devices, halo(): near = lax.ppermute(jnp.where(even, last, first), 'wa', inner)  6.18 us
  transfers between devices with their start and end apart: 12, of which 6 were waited for; matrix products, arithmetic and copies ran while one was open for 2% of the time, Pallas kernels for 5%

profile of v4, /device:TPU:1, one launch (start us, length us, event | category | flops | bytes accessed | tf_op | source)
XLA Modules:
  0.0 128.4 jit_solution(480919872166649962)
XLA Ops:
  0.6 0.7 broadcast_select_fusion.10
  1.4 2.1 %collective-permute-start.1 = (bf16[8,768]{1,0:T(8,128)(2,1)S(1)}, bf16[8,768]{1,0:T(8,128)(2,1)S(1)}, u32[]{:S(2)}, u32[]{:S(2)}) collective-permute-start(bf16[8,768]{1,0:T(8,128)(2,1)S(1)} %get-tuple-element.58), channel_id=1, source_target_pairs={{0,1},{1,0},{2,3},{3,2},{4,5},{5,4},{6,7},{7,6},{8,9},{9,8},{10,11... | collective-permute-start | bytes 36872 | tf_op jit(solution)/shard_map/ppermute | solution.py:362
  3.5 0.8 collective-permute-start
  4.3 1.5 %fusion.1 = (bf16[3,32768]{1,0:T(4,128)(2,1)S(1)}, bf16[3,32768]{1,0:T(4,128)(2,1)S(1)}) fusion(bf16[8,32768]{1,0:T(8,128)(2,1)} %own.1), kind=kLoop, calls=%fused_computation.19 | loop fusion | bytes 786432 | tf_op jit(solution)/shard_map/slice | solution.py:367
  5.8 0.0 copy-start.2
  5.9 1.1 broadcast_select_fusion.2
  6.9 4.4 %collective-permute-start.3 = (bf16[3,34304]{1,0:T(4,128)(2,1)}, bf16[3,34304]{1,0:T(4,128)(2,1)S(1)}, u32[]{:S(2)}, u32[]{:S(2)}) collective-permute-start(bf16[3,34304]{1,0:T(4,128)(2,1)} %get-tuple-element.50), channel_id=1, source_target_pairs={{8,16},{16,8},{24,32},{32,24},{40,48},{48,40},{56,64},{64,56},{72,... | collective-permute-start | bytes 617480 | tf_op jit(solution)/shard_map/ppermute | solution.py:369
  11.3 0.0 copy-start
  11.3 0.0 copy-start.1
  11.3 0.0 copy-start.7
  11.4 0.0 copy-start.8
  11.4 0.0 copy-start.9
  11.4 0.0 copy-start.10
  11.4 0.0 copy-start.11
  11.4 0.0 copy-start.12
  11.4 0.0 copy-start.13
  11.4 0.1 collective-permute-start.2
  11.5 0.2 copy.24
  11.8 0.2 copy.23
  12.0 3.7 %collective-permute-done.3.crossed = bf16[3,34304]{1,0:T(4,128)(2,1)S(1)} collective-permute-done((bf16[3,34304]{1,0:T(4,128)(2,1)}, bf16[3,34304]{1,0:T(4,128)(2,1)S(1)}, u32[]{:S(2)}, u32[]{:S(2)}) %collective-permute-start.3) | collective-permute-done | bytes 205856 | tf_op jit(solution)/shard_map/ppermute | solution.py:369
  15.7 0.7 copy-done.3
  16.4 0.7 copy-done.5
  17.2 0.9 copy-done.4
  18.1 1.0 copy-done.6
  19.1 25.5 %block_backward.1 = (bf16[8,32768]{1,0:T(8,128)(2,1)S(1)}, bf16[128,8,384]{2,1,0:T(8,128)(2,1)S(1)}, bf16[128,8,384]{2,1,0:T(8,128)(2,1)S(1)}) custom-call(s32[1]{0:T(128)} %bitcast.core, bf16[8,32768]{1,0:T(8,128)(2,1)S(1)} %copy-done, bf16[8,768]{1,0:T(8,128)(2,1)S(1)} %get-tuple-element.63.left, bf16[8,768]{1,0:T(8,128)(2,1)S(1)} %get-tuple-element.62.right, ...), custom_call_target="tpu_custom_call" | custom-call | tf_op jit(solution)/shard_map/block_backward/pallas_call | solution.py:290
  44.6 4.1 %collective-permute-start.6 = (bf16[8,768]{1,0:T(8,128)(2,1)S(1)}, bf16[8,768]{1,0:T(8,128)(2,1)S(1)}, u32[]{:S(2)}, u32[]{:S(2)}) collective-permute-start(bf16[8,768]{1,0:T(8,128)(2,1)S(1)} %get-tuple-element.54), channel_id=1, source_target_pairs={{0,1},{1,0},{2,3},{3,2},{4,5},{5,4},{6,7},{7,6},{8,9},{9,8},{10,11... | collective-permute-start | bytes 36872 | tf_op jit(solution)/shard_map/ppermute | solution.py:362
  48.6 0.7 collective-permute-start.5
  49.3 0.1 collective-permute-start.4
  49.4 0.2 fusion
  49.6 0.1 collective-permute-done.6
  49.8 1.9 %collective-permute-done.4 = bf16[128,8,384]{2,1,0:T(8,128)(2,1)S(1)} collective-permute-done((bf16[128,8,384]{2,1,0:T(8,128)(2,1)S(1)}, bf16[128,8,384]{2,1,0:T(8,128)(2,1)S(1)}, u32[]{:S(2)}, u32[]{:S(2)}) %collective-permute-start.4) | collective-permute-done | bytes 786464 | tf_op jit(solution)/shard_map/ppermute | solution.py:407
  51.7 1.1 add_convert_fusion
  52.7 13.9 %all-to-all-start = ((bf16[128,8,384]{2,1,0:T(8,128)(2,1)}), bf16[128,8,384]{2,1,0:T(8,128)(2,1)S(1)}, u32[]{:S(2)}, u32[]{:S(2)}) async-start(bf16[128,8,384]{2,1,0:T(8,128)(2,1)} %add_convert_fusion), calls=%async_computation | async-start | bytes 1572864 | tf_op jit(solution)/shard_map/all_to_all | solution.py:401
  66.7 0.3 broadcast_select_fusion
  67.0 3.5 %collective-permute-start.8 = (bf16[3,34304]{1,0:T(4,128)(2,1)S(1)}, bf16[3,34304]{1,0:T(4,128)(2,1)S(1)}, u32[]{:S(2)}, u32[]{:S(2)}) collective-permute-start(bf16[3,34304]{1,0:T(4,128)(2,1)S(1)} %get-tuple-element.48), channel_id=1, source_target_pairs={{8,16},{16,8},{24,32},{32,24},{40,48},{48,40},{56,64},{64,56},{72,... | collective-permute-start | bytes 617480 | tf_op jit(solution)/shard_map/ppermute | solution.py:369
  70.5 0.1 collective-permute-start.7
  70.6 7.3 %all-to-all-done = bf16[128,8,384]{2,1,0:T(8,128)(2,1)S(1)} async-done(((bf16[128,8,384]{2,1,0:T(8,128)(2,1)}), bf16[128,8,384]{2,1,0:T(8,128)(2,1)S(1)}, u32[]{:S(2)}, u32[]{:S(2)}) %all-to-all-start) | async-done | bytes 786464 | tf_op jit(solution)/shard_map/all_to_all | solution.py:401
  77.8 0.1 convert_reduce_fusion
  77.9 14.6 %all_to_all.20 = f32[8,8,384]{2,1,0:T(8,128)S(1)} all-to-all(f32[8,8,384]{2,1,0:T(8,128)S(1)} %convert_reduce_fusion), channel_id=1, replica_groups={{0,16,32,48,64,80,96,112},{8,24,40,56,72,88,104,120},{1,17,33,49,65,81,..., dimensions={0} | all-to-all | bytes 196608 | tf_op jit(solution)/shard_map/all_to_all | solution.py:401
  92.6 9.4 %all_to_all.21 = bf16[8,8,384]{2,1,0:T(8,128)(2,1)S(1)} all-to-all(bf16[8,8,384]{2,1,0:T(8,128)(2,1)S(1)} %broadcast_in_dim.4), channel_id=1, replica_groups={{0,16,32,48,64,80,96,112},{8,24,40,56,72,88,104,120},{1,17,33,49,65,81,..., dimensions={0} | all-to-all | bytes 98304 | tf_op jit(solution)/shard_map/all_to_all | solution.py:401
  102.0 1.0 broadcast_in_dim.5
  103.0 5.3 %all-to-all-start.3 = ((bf16[128,8,384]{2,1,0:T(8,128)(2,1)}), bf16[128,8,384]{2,1,0:T(8,128)(2,1)S(1)}, u32[]{:S(2)}, u32[]{:S(2)}) async-start(bf16[128,8,384]{2,1,0:T(8,128)(2,1)} %bitcast.10), calls=%async_computation.3 | async-start | bytes 1572864 | tf_op jit(solution)/shard_map/all_to_all | solution.py:401
  108.3 0.1 rev.3.dww
  108.5 6.8 %transposed_conv.1 = bf16[8,32768]{1,0:T(8,128)(2,1)} custom-call(s32[1]{0:T(128)} %bitcast.core, bf16[8,32768]{1,0:T(8,128)(2,1)S(1)} %get-tuple-element.31.own, bf16[8,768]{1,0:T(8,128)(2,1)S(1)} %get-tuple-element.33.left, bf16[8,768]{1,0:T(8,128)(2,1)S(1)} %get-tuple-element.34.right, bf16[3,34304]{1,0:T(4,128)(2,1)S(1)} %collective-permute-done.7.swapped, ...), custom_call_target="tpu_custom_call" | custom-call | flops 200000000 | bytes 41943040 | tf_op jit(solution)/shard_map/transposed_conv/pallas_call | solution.py:322
  115.2 3.1 %all-to-all-done.3.mine = bf16[128,8,384]{2,1,0:T(8,128)(2,1)S(1)} async-done(((bf16[128,8,384]{2,1,0:T(8,128)(2,1)}), bf16[128,8,384]{2,1,0:T(8,128)(2,1)S(1)}, u32[]{:S(2)}, u32[]{:S(2)}) %all-to-all-start.3) | async-done | bytes 786464 | tf_op jit(solution)/shard_map/all_to_all | solution.py:401
  118.3 6.4 %collective-permute-start.9 = (bf16[128,8,384]{2,1,0:T(8,128)(2,1)S(1)}, bf16[128,8,384]{2,1,0:T(8,128)(2,1)S(1)}, u32[]{:S(2)}, u32[]{:S(2)}) collective-permute-start(bf16[128,8,384]{2,1,0:T(8,128)(2,1)S(1)} %all-to-all-done.3.mine), channel_id=1, source_target_pairs={{0,8},{8,0},{16,24},{24,16},{32,40},{40,32},{48,56},{56,48},{64,72... | collective-permute-start | bytes 2359304 | tf_op jit(solution)/shard_map/ppermute | solution.py:418
  124.7 1.9 %collective-permute-done.9.other = bf16[128,8,384]{2,1,0:T(8,128)(2,1)S(1)} collective-permute-done((bf16[128,8,384]{2,1,0:T(8,128)(2,1)S(1)}, bf16[128,8,384]{2,1,0:T(8,128)(2,1)S(1)}, u32[]{:S(2)}, u32[]{:S(2)}) %collective-permute-start.9) | collective-permute-done | bytes 786464 | tf_op jit(solution)/shard_map/ppermute | solution.py:418
  126.6 1.8 %clip.1 = (f32[49,256]{1,0:T(8,128)}, f32[1,256]{1,0:T(1,128)}, f32[1,256]{1,0:T(1,128)}, f32[1,256]{1,0:T(1,128)}, f32[256,1024]{1,0:T(8,128)}, /*index=5*/f32[...) custom-call(s32[1]{0:T(128)} %bitcast.core, bf16[128,8,384]{2,1,0:T(8,128)(2,1)S(1)} %all-to-all-done.3.mine, ...), custom_call_target="tpu_custom_call" | custom-call | tf_op jit(solution)/shard_map/clip/pallas_call | solution.py:337
  (30 shorter events, 0.1 us)
Async XLA Ops:
  1.4 4.4 %collective-permute-start.1 = (bf16[8,768]{1,0:T(8,128)(2,1)S(1)}, bf16[8,768]{1,0:T(8,128)(2,1)S(1)}, u32[]{:S(2)}, u32[]{:S(2)}) collective-permute-start(bf16[8,768]{1,0:T(8,128)(2,1)S(1)} %get-tuple-element.58), channel_id=1, source_target_pairs={{0,1},{1,0},{2,3},{3,2},{4,5},{5,4},{6,7},{7,6},{8,9},{9,8},{10,11... | collective-permute-start | bytes 36872 | tf_op jit(solution)/shard_map/ppermute | solution.py:362
  3.5 8.0 %copy-start.14 = (bf16[1024,256]{1,0:T(8,128)(2,1)S(1)}, bf16[1024,256]{1,0:T(8,128)(2,1)}, u32[]{:S(2)}) copy-start(bf16[1024,256]{1,0:T(8,128)(2,1)} %param.19) | copy-start | bytes 1572868
  3.5 2.3 %collective-permute-start = (bf16[8,768]{1,0:T(8,128)(2,1)S(1)}, bf16[8,768]{1,0:T(8,128)(2,1)S(1)}, u32[]{:S(2)}, u32[]{:S(2)}) collective-permute-start(bf16[8,768]{1,0:T(8,128)(2,1)S(1)} %get-tuple-element.59), channel_id=1, source_target_pairs={{1,2},{2,1},{3,4},{4,3},{5,6},{6,5},{9,10},{10,9},{11,12},{12,11},... | collective-permute-start | bytes 36872 | tf_op jit(solution)/shard_map/ppermute | solution.py:363
  5.8 5.9 %copy-start.2 = (bf16[256,1024]{1,0:T(8,128)(2,1)S(1)}, bf16[256,1024]{1,0:T(8,128)(2,1)}, u32[]{:S(2)}) copy-start(bf16[256,1024]{1,0:T(8,128)(2,1)} %w_in.1) | copy-start | bytes 1572868
  6.9 8.8 %collective-permute-start.3 = (bf16[3,34304]{1,0:T(4,128)(2,1)}, bf16[3,34304]{1,0:T(4,128)(2,1)S(1)}, u32[]{:S(2)}, u32[]{:S(2)}) collective-permute-start(bf16[3,34304]{1,0:T(4,128)(2,1)} %get-tuple-element.50), channel_id=1, source_target_pairs={{8,16},{16,8},{24,32},{32,24},{40,48},{48,40},{56,64},{64,56},{72,... | collective-permute-start | bytes 617480 | tf_op jit(solution)/shard_map/ppermute | solution.py:369
  11.3 5.8 %copy-start = (bf16[8,32768]{1,0:T(8,128)(2,1)S(1)}, bf16[8,32768]{1,0:T(8,128)(2,1)}, u32[]{:S(2)}) copy-start(bf16[8,32768]{1,0:T(8,128)(2,1)} %own.1) | copy-start | bytes 1572868
  11.3 5.8 %copy-start.1 = (bf16[8,32768]{1,0:T(8,128)(2,1)S(1)}, bf16[8,32768]{1,0:T(8,128)(2,1)}, u32[]{:S(2)}) copy-start(bf16[8,32768]{1,0:T(8,128)(2,1)} %grad.3) | copy-start | bytes 1572868
  11.3 5.8 %copy-start.7 = (f32[49,256]{1,0:T(8,128)S(1)}, f32[49,256]{1,0:T(8,128)}, u32[]{:S(2)}) copy-start(f32[49,256]{1,0:T(8,128)} %dww.1) | copy-start | bytes 150532
  11.4 5.8 %copy-start.8 = (f32[1024]{0:T(1024)S(1)}, f32[1024]{0:T(1024)}, u32[]{:S(2)}) copy-start(f32[1024]{0:T(1024)} %param.18) | copy-start | bytes 12292
  11.4 5.8 %copy-start.9 = (f32[256]{0:T(256)S(1)}, f32[256]{0:T(256)}, u32[]{:S(2)}) copy-start(f32[256]{0:T(256)} %param.14) | copy-start | bytes 3076
  11.4 5.8 %copy-start.10 = (f32[256]{0:T(256)S(1)}, f32[256]{0:T(256)}, u32[]{:S(2)}) copy-start(f32[256]{0:T(256)} %param.15) | copy-start | bytes 3076
  11.4 5.8 %copy-start.11 = (f32[256]{0:T(256)S(1)}, f32[256]{0:T(256)}, u32[]{:S(2)}) copy-start(f32[256]{0:T(256)} %param.16) | copy-start | bytes 3076
  11.4 5.8 %copy-start.12 = (f32[256]{0:T(256)S(1)}, f32[256]{0:T(256)}, u32[]{:S(2)}) copy-start(f32[256]{0:T(256)} %param.20) | copy-start | bytes 3076
  11.4 5.8 %copy-start.13 = (f32[256]{0:T(256)S(1)}, f32[256]{0:T(256)}, u32[]{:S(2)}) copy-start(f32[256]{0:T(256)} %param.21) | copy-start | bytes 3076
  11.4 5.0 %collective-permute-start.2 = (bf16[3,34304]{1,0:T(4,128)(2,1)}, bf16[3,34304]{1,0:T(4,128)(2,1)S(1)}, u32[]{:S(2)}, u32[]{:S(2)}) collective-permute-start(bf16[3,34304]{1,0:T(4,128)(2,1)} %get-tuple-element.51), channel_id=1, source_target_pairs={{0,8},{8,0},{16,24},{24,16},{32,40},{40,32},{48,56},{56,48},{64,72... | collective-permute-start | bytes 617480 | tf_op jit(solution)/shard_map/ppermute | solution.py:370
  15.7 0.7 copy-start.3
  16.4 0.7 copy-start.5
  17.2 1.0 copy-start.4
  18.1 1.0 copy-start.6
  44.6 5.1 %collective-permute-start.6 = (bf16[8,768]{1,0:T(8,128)(2,1)S(1)}, bf16[8,768]{1,0:T(8,128)(2,1)S(1)}, u32[]{:S(2)}, u32[]{:S(2)}) collective-permute-start(bf16[8,768]{1,0:T(8,128)(2,1)S(1)} %get-tuple-element.54), channel_id=1, source_target_pairs={{0,1},{1,0},{2,3},{3,2},{4,5},{5,4},{6,7},{7,6},{8,9},{9,8},{10,11... | collective-permute-start | bytes 36872 | tf_op jit(solution)/shard_map/ppermute | solution.py:362
  48.6 1.1 collective-permute-start.5
  49.3 2.4 %collective-permute-start.4 = (bf16[128,8,384]{2,1,0:T(8,128)(2,1)S(1)}, bf16[128,8,384]{2,1,0:T(8,128)(2,1)S(1)}, u32[]{:S(2)}, u32[]{:S(2)}) collective-permute-start(bf16[128,8,384]{2,1,0:T(8,128)(2,1)S(1)} %get-tuple-element.30), channel_id=1, source_target_pairs={{0,8},{8,0},{16,24},{24,16},{32,40},{40,32},{48,56},{56,48},{64,72... | collective-permute-start | bytes 2359304 | tf_op jit(solution)/shard_map/ppermute | solution.py:407
  52.7 25.1 %all-to-all-start = ((bf16[128,8,384]{2,1,0:T(8,128)(2,1)}), bf16[128,8,384]{2,1,0:T(8,128)(2,1)S(1)}, u32[]{:S(2)}, u32[]{:S(2)}) async-start(bf16[128,8,384]{2,1,0:T(8,128)(2,1)} %add_convert_fusion), calls=%async_computation | async-start | bytes 1572864 | tf_op jit(solution)/shard_map/all_to_all | solution.py:401
  67.0 25.6 %collective-permute-start.8 = (bf16[3,34304]{1,0:T(4,128)(2,1)S(1)}, bf16[3,34304]{1,0:T(4,128)(2,1)S(1)}, u32[]{:S(2)}, u32[]{:S(2)}) collective-permute-start(bf16[3,34304]{1,0:T(4,128)(2,1)S(1)} %get-tuple-element.48), channel_id=1, source_target_pairs={{8,16},{16,8},{24,32},{32,24},{40,48},{48,40},{56,64},{64,56},{72,... | collective-permute-start | bytes 617480 | tf_op jit(solution)/shard_map/ppermute | solution.py:369
  70.5 22.1 %collective-permute-start.7 = (bf16[3,34304]{1,0:T(4,128)(2,1)S(1)}, bf16[3,34304]{1,0:T(4,128)(2,1)S(1)}, u32[]{:S(2)}, u32[]{:S(2)}) collective-permute-start(bf16[3,34304]{1,0:T(4,128)(2,1)S(1)} %get-tuple-element.49), channel_id=1, source_target_pairs={{0,8},{8,0},{16,24},{24,16},{32,40},{40,32},{48,56},{56,48},{64,72... | collective-permute-start | bytes 617480 | tf_op jit(solution)/shard_map/ppermute | solution.py:370
  103.0 15.3 %all-to-all-start.3 = ((bf16[128,8,384]{2,1,0:T(8,128)(2,1)}), bf16[128,8,384]{2,1,0:T(8,128)(2,1)S(1)}, u32[]{:S(2)}, u32[]{:S(2)}) async-start(bf16[128,8,384]{2,1,0:T(8,128)(2,1)} %bitcast.10), calls=%async_computation.3 | async-start | bytes 1572864 | tf_op jit(solution)/shard_map/all_to_all | solution.py:401
  118.3 8.3 %collective-permute-start.9 = (bf16[128,8,384]{2,1,0:T(8,128)(2,1)S(1)}, bf16[128,8,384]{2,1,0:T(8,128)(2,1)S(1)}, u32[]{:S(2)}, u32[]{:S(2)}) collective-permute-start(bf16[128,8,384]{2,1,0:T(8,128)(2,1)S(1)} %all-to-all-done.3.mine), channel_id=1, source_target_pairs={{0,8},{8,0},{16,24},{24,16},{32,40},{40,32},{48,56},{56,48},{64,72... | collective-permute-start | bytes 2359304 | tf_op jit(solution)/shard_map/ppermute | solution.py:418

commit v5 on v4

--- a/solution.py
+++ b/solution.py
@@ -17,15 +17,12 @@
 MIB = 1024 * 1024
 
 
-def shift_rows(core, own, left, right, swapped, crossed, tall, shifted):
-    even = core[0] == 0
-
+def shift_rows(own, left, right, rows, tall, shifted):
     def place(j, mid, at):
-        inner = swapped[:, pl.ds(at, C)].astype(F32)
-        outer = crossed[:, pl.ds(at, C)].astype(F32)
+        edge = rows[:, pl.ds(at, C)].astype(F32)
         tall[j, 8:16, :] = mid.astype(F32)
-        tall[j, 5:8, :] = jnp.where(even, outer, inner)
-        tall[j, 16:19, :] = jnp.where(even, inner, outer)
+        tall[j, 5:8, :] = edge[0:3]
+        tall[j, 16:19, :] = edge[3:6]
         for a in range(7):
             shifted[a, j] = tall[j, 5 + a : 13 + a, :]
 
@@ -66,12 +63,12 @@
 
 
 def main_kernel(
-    core, own, left, right, swapped, crossed, grad, dww, dwb, gain, lnb, w_in, w_in_t, b_in, w_out_t, b_out, scale,
+    core, own, left, right, rows, grad, dww, dwb, gain, lnb, w_in, w_in_t, b_in, w_out_t, b_out, scale,
     dconv_out, keep, send,
     tall, shifted, spread, conv, normed, inv, lnout, lnout_t, grad_flat, grad_t, pre, dact, act, dpre, dcw, small,
     pay,
 ):
-    shift_rows(core, own, left, right, swapped, crossed, tall, shifted)
+    shift_rows(own, left, right, rows, tall, shifted)
     spread_weights(dww, spread)
 
     def forward(n, carry):
@@ -116,8 +113,10 @@
             for q in range(4):
                 lanes = slice(q * 256, q * 256 + 256)
                 v = pre[sub, lanes]
-                e = jnp.exp(v * v * -0.5)
-                t = 1.0 / (1.0 + (0.3275911 / math.sqrt(2.0)) * jnp.abs(v))
+                e = jnp.exp2(v * v * (-0.5 / math.log(2.0)))
+                d = 1.0 + (0.3275911 / math.sqrt(2.0)) * jnp.abs(v)
+                t = pl.reciprocal(d, approx=True)
+                t = t * (2.0 - d * t)
                 poly = 0.5 * 1.061405429 * t - 0.5 * 1.453152027
                 poly = poly * t + 0.5 * 1.421413741
                 poly = poly * t - 0.5 * 0.284496736
@@ -226,9 +225,9 @@
 
 
 def transposed_kernel(
-    core, own, left, right, swapped, crossed, grad, dww, out, tall, shifted, spread
+    own, left, right, rows, grad, dww, out, tall, shifted, spread
 ):
-    shift_rows(core, own, left, right, swapped, crossed, tall, shifted)
+    shift_rows(own, left, right, rows, tall, shifted)
     spread_weights(dww, spread)
 
     def step(n, carry):
@@ -322,8 +321,6 @@
     return pl.pallas_call(
         transposed_kernel,
         out_shape=jax.ShapeDtypeStruct((ROWS, COLS * C), BF16),
-        in_specs=[pl.BlockSpec(memory_space=pltpu.SMEM)]
-        + [pl.BlockSpec(memory_space=pltpu.VMEM)] * (len(operands) - 1),
         scratch_shapes=CONV_SCRATCH,
         compiler_params=pltpu.CompilerParams(vmem_limit_bytes=20 * MIB),
         cost_estimate=pl.CostEstimate(flops=200_000_000, bytes_accessed=40 * MIB, transcendentals=0),
@@ -355,7 +352,7 @@
     return inner, outer
 
 
-def halo(x, core):
+def halo(x, core, after=None):
     inner, outer = pair_swaps(lax.axis_size("wa"))
     even = lax.rem(lax.axis_index("wa"), 2) == 0
     first, last = x[:, : 3 * C], x[:, -3 * C :]
@@ -366,9 +363,12 @@
     even = core[0] == 0
     last = jnp.concatenate([left[5:], x[5:], right[5:]], axis=1)
     lead = jnp.concatenate([left[:3], x[:3], right[:3]], axis=1)
+    if after is not None:
+        lead, last, after = lax.optimization_barrier((lead, last, after))
     crossed = lax.ppermute(jnp.where(even, lead, last), "ha", outer)
     swapped = lax.ppermute(jnp.where(even, last, lead), "ha", inner)
-    return left, right, swapped, crossed
+    top, bottom = jnp.where(even, crossed, swapped), jnp.where(even, swapped, crossed)
+    return left, right, jnp.concatenate([top, bottom], axis=0)
 
 
 def plane_and_line():
@@ -405,15 +405,17 @@
         row(ln_bias), w_in, w_in.T, row(b_in), w_out.T, row(b_out), row(scale),
     )
     half = (keep.astype(F32) + lax.ppermute(send, "ha", swap).astype(F32)).astype(BF16)
+    half, dconv = lax.optimization_barrier((half, dconv))
     terms = exchange(half, plane)
-    edges = halo(dconv, core)
-    sums = jnp.sum(terms.reshape(len(plane[0]), -1, 8, 384).astype(F32), axis=0)
-    total = jnp.sum(exchange(sums, line), axis=0).astype(BF16)
+    edges = halo(dconv, core, terms)
+    fold_first = lambda v, n: jnp.sum(v.reshape((n, -1) + v.shape[1:]).astype(F32), axis=0).astype(BF16)
+    sums = fold_first(terms, len(plane[0]))
+    every = jnp.broadcast_to(sums[None], (len(line[0]),) + sums.shape)
+    total = fold_first(exchange(every.reshape((-1,) + sums.shape[1:]), line), len(line[0]))
     total, edges = lax.optimization_barrier((total, edges))
-    mine = exchange(jnp.broadcast_to(total[None], sums.shape), line)
-    mine = jnp.broadcast_to(mine[None], (len(plane[0]),) + mine.shape).reshape(half.shape)
+    mine = jnp.broadcast_to(total[None], (len(plane[0]),) + total.shape).reshape(half.shape)
     mine = exchange(mine, plane)
-    grad_features = run_transposed(core, dconv, *edges, grad_out, dw_weight[::-1])
+    grad_features = run_transposed(dconv, *edges, grad_out, dw_weight[::-1])
     mine, grad_features = lax.optimization_barrier((mine, grad_features))
     other = lax.ppermute(mine, "ha", swap)
     o_dw, o_dwb, o_gain, o_lnb, o_win, o_bin, o_wout, o_bout, o_scale = run_finish(

time: 129 us -> 128 us (level)
  blocking collectives: 24.1 us -> 0 us
  waiting for transfers between devices: 18 us -> 40 us
  local copies, waits for them, and re-layouts: 6.55 us -> 4.07 us
  starting transfers between devices: 41.4 us -> 43.6 us
  other arithmetic: 3.33 us -> 4.71 us
    all_to_all x2 -> x0, blocking collectives: 24.1 us -> none  [exchange(): lax.all_to_all(x, ('ha', 'wa'), 0, 0, axis_index_groups=groups, tiled=True)]
    all_to_all x2 -> x3, waiting for transfers between devices: 10.3 us -> 32.3 us  [exchange(): lax.all_to_all(x, ('ha', 'wa'), 0, 0, axis_index_groups=groups, tiled=True)]
    all_to_all x2 -> x3, starting transfers between devices: 19.2 us -> 24.9 us  [exchange(): lax.all_to_all(x, ('ha', 'wa'), 0, 0, axis_index_groups=groups, tiled=True)]
    ppermute x1, starting transfers between devices: 6.41 us -> 1.96 us  [on_device(): other = lax.ppermute(mine, 'ha', swap)]
    unnamed x32 -> x24, local copies, waits for them, and re-layouts: 3.79 us -> 0.48 us
    slice x0 -> x2, local copies, waits for them, and re-layouts: none -> 1.54 us  [halo(): lead = jnp.concatenate([left[:3], x[:3], right[:3]], axis=1)]
    slice x5 -> x3, local copies, waits for them, and re-layouts: 1.68 us -> 0.19 us  [halo(): last = jnp.concatenate([left[5:], x[5:], right[5:]], axis=1)]
    select_n x0 -> x2, other arithmetic: none -> 1.41 us  [halo(): jnp.where(even, crossed, swapped)]
  transfers between devices with their start and end apart: 12 -> 13, of which waited for: 6 -> 6; matrix products, arithmetic and copies ran while one was open for 2% -> 3% of each run, Pallas kernels for 5% -> 5%
where the time goes in v5:
time: 128 us; the launch traced here: 127 us
  starting transfers between devices  43.6 us (34%)
  waiting for transfers between devices  40 us (31%)
  Pallas kernels  33.9 us (26%)
  other arithmetic  4.71 us (4%)
  local copies, waits for them, and re-layouts  4.07 us (3%)
    all_to_all x3, waiting for transfers between devices, exchange(): lax.all_to_all(x, ('ha', 'wa'), 0, 0, axis_index_groups=groups, tiled=True)  32.3 us
    pallas_call x1, Pallas kernels, run_main(): pl.pallas_call(main_kernel, out_shape=(jax.ShapeDtypeStruct((ROWS, COLS *...  25.5 us
    all_to_all x3, starting transfers between devices, exchange(): lax.all_to_all(x, ('ha', 'wa'), 0, 0, axis_index_groups=groups, tiled=True)  24.9 us
    ppermute x2, starting transfers between devices, halo(): crossed = lax.ppermute(jnp.where(even, lead, last), 'ha', outer)  8.95 us
    pallas_call x1, Pallas kernels, run_transposed(): pl.pallas_call(transposed_kernel, out_shape=jax.ShapeDtypeStruct((ROWS, C...  6.56 us
    ppermute x2, starting transfers between devices, halo(): near = lax.ppermute(jnp.where(even, last, first), 'wa', inner)  6.04 us
    ppermute x2, waiting for transfers between devices, halo(): crossed = lax.ppermute(jnp.where(even, lead, last), 'ha', outer)  3.52 us
  transfers between devices with their start and end apart: 13, of which 6 were waited for; matrix products, arithmetic and copies ran while one was open for 3% of the time, Pallas kernels for 5%

profile of v5, /device:TPU:1, one launch (start us, length us, event | category | flops | bytes accessed | tf_op | source)
XLA Modules:
  0.0 127.3 jit_solution(8158120736869805928)
XLA Ops:
  0.6 0.7 broadcast_select_fusion.14
  1.4 2.1 %collective-permute-start.1 = (bf16[8,768]{1,0:T(8,128)(2,1)S(1)}, bf16[8,768]{1,0:T(8,128)(2,1)S(1)}, u32[]{:S(2)}, u32[]{:S(2)}) collective-permute-start(bf16[8,768]{1,0:T(8,128)(2,1)S(1)} %get-tuple-element.68), channel_id=1, source_target_pairs={{0,1},{1,0},{2,3},{3,2},{4,5},{5,4},{6,7},{7,6},{8,9},{9,8},{10,11... | collective-permute-start | bytes 36872 | tf_op jit(solution)/shard_map/ppermute | solution.py:359
  3.5 0.8 collective-permute-start
  4.3 1.5 %fusion.1 = (bf16[3,32768]{1,0:T(4,128)(2,1)S(1)}, bf16[3,32768]{1,0:T(4,128)(2,1)S(1)}) fusion(bf16[8,32768]{1,0:T(8,128)(2,1)} %own.1), kind=kLoop, calls=%fused_computation.24 | loop fusion | bytes 786432 | tf_op jit(solution)/shard_map/slice | solution.py:365
  5.9 0.0 copy-start.1
  5.9 0.3 broadcast_select_fusion.7
  6.2 4.4 %collective-permute-start.2 = (bf16[3,34304]{1,0:T(4,128)(2,1)S(1)}, bf16[3,34304]{1,0:T(4,128)(2,1)S(1)}, u32[]{:S(2)}, u32[]{:S(2)}) collective-permute-start(bf16[3,34304]{1,0:T(4,128)(2,1)S(1)} %get-tuple-element.60), channel_id=1, source_target_pairs={{8,16},{16,8},{24,32},{32,24},{40,48},{48,40},{56,64},{64,56},{72,... | collective-permute-start | bytes 617480 | tf_op jit(solution)/shard_map/ppermute | solution.py:368
  10.6 0.1 collective-permute-start.3
  10.7 0.2 copy.24
  10.9 0.2 copy.23
  11.1 0.0 copy-start
  11.2 0.0 copy-start.2
  11.2 0.0 copy-start.3
  11.2 0.0 copy-start.4
  11.2 0.0 copy-start.7
  11.2 0.0 copy-start.8
  11.2 3.5 %collective-permute-done.2 = bf16[3,34304]{1,0:T(4,128)(2,1)S(1)} collective-permute-done((bf16[3,34304]{1,0:T(4,128)(2,1)S(1)}, bf16[3,34304]{1,0:T(4,128)(2,1)S(1)}, u32[]{:S(2)}, u32[]{:S(2)}) %collective-permute-start.2) | collective-permute-done | bytes 205856 | tf_op jit(solution)/shard_map/ppermute | solution.py:368
  14.8 1.2 broadcast_select_fusion.5
  16.0 0.3 pad_maximum_fusion.rows
  16.3 25.5 %block_backward.1 = (bf16[8,32768]{1,0:T(8,128)(2,1)S(1)}, bf16[128,8,384]{2,1,0:T(8,128)(2,1)S(1)}, bf16[128,8,384]{2,1,0:T(8,128)(2,1)S(1)}) custom-call(s32[1]{0:T(128)} %bitcast.core, bf16[8,32768]{1,0:T(8,128)(2,1)S(1)} %copy-done, bf16[8,768]{1,0:T(8,128)(2,1)S(1)} %get-tuple-element.73.left, bf16[8,768]{1,0:T(8,128)(2,1)S(1)} %get-tuple-element.72.right, ...), custom_call_target="tpu_custom_call" | custom-call | tf_op jit(solution)/shard_map/block_backward/pallas_call | solution.py:289
  41.8 0.1 collective-permute-start.4
  41.9 2.3 %collective-permute-done.4 = bf16[128,8,384]{2,1,0:T(8,128)(2,1)S(1)} collective-permute-done((bf16[128,8,384]{2,1,0:T(8,128)(2,1)S(1)}, bf16[128,8,384]{2,1,0:T(8,128)(2,1)S(1)}, u32[]{:S(2)}, u32[]{:S(2)}) %collective-permute-start.4) | collective-permute-done | bytes 786464 | tf_op jit(solution)/shard_map/ppermute | solution.py:407
  44.2 1.1 add_convert_fusion
  45.3 3.9 %collective-permute-start.6 = (bf16[8,768]{1,0:T(8,128)(2,1)S(1)}, bf16[8,768]{1,0:T(8,128)(2,1)S(1)}, u32[]{:S(2)}, u32[]{:S(2)}) collective-permute-start(bf16[8,768]{1,0:T(8,128)(2,1)S(1)} %get-tuple-element.64), channel_id=1, source_target_pairs={{0,1},{1,0},{2,3},{3,2},{4,5},{5,4},{6,7},{7,6},{8,9},{9,8},{10,11... | collective-permute-start | bytes 36872 | tf_op jit(solution)/shard_map/ppermute | solution.py:359
  49.2 0.7 collective-permute-start.5
  49.9 0.2 fusion
  50.1 13.4 %all-to-all-start = ((bf16[128,8,384]{2,1,0:T(8,128)(2,1)}), bf16[128,8,384]{2,1,0:T(8,128)(2,1)S(1)}, u32[]{:S(2)}, u32[]{:S(2)}) async-start(bf16[128,8,384]{2,1,0:T(8,128)(2,1)} %add_convert_fusion), calls=%async_computation | async-start | bytes 1572864 | tf_op jit(solution)/shard_map/all_to_all | solution.py:401
  63.5 0.1 pad_maximum_fusion.5
  63.6 0.1 pad_maximum_fusion.4
  63.8 11.7 %all-to-all-done = bf16[128,8,384]{2,1,0:T(8,128)(2,1)S(1)} async-done(((bf16[128,8,384]{2,1,0:T(8,128)(2,1)}), bf16[128,8,384]{2,1,0:T(8,128)(2,1)S(1)}, u32[]{:S(2)}, u32[]{:S(2)}) %all-to-all-start) | async-done | bytes 786464 | tf_op jit(solution)/shard_map/all_to_all | solution.py:401
  75.4 0.2 broadcast_select_fusion.3
  75.7 4.6 %collective-permute-start.7 = (bf16[3,34304]{1,0:T(4,128)(2,1)S(1)}, bf16[3,34304]{1,0:T(4,128)(2,1)S(1)}, u32[]{:S(2)}, u32[]{:S(2)}) collective-permute-start(bf16[3,34304]{1,0:T(4,128)(2,1)S(1)} %get-tuple-element.56), channel_id=1, source_target_pairs={{8,16},{16,8},{24,32},{32,24},{40,48},{48,40},{56,64},{64,56},{72,... | collective-permute-start | bytes 617480 | tf_op jit(solution)/shard_map/ppermute | solution.py:368
  80.2 0.1 collective-permute-start.8
  80.3 0.1 reduce_sum.24
  80.4 0.8 broadcast_in_dim.4
  81.2 7.9 %all-to-all-start.1 = ((bf16[64,8,384]{2,1,0:T(8,128)(2,1)}), bf16[64,8,384]{2,1,0:T(8,128)(2,1)S(1)}, u32[]{:S(2)}, u32[]{:S(2)}) async-start(bf16[64,8,384]{2,1,0:T(8,128)(2,1)} %bitcast.10), calls=%async_computation.1 | async-start | bytes 786432 | tf_op jit(solution)/shard_map/all_to_all | solution.py:401
  89.2 0.2 broadcast_select_fusion.1
  89.4 0.3 pad_maximum_fusion.1.rows
  89.7 14.6 %all-to-all-done.1 = bf16[64,8,384]{2,1,0:T(8,128)(2,1)S(1)} async-done(((bf16[64,8,384]{2,1,0:T(8,128)(2,1)}), bf16[64,8,384]{2,1,0:T(8,128)(2,1)S(1)}, u32[]{:S(2)}, u32[]{:S(2)}) %all-to-all-start.1) | async-done | bytes 393248 | tf_op jit(solution)/shard_map/all_to_all | solution.py:401
  104.2 0.1 reduce_sum.25
  104.3 1.0 broadcast_in_dim.5
  105.3 3.6 %all-to-all-start.2 = ((bf16[128,8,384]{2,1,0:T(8,128)(2,1)}), bf16[128,8,384]{2,1,0:T(8,128)(2,1)S(1)}, u32[]{:S(2)}, u32[]{:S(2)}) async-start(bf16[128,8,384]{2,1,0:T(8,128)(2,1)} %bitcast.12), calls=%async_computation.2 | async-start | bytes 1572864 | tf_op jit(solution)/shard_map/all_to_all | solution.py:401
  108.9 0.1 rev.3.dww
  109.0 6.6 %transposed_conv.1 = bf16[8,32768]{1,0:T(8,128)(2,1)} custom-call(bf16[8,32768]{1,0:T(8,128)(2,1)S(1)} %get-tuple-element.36.own, bf16[8,768]{1,0:T(8,128)(2,1)S(1)} %get-tuple-element.40.left, bf16[8,768]{1,0:T(8,128)(2,1)S(1)} %get-tuple-element.41.right, bf16[6,34304]{1,0:T(8,128)(2,1)S(1)} %pad_maximum_fusion.1.rows, bf16[8,32768]{1,0:T(8,128)(2,1)S(1)} %copy-done.2, ...), custom_call_target="tpu_custom_call" | custom-call | flops 200000000 | bytes 41943040 | tf_op jit(solution)/shard_map/transposed_conv/pallas_call | solution.py:321
  115.6 6.0 %all-to-all-done.2.mine = bf16[128,8,384]{2,1,0:T(8,128)(2,1)S(1)} async-done(((bf16[128,8,384]{2,1,0:T(8,128)(2,1)}), bf16[128,8,384]{2,1,0:T(8,128)(2,1)S(1)}, u32[]{:S(2)}, u32[]{:S(2)}) %all-to-all-start.2) | async-done | bytes 786464 | tf_op jit(solution)/shard_map/all_to_all | solution.py:401
  121.6 2.0 %collective-permute-start.9 = (bf16[128,8,384]{2,1,0:T(8,128)(2,1)S(1)}, bf16[128,8,384]{2,1,0:T(8,128)(2,1)S(1)}, u32[]{:S(2)}, u32[]{:S(2)}) collective-permute-start(bf16[128,8,384]{2,1,0:T(8,128)(2,1)S(1)} %all-to-all-done.2.mine), channel_id=1, source_target_pairs={{0,8},{8,0},{16,24},{24,16},{32,40},{40,32},{48,56},{56,48},{64,72... | collective-permute-start | bytes 2359304 | tf_op jit(solution)/shard_map/ppermute | solution.py:420
  123.6 1.9 %collective-permute-done.9.other = bf16[128,8,384]{2,1,0:T(8,128)(2,1)S(1)} collective-permute-done((bf16[128,8,384]{2,1,0:T(8,128)(2,1)S(1)}, bf16[128,8,384]{2,1,0:T(8,128)(2,1)S(1)}, u32[]{:S(2)}, u32[]{:S(2)}) %collective-permute-start.9) | collective-permute-done | bytes 786464 | tf_op jit(solution)/shard_map/ppermute | solution.py:420
  125.5 1.8 %clip.1 = (f32[49,256]{1,0:T(8,128)}, f32[1,256]{1,0:T(1,128)}, f32[1,256]{1,0:T(1,128)}, f32[1,256]{1,0:T(1,128)}, f32[256,1024]{1,0:T(8,128)}, /*index=5*/f32[...) custom-call(s32[1]{0:T(128)} %bitcast.core, bf16[128,8,384]{2,1,0:T(8,128)(2,1)S(1)} %all-to-all-done.2.mine, ...), custom_call_target="tpu_custom_call" | custom-call | tf_op jit(solution)/shard_map/clip/pallas_call | solution.py:334
  (28 shorter events, 0.1 us)
Async XLA Ops:
  1.4 4.5 %collective-permute-start.1 = (bf16[8,768]{1,0:T(8,128)(2,1)S(1)}, bf16[8,768]{1,0:T(8,128)(2,1)S(1)}, u32[]{:S(2)}, u32[]{:S(2)}) collective-permute-start(bf16[8,768]{1,0:T(8,128)(2,1)S(1)} %get-tuple-element.68), channel_id=1, source_target_pairs={{0,1},{1,0},{2,3},{3,2},{4,5},{5,4},{6,7},{7,6},{8,9},{9,8},{10,11... | collective-permute-start | bytes 36872 | tf_op jit(solution)/shard_map/ppermute | solution.py:359
  3.5 7.2 %copy-start.10 = (bf16[1024,256]{1,0:T(8,128)(2,1)S(1)}, bf16[1024,256]{1,0:T(8,128)(2,1)}, u32[]{:S(2)}) copy-start(bf16[1024,256]{1,0:T(8,128)(2,1)} %param.19) | copy-start | bytes 1572868
  3.5 2.3 %collective-permute-start = (bf16[8,768]{1,0:T(8,128)(2,1)S(1)}, bf16[8,768]{1,0:T(8,128)(2,1)S(1)}, u32[]{:S(2)}, u32[]{:S(2)}) collective-permute-start(bf16[8,768]{1,0:T(8,128)(2,1)S(1)} %get-tuple-element.69), channel_id=1, source_target_pairs={{1,2},{2,1},{3,4},{4,3},{5,6},{6,5},{9,10},{10,9},{11,12},{12,11},... | collective-permute-start | bytes 36872 | tf_op jit(solution)/shard_map/ppermute | solution.py:360
  5.9 5.0 %copy-start.1 = (bf16[256,1024]{1,0:T(8,128)(2,1)S(1)}, bf16[256,1024]{1,0:T(8,128)(2,1)}, u32[]{:S(2)}) copy-start(bf16[256,1024]{1,0:T(8,128)(2,1)} %w_in.1) | copy-start | bytes 1572868
  6.2 8.6 %collective-permute-start.2 = (bf16[3,34304]{1,0:T(4,128)(2,1)S(1)}, bf16[3,34304]{1,0:T(4,128)(2,1)S(1)}, u32[]{:S(2)}, u32[]{:S(2)}) collective-permute-start(bf16[3,34304]{1,0:T(4,128)(2,1)S(1)} %get-tuple-element.60), channel_id=1, source_target_pairs={{8,16},{16,8},{24,32},{32,24},{40,48},{48,40},{56,64},{64,56},{72,... | collective-permute-start | bytes 617480 | tf_op jit(solution)/shard_map/ppermute | solution.py:368
  10.6 4.2 %collective-permute-start.3 = (bf16[3,34304]{1,0:T(4,128)(2,1)S(1)}, bf16[3,34304]{1,0:T(4,128)(2,1)}, u32[]{:S(2)}, u32[]{:S(2)}) collective-permute-start(bf16[3,34304]{1,0:T(4,128)(2,1)S(1)} %get-tuple-element.61), channel_id=1, source_target_pairs={{0,8},{8,0},{16,24},{24,16},{32,40},{40,32},{48,56},{56,48},{64,72... | collective-permute-start | bytes 617480 | tf_op jit(solution)/shard_map/ppermute | solution.py:369
  11.1 5.1 %copy-start = (bf16[8,32768]{1,0:T(8,128)(2,1)S(1)}, bf16[8,32768]{1,0:T(8,128)(2,1)}, u32[]{:S(2)}) copy-start(bf16[8,32768]{1,0:T(8,128)(2,1)} %own.1) | copy-start | bytes 1572868
  11.2 5.1 %copy-start.2 = (bf16[8,32768]{1,0:T(8,128)(2,1)S(1)}, bf16[8,32768]{1,0:T(8,128)(2,1)}, u32[]{:S(2)}) copy-start(bf16[8,32768]{1,0:T(8,128)(2,1)} %grad.3) | copy-start | bytes 1572868
  11.2 5.1 %copy-start.3 = (f32[49,256]{1,0:T(8,128)S(1)}, f32[49,256]{1,0:T(8,128)}, u32[]{:S(2)}) copy-start(f32[49,256]{1,0:T(8,128)} %dww.1) | copy-start | bytes 150532
  11.2 5.1 %copy-start.4 = (f32[1024]{0:T(1024)S(1)}, f32[1024]{0:T(1024)}, u32[]{:S(2)}) copy-start(f32[1024]{0:T(1024)} %param.18) | copy-start | bytes 12292
  11.2 5.1 %copy-start.5 = (f32[256]{0:T(256)S(1)}, f32[256]{0:T(256)}, u32[]{:S(2)}) copy-start(f32[256]{0:T(256)} %param.14) | copy-start | bytes 3076
  11.2 5.1 %copy-start.6 = (f32[256]{0:T(256)S(1)}, f32[256]{0:T(256)}, u32[]{:S(2)}) copy-start(f32[256]{0:T(256)} %param.15) | copy-start | bytes 3076
  11.2 5.1 %copy-start.7 = (f32[256]{0:T(256)S(1)}, f32[256]{0:T(256)}, u32[]{:S(2)}) copy-start(f32[256]{0:T(256)} %param.16) | copy-start | bytes 3076
  11.2 5.1 %copy-start.8 = (f32[256]{0:T(256)S(1)}, f32[256]{0:T(256)}, u32[]{:S(2)}) copy-start(f32[256]{0:T(256)} %param.20) | copy-start | bytes 3076
  11.2 5.1 %copy-start.9 = (f32[256]{0:T(256)S(1)}, f32[256]{0:T(256)}, u32[]{:S(2)}) copy-start(f32[256]{0:T(256)} %param.21) | copy-start | bytes 3076
  41.8 2.4 %collective-permute-start.4 = (bf16[128,8,384]{2,1,0:T(8,128)(2,1)S(1)}, bf16[128,8,384]{2,1,0:T(8,128)(2,1)S(1)}, u32[]{:S(2)}, u32[]{:S(2)}) collective-permute-start(bf16[128,8,384]{2,1,0:T(8,128)(2,1)S(1)} %get-tuple-element.33), channel_id=1, source_target_pairs={{0,8},{8,0},{16,24},{24,16},{32,40},{40,32},{48,56},{56,48},{64,72... | collective-permute-start | bytes 2359304 | tf_op jit(solution)/shard_map/ppermute | solution.py:407
  45.3 18.1 %collective-permute-start.6 = (bf16[8,768]{1,0:T(8,128)(2,1)S(1)}, bf16[8,768]{1,0:T(8,128)(2,1)S(1)}, u32[]{:S(2)}, u32[]{:S(2)}) collective-permute-start(bf16[8,768]{1,0:T(8,128)(2,1)S(1)} %get-tuple-element.64), channel_id=1, source_target_pairs={{0,1},{1,0},{2,3},{3,2},{4,5},{5,4},{6,7},{7,6},{8,9},{9,8},{10,11... | collective-permute-start | bytes 36872 | tf_op jit(solution)/shard_map/ppermute | solution.py:359
  49.2 14.2 %collective-permute-start.5 = (bf16[8,768]{1,0:T(8,128)(2,1)S(1)}, bf16[8,768]{1,0:T(8,128)(2,1)S(1)}, u32[]{:S(2)}, u32[]{:S(2)}) collective-permute-start(bf16[8,768]{1,0:T(8,128)(2,1)S(1)} %get-tuple-element.65), channel_id=1, source_target_pairs={{1,2},{2,1},{3,4},{4,3},{5,6},{6,5},{9,10},{10,9},{11,12},{12,11},... | collective-permute-start | bytes 36872 | tf_op jit(solution)/shard_map/ppermute | solution.py:360
  50.1 25.4 %all-to-all-start = ((bf16[128,8,384]{2,1,0:T(8,128)(2,1)}), bf16[128,8,384]{2,1,0:T(8,128)(2,1)S(1)}, u32[]{:S(2)}, u32[]{:S(2)}) async-start(bf16[128,8,384]{2,1,0:T(8,128)(2,1)} %add_convert_fusion), calls=%async_computation | async-start | bytes 1572864 | tf_op jit(solution)/shard_map/all_to_all | solution.py:401
  75.7 13.5 %collective-permute-start.7 = (bf16[3,34304]{1,0:T(4,128)(2,1)S(1)}, bf16[3,34304]{1,0:T(4,128)(2,1)S(1)}, u32[]{:S(2)}, u32[]{:S(2)}) collective-permute-start(bf16[3,34304]{1,0:T(4,128)(2,1)S(1)} %get-tuple-element.56), channel_id=1, source_target_pairs={{8,16},{16,8},{24,32},{32,24},{40,48},{48,40},{56,64},{64,56},{72,... | collective-permute-start | bytes 617480 | tf_op jit(solution)/shard_map/ppermute | solution.py:368
  80.2 8.9 %collective-permute-start.8 = (bf16[3,34304]{1,0:T(4,128)(2,1)S(1)}, bf16[3,34304]{1,0:T(4,128)(2,1)S(1)}, u32[]{:S(2)}, u32[]{:S(2)}) collective-permute-start(bf16[3,34304]{1,0:T(4,128)(2,1)S(1)} %get-tuple-element.57), channel_id=1, source_target_pairs={{0,8},{8,0},{16,24},{24,16},{32,40},{40,32},{48,56},{56,48},{64,72... | collective-permute-start | bytes 617480 | tf_op jit(solution)/shard_map/ppermute | solution.py:369
  81.2 23.0 %all-to-all-start.1 = ((bf16[64,8,384]{2,1,0:T(8,128)(2,1)}), bf16[64,8,384]{2,1,0:T(8,128)(2,1)S(1)}, u32[]{:S(2)}, u32[]{:S(2)}) async-start(bf16[64,8,384]{2,1,0:T(8,128)(2,1)} %bitcast.10), calls=%async_computation.1 | async-start | bytes 786432 | tf_op jit(solution)/shard_map/all_to_all | solution.py:401
  105.3 16.3 %all-to-all-start.2 = ((bf16[128,8,384]{2,1,0:T(8,128)(2,1)}), bf16[128,8,384]{2,1,0:T(8,128)(2,1)S(1)}, u32[]{:S(2)}, u32[]{:S(2)}) async-start(bf16[128,8,384]{2,1,0:T(8,128)(2,1)} %bitcast.12), calls=%async_computation.2 | async-start | bytes 1572864 | tf_op jit(solution)/shard_map/all_to_all | solution.py:401
  121.6 3.9 %collective-permute-start.9 = (bf16[128,8,384]{2,1,0:T(8,128)(2,1)S(1)}, bf16[128,8,384]{2,1,0:T(8,128)(2,1)S(1)}, u32[]{:S(2)}, u32[]{:S(2)}) collective-permute-start(bf16[128,8,384]{2,1,0:T(8,128)(2,1)S(1)} %all-to-all-done.2.mine), channel_id=1, source_target_pairs={{0,8},{8,0},{16,24},{24,16},{32,40},{40,32},{48,56},{56,48},{64,72... | collective-permute-start | bytes 2359304 | tf_op jit(solution)/shard_map/ppermute | solution.py:420

commit v6 on v5

--- a/solution.py
+++ b/solution.py
@@ -71,27 +71,36 @@
     shift_rows(own, left, right, rows, tall, shifted)
     spread_weights(dww, spread)
 
-    def forward(n, carry):
+    def normalize(n):
+        first = n * JB
+        block = conv[pl.ds(first, JB)].reshape(JB * 8, C) + dwb[...]
+        center = block - jnp.mean(block, axis=-1, keepdims=True)
+        inverse = lax.rsqrt(jnp.mean(center * center, axis=-1, keepdims=True) + eps_norm)
+        norm = center * inverse
+        at = pl.ds(pl.multiple_of(first * 8, 64), JB * 8)
+        normed[at, :] = norm
+        inv[at, :] = inverse
+        lnout[at, :] = (norm * gain[...] + lnb[...]).astype(BF16)
+
+    def convolve(n):
         first = n * JB
         for lane in range(2):
             lanes = slice(lane * 128, lane * 128 + 128)
             for o, acc in enumerate(conv_block(shifted, spread, first, lane)):
                 conv[first + o, :, lanes] = acc
-        block = conv[pl.ds(first, JB)].reshape(JB * 8, C) + dwb[...]
-        center = block - jnp.mean(block, axis=-1, keepdims=True)
-        inverse = lax.rsqrt(jnp.mean(center * center, axis=-1, keepdims=True) + eps_norm)
-        norm = center * inverse
-        rows = pl.ds(pl.multiple_of(first * 8, 64), JB * 8)
-        normed[rows, :] = norm
-        inv[rows, :] = inverse
-        lnout[rows, :] = (norm * gain[...] + lnb[...]).astype(BF16)
         for o in range(JB):
             at = pl.multiple_of((first + o) * C, C)
             g = grad[:, pl.ds(at, C)].astype(F32)
             grad_flat[pl.ds(pl.multiple_of((first + o) * 8, 8), 8), :] = g
+
+    def forward(n, carry):
+        normalize(n - 1)
+        convolve(n)
         return carry
 
-    lax.fori_loop(0, COLS // JB, forward, 0)
+    convolve(0)
+    lax.fori_loop(1, COLS // JB, forward, 0)
+    normalize(COLS // JB - 1)
 
     CH = 256
 
@@ -128,7 +137,7 @@
                 dpre[out, lanes] = (dact[sub, lanes] * slope).astype(BF16)
             return c
 
-        lax.fori_loop(0, CH // 16, gelu, 0)
+        lax.fori_loop(0, CH // 16, gelu, 0, unroll=4)
         dact[:, 0:C] = jnp.dot(dpre[rows, :], w_in_t[...], preferred_element_type=F32)
 
         def back(m, c):
@@ -153,7 +162,7 @@
                 dconv_out[:, pl.ds(pl.multiple_of((j0 + o) * C, C), C)] = wide[o].astype(BF16)
             return s_gain, s_lnb, s_dwb
 
-        s_gain, s_lnb, s_dwb = lax.fori_loop(0, CH // 64, back, (s_gain, s_lnb, s_dwb))
+        s_gain, s_lnb, s_dwb = lax.fori_loop(0, CH // 64, back, (s_gain, s_lnb, s_dwb), unroll=2)
         return s_gain, s_lnb, s_g, s_dwb
 
     for n in range(PIX // CH):
@@ -358,13 +367,13 @@
     first, last = x[:, : 3 * C], x[:, -3 * C :]
     near = lax.ppermute(jnp.where(even, last, first), "wa", inner)
     far = lax.ppermute(jnp.where(even, first, last), "wa", outer)
+    if after is not None:
+        near, far, after = lax.optimization_barrier((near, far, after))
     left, right = jnp.where(even, far, near), jnp.where(even, near, far)
     inner, outer = pair_swaps(lax.axis_size("ha"))
     even = core[0] == 0
     last = jnp.concatenate([left[5:], x[5:], right[5:]], axis=1)
     lead = jnp.concatenate([left[:3], x[:3], right[:3]], axis=1)
-    if after is not None:
-        lead, last, after = lax.optimization_barrier((lead, last, after))
     crossed = lax.ppermute(jnp.where(even, lead, last), "ha", outer)
     swapped = lax.ppermute(jnp.where(even, last, lead), "ha", inner)
     top, bottom = jnp.where(even, crossed, swapped), jnp.where(even, swapped, crossed)

time: 128 us -> 118 us (0.922)
  waiting for transfers between devices: 40 us -> 34.8 us
  Pallas kernels: 33.9 us -> 31.4 us
    all_to_all x3, waiting for transfers between devices: 32.3 us -> 24.8 us  [exchange(): lax.all_to_all(x, ('ha', 'wa'), 0, 0, axis_index_groups=groups, tiled=True)]
    pallas_call x1, Pallas kernels: 25.5 us -> 22.2 us  [run_main(): pl.pallas_call(main_kernel, out_shape=(jax.ShapeDtypeStruct((ROWS, COLS *...]
    ppermute x2, waiting for transfers between devices: 0.01 us -> 2.23 us  [halo(): near = lax.ppermute(jnp.where(even, last, first), 'wa', inner)]
  transfers between devices with their start and end apart: 13 -> 13, of which waited for: 6 -> 7; matrix products, arithmetic and copies ran while one was open for 3% -> 3% of each run, Pallas kernels for 5% -> 6%
where the time goes in v6:
time: 118 us
  starting transfers between devices  43.1 us (37%)
  waiting for transfers between devices  34.8 us (29%)
  Pallas kernels  31.4 us (27%)
  local copies, waits for them, and re-layouts  4.01 us (3%)
  other arithmetic  3.56 us (3%)
    all_to_all x3, waiting for transfers between devices, exchange(): lax.all_to_all(x, ('ha', 'wa'), 0, 0, axis_index_groups=groups, tiled=True)  24.8 us
    all_to_all x3, starting transfers between devices, exchange(): lax.all_to_all(x, ('ha', 'wa'), 0, 0, axis_index_groups=groups, tiled=True)  24.7 us
    pallas_call x1, Pallas kernels, run_main(): pl.pallas_call(main_kernel, out_shape=(jax.ShapeDtypeStruct((ROWS, COLS *...  22.2 us
    ppermute x2, starting transfers between devices, halo(): crossed = lax.ppermute(jnp.where(even, lead, last), 'ha', outer)  7.92 us
    pallas_call x1, Pallas kernels, run_transposed(): pl.pallas_call(transposed_kernel, out_shape=jax.ShapeDtypeStruct((ROWS, C...  7.47 us
    ppermute x2, starting transfers between devices, halo(): near = lax.ppermute(jnp.where(even, last, first), 'wa', inner)  6 us
    ppermute x2, waiting for transfers between devices, halo(): crossed = lax.ppermute(jnp.where(even, lead, last), 'ha', outer)  3.53 us
    ppermute x1, starting transfers between devices, on_device(): other = lax.ppermute(mine, 'ha', swap)  2.72 us
  transfers between devices with their start and end apart: 13, of which 7 were waited for; matrix products, arithmetic and copies ran while one was open for 3% of the time, Pallas kernels for 6%

profile of v6, /device:TPU:1, one launch (start us, length us, event | category | flops | bytes accessed | tf_op | source)
XLA Modules:
  0.0 117.9 jit_solution(9187643990763986463)
XLA Ops:
  0.6 0.7 broadcast_select_fusion.14
  1.4 2.1 %collective-permute-start.1 = (bf16[8,768]{1,0:T(8,128)(2,1)S(1)}, bf16[8,768]{1,0:T(8,128)(2,1)S(1)}, u32[]{:S(2)}, u32[]{:S(2)}) collective-permute-start(bf16[8,768]{1,0:T(8,128)(2,1)S(1)} %get-tuple-element.68), channel_id=1, source_target_pairs={{0,1},{1,0},{2,3},{3,2},{4,5},{5,4},{6,7},{7,6},{8,9},{9,8},{10,11... | collective-permute-start | bytes 36872 | tf_op jit(solution)/shard_map/ppermute | solution.py:368
  3.5 0.8 collective-permute-start
  4.3 1.5 %fusion.1 = (bf16[3,32768]{1,0:T(4,128)(2,1)S(1)}, bf16[3,32768]{1,0:T(4,128)(2,1)S(1)}) fusion(bf16[8,32768]{1,0:T(8,128)(2,1)} %own.1), kind=kLoop, calls=%fused_computation.24 | loop fusion | bytes 786432 | tf_op jit(solution)/shard_map/slice | solution.py:376
  5.8 0.0 copy-start.1
  5.9 0.3 broadcast_select_fusion.7
  6.1 4.4 %collective-permute-start.2 = (bf16[3,34304]{1,0:T(4,128)(2,1)S(1)}, bf16[3,34304]{1,0:T(4,128)(2,1)S(1)}, u32[]{:S(2)}, u32[]{:S(2)}) collective-permute-start(bf16[3,34304]{1,0:T(4,128)(2,1)S(1)} %get-tuple-element.60), channel_id=1, source_target_pairs={{8,16},{16,8},{24,32},{32,24},{40,48},{48,40},{56,64},{64,56},{72,... | collective-permute-start | bytes 617480 | tf_op jit(solution)/shard_map/ppermute | solution.py:377
  10.5 0.1 collective-permute-start.3
  10.7 0.2 copy.24
  10.9 0.2 copy.23
  11.1 0.0 copy-start
  11.1 0.0 copy-start.2
  11.1 0.0 copy-start.3
  11.1 0.0 copy-start.4
  11.1 0.0 copy-start.5
  11.2 0.0 copy-start.8
  11.2 0.0 copy-start.9
  11.2 3.5 %collective-permute-done.2 = bf16[3,34304]{1,0:T(4,128)(2,1)S(1)} collective-permute-done((bf16[3,34304]{1,0:T(4,128)(2,1)S(1)}, bf16[3,34304]{1,0:T(4,128)(2,1)S(1)}, u32[]{:S(2)}, u32[]{:S(2)}) %collective-permute-start.2) | collective-permute-done | bytes 205856 | tf_op jit(solution)/shard_map/ppermute | solution.py:377
  14.7 0.2 broadcast_select_fusion.5
  14.9 0.3 pad_maximum_fusion.rows
  15.3 22.2 %block_backward.1 = (bf16[8,32768]{1,0:T(8,128)(2,1)S(1)}, bf16[128,8,384]{2,1,0:T(8,128)(2,1)S(1)}, bf16[128,8,384]{2,1,0:T(8,128)(2,1)S(1)}) custom-call(s32[1]{0:T(128)} %bitcast.core, bf16[8,32768]{1,0:T(8,128)(2,1)S(1)} %copy-done, bf16[8,768]{1,0:T(8,128)(2,1)S(1)} %get-tuple-element.73.left, bf16[8,768]{1,0:T(8,128)(2,1)S(1)} %get-tuple-element.72.right, ...), custom_call_target="tpu_custom_call" | custom-call | tf_op jit(solution)/shard_map/block_backward/pallas_call | solution.py:298
  37.5 0.1 collective-permute-start.4
  37.6 2.3 %collective-permute-done.4 = bf16[128,8,384]{2,1,0:T(8,128)(2,1)S(1)} collective-permute-done((bf16[128,8,384]{2,1,0:T(8,128)(2,1)S(1)}, bf16[128,8,384]{2,1,0:T(8,128)(2,1)S(1)}, u32[]{:S(2)}, u32[]{:S(2)}) %collective-permute-start.4) | collective-permute-done | bytes 786464 | tf_op jit(solution)/shard_map/ppermute | solution.py:416
  39.8 1.1 add_convert_fusion
  40.9 13.2 %all-to-all-start = ((bf16[128,8,384]{2,1,0:T(8,128)(2,1)}), bf16[128,8,384]{2,1,0:T(8,128)(2,1)S(1)}, u32[]{:S(2)}, u32[]{:S(2)}) async-start(bf16[128,8,384]{2,1,0:T(8,128)(2,1)} %add_convert_fusion), calls=%async_computation | async-start | bytes 1572864 | tf_op jit(solution)/shard_map/all_to_all | solution.py:410
  54.1 0.7 collective-permute-start.6
  54.8 3.9 %collective-permute-start.5 = (bf16[8,768]{1,0:T(8,128)(2,1)S(1)}, bf16[8,768]{1,0:T(8,128)(2,1)S(1)}, u32[]{:S(2)}, u32[]{:S(2)}) collective-permute-start(bf16[8,768]{1,0:T(8,128)(2,1)S(1)} %get-tuple-element.65), channel_id=1, source_target_pairs={{0,1},{1,0},{2,3},{3,2},{4,5},{5,4},{6,7},{7,6},{8,9},{9,8},{10,11... | collective-permute-start | bytes 36872 | tf_op jit(solution)/shard_map/ppermute | solution.py:368
  58.7 0.2 fusion
  58.9 2.2 %collective-permute-done.5 = bf16[8,768]{1,0:T(8,128)(2,1)S(1)} collective-permute-done((bf16[8,768]{1,0:T(8,128)(2,1)S(1)}, bf16[8,768]{1,0:T(8,128)(2,1)S(1)}, u32[]{:S(2)}, u32[]{:S(2)}) %collective-permute-start.5) | collective-permute-done | bytes 12320 | tf_op jit(solution)/shard_map/ppermute | solution.py:368
  61.1 5.7 %all-to-all-done = bf16[128,8,384]{2,1,0:T(8,128)(2,1)S(1)} async-done(((bf16[128,8,384]{2,1,0:T(8,128)(2,1)}), bf16[128,8,384]{2,1,0:T(8,128)(2,1)S(1)}, u32[]{:S(2)}, u32[]{:S(2)}) %all-to-all-start) | async-done | bytes 786464 | tf_op jit(solution)/shard_map/all_to_all | solution.py:410
  66.8 0.3 broadcast_select_fusion.3
  67.1 3.5 %collective-permute-start.7 = (bf16[3,34304]{1,0:T(4,128)(2,1)S(1)}, bf16[3,34304]{1,0:T(4,128)(2,1)S(1)}, u32[]{:S(2)}, u32[]{:S(2)}) collective-permute-start(bf16[3,34304]{1,0:T(4,128)(2,1)S(1)} %get-tuple-element.56), channel_id=1, source_target_pairs={{8,16},{16,8},{24,32},{32,24},{40,48},{48,40},{56,64},{64,56},{72,... | collective-permute-start | bytes 617480 | tf_op jit(solution)/shard_map/ppermute | solution.py:377
  70.7 0.1 collective-permute-start.8
  70.8 0.1 reduce_sum.24
  70.9 0.8 broadcast_in_dim.4
  71.7 7.9 %all-to-all-start.1 = ((bf16[64,8,384]{2,1,0:T(8,128)(2,1)}), bf16[64,8,384]{2,1,0:T(8,128)(2,1)S(1)}, u32[]{:S(2)}, u32[]{:S(2)}) async-start(bf16[64,8,384]{2,1,0:T(8,128)(2,1)} %bitcast.10), calls=%async_computation.1 | async-start | bytes 786432 | tf_op jit(solution)/shard_map/all_to_all | solution.py:410
  79.6 0.2 broadcast_select_fusion.1
  79.8 0.3 pad_maximum_fusion.1.rows
  80.1 14.6 %all-to-all-done.1 = bf16[64,8,384]{2,1,0:T(8,128)(2,1)S(1)} async-done(((bf16[64,8,384]{2,1,0:T(8,128)(2,1)}), bf16[64,8,384]{2,1,0:T(8,128)(2,1)S(1)}, u32[]{:S(2)}, u32[]{:S(2)}) %all-to-all-start.1) | async-done | bytes 393248 | tf_op jit(solution)/shard_map/all_to_all | solution.py:410
  94.7 0.1 reduce_sum.25
  94.7 1.0 broadcast_in_dim.5
  95.7 3.6 %all-to-all-start.2 = ((bf16[128,8,384]{2,1,0:T(8,128)(2,1)}), bf16[128,8,384]{2,1,0:T(8,128)(2,1)S(1)}, u32[]{:S(2)}, u32[]{:S(2)}) async-start(bf16[128,8,384]{2,1,0:T(8,128)(2,1)} %bitcast.12), calls=%async_computation.2 | async-start | bytes 1572864 | tf_op jit(solution)/shard_map/all_to_all | solution.py:410
  99.3 0.1 rev.3.dww
  99.4 7.5 %transposed_conv.1 = bf16[8,32768]{1,0:T(8,128)(2,1)} custom-call(bf16[8,32768]{1,0:T(8,128)(2,1)S(1)} %get-tuple-element.36.own, bf16[8,768]{1,0:T(8,128)(2,1)S(1)} %get-tuple-element.40.left, bf16[8,768]{1,0:T(8,128)(2,1)S(1)} %get-tuple-element.41.right, bf16[6,34304]{1,0:T(8,128)(2,1)S(1)} %pad_maximum_fusion.1.rows, bf16[8,32768]{1,0:T(8,128)(2,1)S(1)} %copy-done.2, ...), custom_call_target="tpu_custom_call" | custom-call | flops 200000000 | bytes 41943040 | tf_op jit(solution)/shard_map/transposed_conv/pallas_call | solution.py:330
  106.9 4.6 %all-to-all-done.2.mine = bf16[128,8,384]{2,1,0:T(8,128)(2,1)S(1)} async-done(((bf16[128,8,384]{2,1,0:T(8,128)(2,1)}), bf16[128,8,384]{2,1,0:T(8,128)(2,1)S(1)}, u32[]{:S(2)}, u32[]{:S(2)}) %all-to-all-start.2) | async-done | bytes 786464 | tf_op jit(solution)/shard_map/all_to_all | solution.py:410
  111.5 2.7 %collective-permute-start.9 = (bf16[128,8,384]{2,1,0:T(8,128)(2,1)S(1)}, bf16[128,8,384]{2,1,0:T(8,128)(2,1)S(1)}, u32[]{:S(2)}, u32[]{:S(2)}) collective-permute-start(bf16[128,8,384]{2,1,0:T(8,128)(2,1)S(1)} %all-to-all-done.2.mine), channel_id=1, source_target_pairs={{0,8},{8,0},{16,24},{24,16},{32,40},{40,32},{48,56},{56,48},{64,72... | collective-permute-start | bytes 2359304 | tf_op jit(solution)/shard_map/ppermute | solution.py:429
  114.2 1.9 %collective-permute-done.9.other = bf16[128,8,384]{2,1,0:T(8,128)(2,1)S(1)} collective-permute-done((bf16[128,8,384]{2,1,0:T(8,128)(2,1)S(1)}, bf16[128,8,384]{2,1,0:T(8,128)(2,1)S(1)}, u32[]{:S(2)}, u32[]{:S(2)}) %collective-permute-start.9) | collective-permute-done | bytes 786464 | tf_op jit(solution)/shard_map/ppermute | solution.py:429
  116.1 1.8 %clip.1 = (f32[49,256]{1,0:T(8,128)}, f32[1,256]{1,0:T(1,128)}, f32[1,256]{1,0:T(1,128)}, f32[1,256]{1,0:T(1,128)}, f32[256,1024]{1,0:T(8,128)}, /*index=5*/f32[...) custom-call(s32[1]{0:T(128)} %bitcast.core, bf16[128,8,384]{2,1,0:T(8,128)(2,1)S(1)} %all-to-all-done.2.mine, ...), custom_call_target="tpu_custom_call" | custom-call | tf_op jit(solution)/shard_map/clip/pallas_call | solution.py:343
  (26 shorter events, 0.1 us)
Async XLA Ops:
  1.4 4.4 %collective-permute-start.1 = (bf16[8,768]{1,0:T(8,128)(2,1)S(1)}, bf16[8,768]{1,0:T(8,128)(2,1)S(1)}, u32[]{:S(2)}, u32[]{:S(2)}) collective-permute-start(bf16[8,768]{1,0:T(8,128)(2,1)S(1)} %get-tuple-element.68), channel_id=1, source_target_pairs={{0,1},{1,0},{2,3},{3,2},{4,5},{5,4},{6,7},{7,6},{8,9},{9,8},{10,11... | collective-permute-start | bytes 36872 | tf_op jit(solution)/shard_map/ppermute | solution.py:368
  3.5 7.1 %copy-start.10 = (bf16[1024,256]{1,0:T(8,128)(2,1)S(1)}, bf16[1024,256]{1,0:T(8,128)(2,1)}, u32[]{:S(2)}) copy-start(bf16[1024,256]{1,0:T(8,128)(2,1)} %param.19) | copy-start | bytes 1572868
  3.5 2.3 %collective-permute-start = (bf16[8,768]{1,0:T(8,128)(2,1)S(1)}, bf16[8,768]{1,0:T(8,128)(2,1)S(1)}, u32[]{:S(2)}, u32[]{:S(2)}) collective-permute-start(bf16[8,768]{1,0:T(8,128)(2,1)S(1)} %get-tuple-element.69), channel_id=1, source_target_pairs={{1,2},{2,1},{3,4},{4,3},{5,6},{6,5},{9,10},{10,9},{11,12},{12,11},... | collective-permute-start | bytes 36872 | tf_op jit(solution)/shard_map/ppermute | solution.py:369
  5.8 5.0 %copy-start.1 = (bf16[256,1024]{1,0:T(8,128)(2,1)S(1)}, bf16[256,1024]{1,0:T(8,128)(2,1)}, u32[]{:S(2)}) copy-start(bf16[256,1024]{1,0:T(8,128)(2,1)} %w_in.1) | copy-start | bytes 1572868
  6.1 8.6 %collective-permute-start.2 = (bf16[3,34304]{1,0:T(4,128)(2,1)S(1)}, bf16[3,34304]{1,0:T(4,128)(2,1)S(1)}, u32[]{:S(2)}, u32[]{:S(2)}) collective-permute-start(bf16[3,34304]{1,0:T(4,128)(2,1)S(1)} %get-tuple-element.60), channel_id=1, source_target_pairs={{8,16},{16,8},{24,32},{32,24},{40,48},{48,40},{56,64},{64,56},{72,... | collective-permute-start | bytes 617480 | tf_op jit(solution)/shard_map/ppermute | solution.py:377
  10.5 4.2 %collective-permute-start.3 = (bf16[3,34304]{1,0:T(4,128)(2,1)S(1)}, bf16[3,34304]{1,0:T(4,128)(2,1)S(1)}, u32[]{:S(2)}, u32[]{:S(2)}) collective-permute-start(bf16[3,34304]{1,0:T(4,128)(2,1)S(1)} %get-tuple-element.61), channel_id=1, source_target_pairs={{0,8},{8,0},{16,24},{24,16},{32,40},{40,32},{48,56},{56,48},{64,72... | collective-permute-start | bytes 617480 | tf_op jit(solution)/shard_map/ppermute | solution.py:378
  11.1 4.1 %copy-start = (bf16[8,32768]{1,0:T(8,128)(2,1)S(1)}, bf16[8,32768]{1,0:T(8,128)(2,1)}, u32[]{:S(2)}) copy-start(bf16[8,32768]{1,0:T(8,128)(2,1)} %own.1) | copy-start | bytes 1572868
  11.1 4.1 %copy-start.2 = (bf16[8,32768]{1,0:T(8,128)(2,1)S(1)}, bf16[8,32768]{1,0:T(8,128)(2,1)}, u32[]{:S(2)}) copy-start(bf16[8,32768]{1,0:T(8,128)(2,1)} %grad.3) | copy-start | bytes 1572868
  11.1 4.1 %copy-start.3 = (f32[49,256]{1,0:T(8,128)S(1)}, f32[49,256]{1,0:T(8,128)}, u32[]{:S(2)}) copy-start(f32[49,256]{1,0:T(8,128)} %dww.1) | copy-start | bytes 150532
  11.1 4.1 %copy-start.4 = (f32[1024]{0:T(1024)S(1)}, f32[1024]{0:T(1024)}, u32[]{:S(2)}) copy-start(f32[1024]{0:T(1024)} %param.18) | copy-start | bytes 12292
  11.1 4.1 %copy-start.5 = (f32[256]{0:T(256)S(1)}, f32[256]{0:T(256)}, u32[]{:S(2)}) copy-start(f32[256]{0:T(256)} %param.14) | copy-start | bytes 3076
  11.1 4.1 %copy-start.6 = (f32[256]{0:T(256)S(1)}, f32[256]{0:T(256)}, u32[]{:S(2)}) copy-start(f32[256]{0:T(256)} %param.15) | copy-start | bytes 3076
  11.2 4.1 %copy-start.7 = (f32[256]{0:T(256)S(1)}, f32[256]{0:T(256)}, u32[]{:S(2)}) copy-start(f32[256]{0:T(256)} %param.16) | copy-start | bytes 3076
  11.2 4.1 %copy-start.8 = (f32[256]{0:T(256)S(1)}, f32[256]{0:T(256)}, u32[]{:S(2)}) copy-start(f32[256]{0:T(256)} %param.20) | copy-start | bytes 3076
  11.2 4.1 %copy-start.9 = (f32[256]{0:T(256)S(1)}, f32[256]{0:T(256)}, u32[]{:S(2)}) copy-start(f32[256]{0:T(256)} %param.21) | copy-start | bytes 3076
  37.5 2.4 %collective-permute-start.4 = (bf16[128,8,384]{2,1,0:T(8,128)(2,1)S(1)}, bf16[128,8,384]{2,1,0:T(8,128)(2,1)S(1)}, u32[]{:S(2)}, u32[]{:S(2)}) collective-permute-start(bf16[128,8,384]{2,1,0:T(8,128)(2,1)S(1)} %get-tuple-element.33), channel_id=1, source_target_pairs={{0,8},{8,0},{16,24},{24,16},{32,40},{40,32},{48,56},{56,48},{64,72... | collective-permute-start | bytes 2359304 | tf_op jit(solution)/shard_map/ppermute | solution.py:416
  40.9 25.9 %all-to-all-start = ((bf16[128,8,384]{2,1,0:T(8,128)(2,1)}), bf16[128,8,384]{2,1,0:T(8,128)(2,1)S(1)}, u32[]{:S(2)}, u32[]{:S(2)}) async-start(bf16[128,8,384]{2,1,0:T(8,128)(2,1)} %add_convert_fusion), calls=%async_computation | async-start | bytes 1572864 | tf_op jit(solution)/shard_map/all_to_all | solution.py:410
  54.1 4.7 %collective-permute-start.6 = (bf16[8,768]{1,0:T(8,128)(2,1)S(1)}, bf16[8,768]{1,0:T(8,128)(2,1)S(1)}, u32[]{:S(2)}, u32[]{:S(2)}) collective-permute-start(bf16[8,768]{1,0:T(8,128)(2,1)S(1)} %get-tuple-element.64), channel_id=1, source_target_pairs={{1,2},{2,1},{3,4},{4,3},{5,6},{6,5},{9,10},{10,9},{11,12},{12,11},... | collective-permute-start | bytes 36872 | tf_op jit(solution)/shard_map/ppermute | solution.py:369
  54.8 6.3 %collective-permute-start.5 = (bf16[8,768]{1,0:T(8,128)(2,1)S(1)}, bf16[8,768]{1,0:T(8,128)(2,1)S(1)}, u32[]{:S(2)}, u32[]{:S(2)}) collective-permute-start(bf16[8,768]{1,0:T(8,128)(2,1)S(1)} %get-tuple-element.65), channel_id=1, source_target_pairs={{0,1},{1,0},{2,3},{3,2},{4,5},{5,4},{6,7},{7,6},{8,9},{9,8},{10,11... | collective-permute-start | bytes 36872 | tf_op jit(solution)/shard_map/ppermute | solution.py:368
  67.1 12.5 %collective-permute-start.7 = (bf16[3,34304]{1,0:T(4,128)(2,1)S(1)}, bf16[3,34304]{1,0:T(4,128)(2,1)S(1)}, u32[]{:S(2)}, u32[]{:S(2)}) collective-permute-start(bf16[3,34304]{1,0:T(4,128)(2,1)S(1)} %get-tuple-element.56), channel_id=1, source_target_pairs={{8,16},{16,8},{24,32},{32,24},{40,48},{48,40},{56,64},{64,56},{72,... | collective-permute-start | bytes 617480 | tf_op jit(solution)/shard_map/ppermute | solution.py:377
  70.7 8.9 %collective-permute-start.8 = (bf16[3,34304]{1,0:T(4,128)(2,1)S(1)}, bf16[3,34304]{1,0:T(4,128)(2,1)S(1)}, u32[]{:S(2)}, u32[]{:S(2)}) collective-permute-start(bf16[3,34304]{1,0:T(4,128)(2,1)S(1)} %get-tuple-element.57), channel_id=1, source_target_pairs={{0,8},{8,0},{16,24},{24,16},{32,40},{40,32},{48,56},{56,48},{64,72... | collective-permute-start | bytes 617480 | tf_op jit(solution)/shard_map/ppermute | solution.py:378
  71.7 23.0 %all-to-all-start.1 = ((bf16[64,8,384]{2,1,0:T(8,128)(2,1)}), bf16[64,8,384]{2,1,0:T(8,128)(2,1)S(1)}, u32[]{:S(2)}, u32[]{:S(2)}) async-start(bf16[64,8,384]{2,1,0:T(8,128)(2,1)} %bitcast.10), calls=%async_computation.1 | async-start | bytes 786432 | tf_op jit(solution)/shard_map/all_to_all | solution.py:410
  95.7 15.8 %all-to-all-start.2 = ((bf16[128,8,384]{2,1,0:T(8,128)(2,1)}), bf16[128,8,384]{2,1,0:T(8,128)(2,1)S(1)}, u32[]{:S(2)}, u32[]{:S(2)}) async-start(bf16[128,8,384]{2,1,0:T(8,128)(2,1)} %bitcast.12), calls=%async_computation.2 | async-start | bytes 1572864 | tf_op jit(solution)/shard_map/all_to_all | solution.py:410
  111.5 4.6 %collective-permute-start.9 = (bf16[128,8,384]{2,1,0:T(8,128)(2,1)S(1)}, bf16[128,8,384]{2,1,0:T(8,128)(2,1)S(1)}, u32[]{:S(2)}, u32[]{:S(2)}) collective-permute-start(bf16[128,8,384]{2,1,0:T(8,128)(2,1)S(1)} %all-to-all-done.2.mine), channel_id=1, source_target_pairs={{0,8},{8,0},{16,24},{24,16},{32,40},{40,32},{48,56},{56,48},{64,72... | collective-permute-start | bytes 2359304 | tf_op jit(solution)/shard_map/ppermute | solution.py:429

commit v7 on v6

--- a/solution.py
+++ b/solution.py
@@ -178,7 +178,6 @@
     small[51:52, :] = down(s_lnb)
     small[52:53, :] = sum_g * scale[...]
 
-    pay[:, :, :, C:] = jnp.zeros((2, 128, 8, 128), BF16)
     s_scale = jnp.zeros((C, 1), F32)
     for q in range(4):
         lanes = slice(q * 256, q * 256 + 256)
@@ -187,7 +186,7 @@
             part = slice(n * CH, (n + 1) * CH)
             total = total + jnp.dot(lnout_t[n], dpre[part, lanes], preferred_element_type=F32)
         small[54 + q : 55 + q, :] = total[C : C + 1]
-        pay[0, q * 32 : q * 32 + 32, :, 0:C] = total[0:C].reshape(32, 8, C).astype(BF16)
+        pay[0, q * 4 : q * 4 + 4] = total[0:C].reshape(4, 64, C)
     for q in range(4):
         lanes = slice(q * 256, q * 256 + 256)
         total = jnp.zeros((C, 256), F32)
@@ -195,9 +194,7 @@
             part = slice(n * CH, (n + 1) * CH)
             total = total + jnp.dot(grad_t[n], act[part, lanes], preferred_element_type=F32)
         s_scale = s_scale + jnp.sum(total * w_out_t[:, lanes].astype(F32), axis=1, keepdims=True)
-        pay[1, q * 32 : q * 32 + 32, :, 0:C] = (
-            (total.T * scale[...]).reshape(32, 8, C).astype(BF16)
-        )
+        pay[1, q * 4 : q * 4 + 4] = (total.T * scale[...]).reshape(4, 64, C)
     wide_scale = jnp.broadcast_to(s_scale, (C, 128)).T
     small[53:54, :] = wide_scale[0:1, :] + b_out[...] * sum_g
 
@@ -225,12 +222,13 @@
                     k = a * 7 + b
                     small[k : k + 1, lanes] = down(acc[p * 7 + b])
 
-    for k in range(8):
-        for lane in range(2):
-            part = small[k * 8 : k * 8 + 8, lane * 128 : lane * 128 + 128]
-            pay[0, k * 2 + lane, :, C:] = part.astype(BF16)
-    keep[...] = pay[core[0]]
-    send[...] = pay[1 - core[0]]
+    even = core[0] == 0
+    for k in range(16):
+        rest = small[k * 8 : k * 8 + 8, :] if k < 8 else jnp.zeros((8, C), F32)
+        none = jnp.zeros((8, C), F32)
+        for out, half, first in ((keep, core[0], even), (send, 1 - core[0], jnp.logical_not(even))):
+            extra = jnp.where(first, rest, none)
+            out[k] = jnp.concatenate([pay[half, k], extra], axis=0).astype(BF16)
 
 
 def transposed_kernel(
@@ -255,22 +253,16 @@
 ):
     even = core[0] == 0
     total = jnp.zeros((8, 256), F32)
-    for q in range(4):
-        for part in range(4):
-            at = slice(q * 32 + part * 8, q * 32 + part * 8 + 8)
-            a = mine[at, :, 0:C].astype(F32)
-            b = other[at, :, 0:C].astype(F32)
-            first = jnp.where(even, a, b)
-            second = jnp.where(even, b, a)
-            total = total + jnp.sum(first * first + second * second, axis=0)
-            win[part * 64 : part * 64 + 64, q * 256 : q * 256 + 256] = first.reshape(64, C)
-            row = q * 256 + part * 64
-            wout[row : row + 64, :] = second.reshape(64, C)
-    for k in range(8):
-        for lane in range(2):
-            a = mine[k * 2 + lane, :, C:].astype(F32)
-            b = other[k * 2 + lane, :, C:].astype(F32)
-            small[k * 8 : k * 8 + 8, lane * 128 : lane * 128 + 128] = jnp.where(even, a, b)
+    for k in range(16):
+        a, b = mine[k].astype(F32), other[k].astype(F32)
+        first, second = jnp.where(even, a, b), jnp.where(even, b, a)
+        squares = first[0:64] * first[0:64] + second[0:64] * second[0:64]
+        total = total + jnp.sum(squares.reshape(8, 8, C), axis=0)
+        q, part = k // 4, k % 4
+        win[part * 64 : part * 64 + 64, q * 256 : q * 256 + 256] = first[0:64]
+        wout[k * 64 : k * 64 + 64, :] = second[0:64]
+        if k < 8:
+            small[k * 8 : k * 8 + 8, :] = first[64:72]
     rest = small[...]
     total = total + jnp.sum((rest * rest).reshape(8, 8, C), axis=0)
     squares = jnp.sum(jnp.sum(total, axis=1, keepdims=True), axis=0, keepdims=True)
@@ -299,8 +291,8 @@
         main_kernel,
         out_shape=(
             jax.ShapeDtypeStruct((ROWS, COLS * C), BF16),
-            jax.ShapeDtypeStruct((128, 8, 384), BF16),
-            jax.ShapeDtypeStruct((128, 8, 384), BF16),
+            jax.ShapeDtypeStruct((16, 72, C), BF16),
+            jax.ShapeDtypeStruct((16, 72, C), BF16),
         ),
         in_specs=[pl.BlockSpec(memory_space=pltpu.SMEM)]
         + [pl.BlockSpec(memory_space=pltpu.VMEM)] * (len(operands) - 1),
@@ -319,7 +311,7 @@
             pltpu.VMEM((PIX, HID), BF16),
             pltpu.VMEM((COLS, 8, C), F32),
             pltpu.VMEM((64, C), F32),
-            pltpu.VMEM((2, 128, 8, 384), BF16),
+            pltpu.VMEM((2, 16, 64, C), F32),
         ),
         compiler_params=pltpu.CompilerParams(vmem_limit_bytes=40 * MIB),
         name="block_backward",
@@ -361,14 +353,14 @@
     return inner, outer
 
 
-def halo(x, core, after=None):
+def halo(x, core, beside_columns=None, beside_rows=None):
     inner, outer = pair_swaps(lax.axis_size("wa"))
     even = lax.rem(lax.axis_index("wa"), 2) == 0
     first, last = x[:, : 3 * C], x[:, -3 * C :]
     near = lax.ppermute(jnp.where(even, last, first), "wa", inner)
     far = lax.ppermute(jnp.where(even, first, last), "wa", outer)
-    if after is not None:
-        near, far, after = lax.optimization_barrier((near, far, after))
+    if beside_columns is not None:
+        near, far, _ = lax.optimization_barrier((near, far, beside_columns))
     left, right = jnp.where(even, far, near), jnp.where(even, near, far)
     inner, outer = pair_swaps(lax.axis_size("ha"))
     even = core[0] == 0
@@ -376,6 +368,8 @@
     lead = jnp.concatenate([left[:3], x[:3], right[:3]], axis=1)
     crossed = lax.ppermute(jnp.where(even, lead, last), "ha", outer)
     swapped = lax.ppermute(jnp.where(even, last, lead), "ha", inner)
+    if beside_rows is not None:
+        crossed, swapped, _ = lax.optimization_barrier((crossed, swapped, beside_rows))
     top, bottom = jnp.where(even, crossed, swapped), jnp.where(even, swapped, crossed)
     return left, right, jnp.concatenate([top, bottom], axis=0)
 
@@ -415,15 +409,14 @@
     )
     half = (keep.astype(F32) + lax.ppermute(send, "ha", swap).astype(F32)).astype(BF16)
     half, dconv = lax.optimization_barrier((half, dconv))
+    add_up = lambda v: jnp.sum(v.astype(F32), axis=0).astype(BF16)
+    repeat = lambda v, n: jnp.broadcast_to(v[None], (n,) + v.shape)
     terms = exchange(half, plane)
-    edges = halo(dconv, core, terms)
-    fold_first = lambda v, n: jnp.sum(v.reshape((n, -1) + v.shape[1:]).astype(F32), axis=0).astype(BF16)
-    sums = fold_first(terms, len(plane[0]))
-    every = jnp.broadcast_to(sums[None], (len(line[0]),) + sums.shape)
-    total = fold_first(exchange(every.reshape((-1,) + sums.shape[1:]), line), len(line[0]))
+    sums = exchange(repeat(add_up(terms), len(line[0])), line)
+    edges = halo(dconv, core, terms, sums)
+    total = add_up(sums)
     total, edges = lax.optimization_barrier((total, edges))
-    mine = jnp.broadcast_to(total[None], (len(plane[0]),) + total.shape).reshape(half.shape)
-    mine = exchange(mine, plane)
+    mine = exchange(repeat(total, len(plane[0])), plane)
     grad_features = run_transposed(dconv, *edges, grad_out, dw_weight[::-1])
     mine, grad_features = lax.optimization_barrier((mine, grad_features))
     other = lax.ppermute(mine, "ha", swap)

time: 118 us -> 108 us (0.915)
  waiting for transfers between devices: 34.8 us -> 21.7 us
  starting transfers between devices: 43.1 us -> 45.7 us
  Pallas kernels: 31.4 us -> 30.2 us
    all_to_all x3, waiting for transfers between devices: 24.8 us -> 6.86 us  [exchange(): lax.all_to_all(x, ('ha', 'wa'), 0, 0, axis_index_groups=groups, tiled=True)]
    ppermute x2, waiting for transfers between devices: 3.53 us -> 9.54 us  [halo(): crossed = lax.ppermute(jnp.where(even, lead, last), 'ha', outer)]
    ppermute x2, starting transfers between devices: 0.19 us -> 2.61 us  [halo(): swapped = lax.ppermute(jnp.where(even, last, lead), 'ha', inner)]
  transfers between devices with their start and end apart: 13 -> 13, of which waited for: 7 -> 7; matrix products, arithmetic and copies ran while one was open for 3% -> 2% of each run, Pallas kernels for 6% -> 6%
where the time goes in v7:
time: 108 us; the launch traced here: 107 us
  starting transfers between devices  45.7 us (42%)
  Pallas kernels  30.2 us (28%)
  waiting for transfers between devices  21.7 us (20%)
  other arithmetic  4.38 us (4%)
  local copies, waits for them, and re-layouts  3.89 us (4%)
    all_to_all x3, starting transfers between devices, exchange(): lax.all_to_all(x, ('ha', 'wa'), 0, 0, axis_index_groups=groups, tiled=True)  24 us
    pallas_call x1, Pallas kernels, run_main(): pl.pallas_call(main_kernel, out_shape=(jax.ShapeDtypeStruct((ROWS, COLS *...  21.9 us
    ppermute x2, waiting for transfers between devices, halo(): crossed = lax.ppermute(jnp.where(even, lead, last), 'ha', outer)  9.54 us
    ppermute x2, starting transfers between devices, halo(): crossed = lax.ppermute(jnp.where(even, lead, last), 'ha', outer)  7.93 us
    all_to_all x3, waiting for transfers between devices, exchange(): lax.all_to_all(x, ('ha', 'wa'), 0, 0, axis_index_groups=groups, tiled=True)  6.86 us
    pallas_call x1, Pallas kernels, run_transposed(): pl.pallas_call(transposed_kernel, out_shape=jax.ShapeDtypeStruct((ROWS, C...  6.56 us
    ppermute x2, starting transfers between devices, halo(): near = lax.ppermute(jnp.where(even, last, first), 'wa', inner)  6 us
    ppermute x1, starting transfers between devices, on_device(): other = lax.ppermute(mine, 'ha', swap)  3.67 us
  transfers between devices with their start and end apart: 13, of which 7 were waited for; matrix products, arithmetic and copies ran while one was open for 2% of the time, Pallas kernels for 6%

profile of v7, /device:TPU:1, one launch (start us, length us, event | category | flops | bytes accessed | tf_op | source)
XLA Modules:
  0.0 107.0 jit_solution(15461003808790535790)
XLA Ops:
  0.6 0.7 broadcast_select_fusion.14
  1.4 2.1 %collective-permute-start.1 = (bf16[8,768]{1,0:T(8,128)(2,1)S(1)}, bf16[8,768]{1,0:T(8,128)(2,1)S(1)}, u32[]{:S(2)}, u32[]{:S(2)}) collective-permute-start(bf16[8,768]{1,0:T(8,128)(2,1)S(1)} %get-tuple-element.72), channel_id=1, source_target_pairs={{0,1},{1,0},{2,3},{3,2},{4,5},{5,4},{6,7},{7,6},{8,9},{9,8},{10,11... | collective-permute-start | bytes 36872 | tf_op jit(solution)/shard_map/ppermute | solution.py:360
  3.5 0.8 collective-permute-start
  4.3 1.5 %fusion.1 = (bf16[3,32768]{1,0:T(4,128)(2,1)S(1)}, bf16[3,32768]{1,0:T(4,128)(2,1)S(1)}) fusion(bf16[8,32768]{1,0:T(8,128)(2,1)} %own.1), kind=kLoop, calls=%fused_computation.24 | loop fusion | bytes 786432 | tf_op jit(solution)/shard_map/slice | solution.py:368
  5.9 0.0 copy-start.1
  5.9 0.3 broadcast_select_fusion.7
  6.2 4.4 %collective-permute-start.2 = (bf16[3,34304]{1,0:T(4,128)(2,1)S(1)}, bf16[3,34304]{1,0:T(4,128)(2,1)S(1)}, u32[]{:S(2)}, u32[]{:S(2)}) collective-permute-start(bf16[3,34304]{1,0:T(4,128)(2,1)S(1)} %get-tuple-element.64), channel_id=1, source_target_pairs={{8,16},{16,8},{24,32},{32,24},{40,48},{48,40},{56,64},{64,56},{72,... | collective-permute-start | bytes 617480 | tf_op jit(solution)/shard_map/ppermute | solution.py:369
  10.6 0.1 collective-permute-start.3
  10.7 0.2 copy.24
  10.9 0.2 copy.23
  11.1 0.0 copy-start
  11.2 0.0 copy-start.2
  11.2 0.0 copy-start.3
  11.2 0.0 copy-start.4
  11.2 0.0 copy-start.5
  11.2 0.0 copy-start.6
  11.2 0.0 copy-start.8
  11.2 0.0 copy-start.9
  11.2 3.5 %collective-permute-done.2 = bf16[3,34304]{1,0:T(4,128)(2,1)S(1)} collective-permute-done((bf16[3,34304]{1,0:T(4,128)(2,1)S(1)}, bf16[3,34304]{1,0:T(4,128)(2,1)S(1)}, u32[]{:S(2)}, u32[]{:S(2)}) %collective-permute-start.2) | collective-permute-done | bytes 205856 | tf_op jit(solution)/shard_map/ppermute | solution.py:369
  14.8 1.2 %broadcast_select_fusion.5 = (bf16[3,34304]{1,0:T(4,128)(2,1)S(1)}, bf16[3,34304]{1,0:T(4,128)(2,1)S(1)}) fusion(bf16[3,34304]{1,0:T(4,128)(2,1)S(1)} %collective-permute-done.2, bf16[3,34304]{1,0:T(4,128)(2,1)} %collective-permute-done.3, pred[]{:T(512)S(6)} %eq.9), kind=kLoop, calls=%fused_computation.12 | loop fusion | flops 205824 | bytes 823297 | tf_op jit(solution)/shard_map/jit(_where)/select_n | solution.py:373
  16.0 0.3 pad_maximum_fusion.rows
  16.3 21.9 %block_backward.1 = (bf16[8,32768]{1,0:T(8,128)(2,1)S(1)}, bf16[16,72,256]{2,1,0:T(8,128)(2,1)S(1)}, bf16[16,72,256]{2,1,0:T(8,128)(2,1)S(1)}) custom-call(s32[1]{0:T(128)} %bitcast.core, bf16[8,32768]{1,0:T(8,128)(2,1)S(1)} %copy-done, bf16[8,768]{1,0:T(8,128)(2,1)S(1)} %get-tuple-element.77.left, bf16[8,768]{1,0:T(8,128)(2,1)S(1)} %get-tuple-element.76.right, ...), custom_call_target="tpu_custom_call" | custom-call | tf_op jit(solution)/shard_map/block_backward/pallas_call | solution.py:290
  38.2 0.1 collective-permute-start.4
  38.3 2.0 %collective-permute-done.4 = bf16[16,72,256]{2,1,0:T(8,128)(2,1)S(1)} collective-permute-done((bf16[16,72,256]{2,1,0:T(8,128)(2,1)S(1)}, bf16[16,72,256]{2,1,0:T(8,128)(2,1)S(1)}, u32[]{:S(2)}, u32[]{:S(2)}) %collective-permute-start.4) | collective-permute-done | bytes 589856 | tf_op jit(solution)/shard_map/ppermute | solution.py:410
  40.3 1.0 add_convert_fusion
  41.3 13.1 %all-to-all-start = ((bf16[16,72,256]{2,1,0:T(8,128)(2,1)}), bf16[16,72,256]{2,1,0:T(8,128)(2,1)S(1)}, u32[]{:S(2)}, u32[]{:S(2)}) async-start(bf16[16,72,256]{2,1,0:T(8,128)(2,1)} %add_convert_fusion), calls=%async_computation | async-start | bytes 1179648 | tf_op jit(solution)/shard_map/all_to_all | solution.py:404
  54.4 0.7 collective-permute-start.6
  55.1 3.9 %collective-permute-start.5 = (bf16[8,768]{1,0:T(8,128)(2,1)S(1)}, bf16[8,768]{1,0:T(8,128)(2,1)S(1)}, u32[]{:S(2)}, u32[]{:S(2)}) collective-permute-start(bf16[8,768]{1,0:T(8,128)(2,1)S(1)} %get-tuple-element.69), channel_id=1, source_target_pairs={{0,1},{1,0},{2,3},{3,2},{4,5},{5,4},{6,7},{7,6},{8,9},{9,8},{10,11... | collective-permute-start | bytes 36872 | tf_op jit(solution)/shard_map/ppermute | solution.py:360
  59.0 0.2 fusion
  59.1 1.7 %collective-permute-done.5 = bf16[8,768]{1,0:T(8,128)(2,1)S(1)} collective-permute-done((bf16[8,768]{1,0:T(8,128)(2,1)S(1)}, bf16[8,768]{1,0:T(8,128)(2,1)S(1)}, u32[]{:S(2)}, u32[]{:S(2)}) %collective-permute-start.5) | collective-permute-done | bytes 12320 | tf_op jit(solution)/shard_map/ppermute | solution.py:360
  60.8 4.2 %all-to-all-done = bf16[16,72,256]{2,1,0:T(8,128)(2,1)S(1)} async-done(((bf16[16,72,256]{2,1,0:T(8,128)(2,1)}), bf16[16,72,256]{2,1,0:T(8,128)(2,1)S(1)}, u32[]{:S(2)}, u32[]{:S(2)}) %all-to-all-start) | async-done | bytes 589856 | tf_op jit(solution)/shard_map/all_to_all | solution.py:404
  65.1 0.1 reduce_sum.24
  65.2 0.7 broadcast_in_dim.4
  65.9 7.3 %all-to-all-start.1 = ((bf16[8,72,256]{2,1,0:T(8,128)(2,1)}), bf16[8,72,256]{2,1,0:T(8,128)(2,1)S(1)}, u32[]{:S(2)}, u32[]{:S(2)}) async-start(bf16[8,72,256]{2,1,0:T(8,128)(2,1)} %broadcast_in_dim.4), calls=%async_computation.1 | async-start | bytes 589824 | tf_op jit(solution)/shard_map/all_to_all | solution.py:404
  73.2 0.3 broadcast_select_fusion.2
  73.5 2.5 %collective-permute-start.8 = (bf16[3,34304]{1,0:T(4,128)(2,1)S(1)}, bf16[3,34304]{1,0:T(4,128)(2,1)S(1)}, u32[]{:S(2)}, u32[]{:S(2)}) collective-permute-start(bf16[3,34304]{1,0:T(4,128)(2,1)S(1)} %get-tuple-element.60), channel_id=1, source_target_pairs={{0,8},{8,0},{16,24},{24,16},{32,40},{40,32},{48,56},{56,48},{64,72... | collective-permute-start | bytes 617480 | tf_op jit(solution)/shard_map/ppermute | solution.py:370
  76.0 3.5 %collective-permute-start.7 = (bf16[3,34304]{1,0:T(4,128)(2,1)S(1)}, bf16[3,34304]{1,0:T(4,128)(2,1)S(1)}, u32[]{:S(2)}, u32[]{:S(2)}) collective-permute-start(bf16[3,34304]{1,0:T(4,128)(2,1)S(1)} %get-tuple-element.61), channel_id=1, source_target_pairs={{8,16},{16,8},{24,32},{32,24},{40,48},{48,40},{56,64},{64,56},{72,... | collective-permute-start | bytes 617480 | tf_op jit(solution)/shard_map/ppermute | solution.py:369
  79.6 6.0 %collective-permute-done.7 = bf16[3,34304]{1,0:T(4,128)(2,1)S(1)} collective-permute-done((bf16[3,34304]{1,0:T(4,128)(2,1)S(1)}, bf16[3,34304]{1,0:T(4,128)(2,1)S(1)}, u32[]{:S(2)}, u32[]{:S(2)}) %collective-permute-start.7) | collective-permute-done | bytes 205856 | tf_op jit(solution)/shard_map/ppermute | solution.py:369
  85.6 0.2 broadcast_select_fusion.1
  85.8 0.3 pad_maximum_fusion.1.rows
  86.1 0.9 broadcast_in_dim.5
  87.0 3.6 %all-to-all-start.2 = ((bf16[16,72,256]{2,1,0:T(8,128)(2,1)}), bf16[16,72,256]{2,1,0:T(8,128)(2,1)S(1)}, u32[]{:S(2)}, u32[]{:S(2)}) async-start(bf16[16,72,256]{2,1,0:T(8,128)(2,1)} %broadcast_in_dim.5), calls=%async_computation.2 | async-start | bytes 1179648 | tf_op jit(solution)/shard_map/all_to_all | solution.py:404
  90.6 0.1 rev.3.dww
  90.7 6.6 %transposed_conv.1 = bf16[8,32768]{1,0:T(8,128)(2,1)} custom-call(bf16[8,32768]{1,0:T(8,128)(2,1)S(1)} %get-tuple-element.38.own, bf16[8,768]{1,0:T(8,128)(2,1)S(1)} %get-tuple-element.44.left, bf16[8,768]{1,0:T(8,128)(2,1)S(1)} %get-tuple-element.45.right, bf16[6,34304]{1,0:T(8,128)(2,1)S(1)} %pad_maximum_fusion.1.rows, bf16[8,32768]{1,0:T(8,128)(2,1)S(1)} %copy-done.2, ...), custom_call_target="tpu_custom_call" | custom-call | flops 200000000 | bytes 41943040 | tf_op jit(solution)/shard_map/transposed_conv/pallas_call | solution.py:322
  97.3 2.6 %all-to-all-done.2.mine = bf16[16,72,256]{2,1,0:T(8,128)(2,1)S(1)} async-done(((bf16[16,72,256]{2,1,0:T(8,128)(2,1)}), bf16[16,72,256]{2,1,0:T(8,128)(2,1)S(1)}, u32[]{:S(2)}, u32[]{:S(2)}) %all-to-all-start.2) | async-done | bytes 589856 | tf_op jit(solution)/shard_map/all_to_all | solution.py:404
  99.9 3.7 %collective-permute-start.9 = (bf16[16,72,256]{2,1,0:T(8,128)(2,1)S(1)}, bf16[16,72,256]{2,1,0:T(8,128)(2,1)S(1)}, u32[]{:S(2)}, u32[]{:S(2)}) collective-permute-start(bf16[16,72,256]{2,1,0:T(8,128)(2,1)S(1)} %all-to-all-done.2.mine), channel_id=1, source_target_pairs={{0,8},{8,0},{16,24},{24,16},{32,40},{40,32},{48,56},{56,48},{64,72... | collective-permute-start | bytes 1769480 | tf_op jit(solution)/shard_map/ppermute | solution.py:422
  103.5 1.6 %collective-permute-done.9.other = bf16[16,72,256]{2,1,0:T(8,128)(2,1)S(1)} collective-permute-done((bf16[16,72,256]{2,1,0:T(8,128)(2,1)S(1)}, bf16[16,72,256]{2,1,0:T(8,128)(2,1)S(1)}, u32[]{:S(2)}, u32[]{:S(2)}) %collective-permute-start.9) | collective-permute-done | bytes 589856 | tf_op jit(solution)/shard_map/ppermute | solution.py:422
  105.2 1.8 %clip.1 = (f32[49,256]{1,0:T(8,128)}, f32[1,256]{1,0:T(1,128)}, f32[1,256]{1,0:T(1,128)}, f32[1,256]{1,0:T(1,128)}, f32[256,1024]{1,0:T(8,128)}, /*index=5*/f32[...) custom-call(s32[1]{0:T(128)} %bitcast.core, bf16[16,72,256]{2,1,0:T(8,128)(2,1)S(1)} %all-to-all-done.2.mine, ...), custom_call_target="tpu_custom_call" | custom-call | tf_op jit(solution)/shard_map/clip/pallas_call | solution.py:335
  (26 shorter events, 0.1 us)
Async XLA Ops:
  1.4 4.5 %collective-permute-start.1 = (bf16[8,768]{1,0:T(8,128)(2,1)S(1)}, bf16[8,768]{1,0:T(8,128)(2,1)S(1)}, u32[]{:S(2)}, u32[]{:S(2)}) collective-permute-start(bf16[8,768]{1,0:T(8,128)(2,1)S(1)} %get-tuple-element.72), channel_id=1, source_target_pairs={{0,1},{1,0},{2,3},{3,2},{4,5},{5,4},{6,7},{7,6},{8,9},{9,8},{10,11... | collective-permute-start | bytes 36872 | tf_op jit(solution)/shard_map/ppermute | solution.py:360
  3.5 7.2 %copy-start.10 = (bf16[1024,256]{1,0:T(8,128)(2,1)S(1)}, bf16[1024,256]{1,0:T(8,128)(2,1)}, u32[]{:S(2)}) copy-start(bf16[1024,256]{1,0:T(8,128)(2,1)} %param.19) | copy-start | bytes 1572868
  3.5 2.3 %collective-permute-start = (bf16[8,768]{1,0:T(8,128)(2,1)S(1)}, bf16[8,768]{1,0:T(8,128)(2,1)S(1)}, u32[]{:S(2)}, u32[]{:S(2)}) collective-permute-start(bf16[8,768]{1,0:T(8,128)(2,1)S(1)} %get-tuple-element.73), channel_id=1, source_target_pairs={{1,2},{2,1},{3,4},{4,3},{5,6},{6,5},{9,10},{10,9},{11,12},{12,11},... | collective-permute-start | bytes 36872 | tf_op jit(solution)/shard_map/ppermute | solution.py:361
  5.9 5.0 %copy-start.1 = (bf16[256,1024]{1,0:T(8,128)(2,1)S(1)}, bf16[256,1024]{1,0:T(8,128)(2,1)}, u32[]{:S(2)}) copy-start(bf16[256,1024]{1,0:T(8,128)(2,1)} %w_in.1) | copy-start | bytes 1572868
  6.2 8.6 %collective-permute-start.2 = (bf16[3,34304]{1,0:T(4,128)(2,1)S(1)}, bf16[3,34304]{1,0:T(4,128)(2,1)S(1)}, u32[]{:S(2)}, u32[]{:S(2)}) collective-permute-start(bf16[3,34304]{1,0:T(4,128)(2,1)S(1)} %get-tuple-element.64), channel_id=1, source_target_pairs={{8,16},{16,8},{24,32},{32,24},{40,48},{48,40},{56,64},{64,56},{72,... | collective-permute-start | bytes 617480 | tf_op jit(solution)/shard_map/ppermute | solution.py:369
  10.6 4.2 %collective-permute-start.3 = (bf16[3,34304]{1,0:T(4,128)(2,1)S(1)}, bf16[3,34304]{1,0:T(4,128)(2,1)}, u32[]{:S(2)}, u32[]{:S(2)}) collective-permute-start(bf16[3,34304]{1,0:T(4,128)(2,1)S(1)} %get-tuple-element.65), channel_id=1, source_target_pairs={{0,8},{8,0},{16,24},{24,16},{32,40},{40,32},{48,56},{56,48},{64,72... | collective-permute-start | bytes 617480 | tf_op jit(solution)/shard_map/ppermute | solution.py:370
  11.1 5.1 %copy-start = (bf16[8,32768]{1,0:T(8,128)(2,1)S(1)}, bf16[8,32768]{1,0:T(8,128)(2,1)}, u32[]{:S(2)}) copy-start(bf16[8,32768]{1,0:T(8,128)(2,1)} %own.1) | copy-start | bytes 1572868
  11.2 5.1 %copy-start.2 = (bf16[8,32768]{1,0:T(8,128)(2,1)S(1)}, bf16[8,32768]{1,0:T(8,128)(2,1)}, u32[]{:S(2)}) copy-start(bf16[8,32768]{1,0:T(8,128)(2,1)} %grad.3) | copy-start | bytes 1572868
  11.2 5.1 %copy-start.3 = (f32[49,256]{1,0:T(8,128)S(1)}, f32[49,256]{1,0:T(8,128)}, u32[]{:S(2)}) copy-start(f32[49,256]{1,0:T(8,128)} %dww.1) | copy-start | bytes 150532
  11.2 5.1 %copy-start.4 = (f32[1024]{0:T(1024)S(1)}, f32[1024]{0:T(1024)}, u32[]{:S(2)}) copy-start(f32[1024]{0:T(1024)} %param.18) | copy-start | bytes 12292
  11.2 5.1 %copy-start.5 = (f32[256]{0:T(256)S(1)}, f32[256]{0:T(256)}, u32[]{:S(2)}) copy-start(f32[256]{0:T(256)} %param.14) | copy-start | bytes 3076
  11.2 5.1 %copy-start.6 = (f32[256]{0:T(256)S(1)}, f32[256]{0:T(256)}, u32[]{:S(2)}) copy-start(f32[256]{0:T(256)} %param.15) | copy-start | bytes 3076
  11.2 5.1 %copy-start.7 = (f32[256]{0:T(256)S(1)}, f32[256]{0:T(256)}, u32[]{:S(2)}) copy-start(f32[256]{0:T(256)} %param.16) | copy-start | bytes 3076
  11.2 5.1 %copy-start.8 = (f32[256]{0:T(256)S(1)}, f32[256]{0:T(256)}, u32[]{:S(2)}) copy-start(f32[256]{0:T(256)} %param.20) | copy-start | bytes 3076
  11.2 5.1 %copy-start.9 = (f32[256]{0:T(256)S(1)}, f32[256]{0:T(256)}, u32[]{:S(2)}) copy-start(f32[256]{0:T(256)} %param.21) | copy-start | bytes 3076
  38.2 2.1 %collective-permute-start.4 = (bf16[16,72,256]{2,1,0:T(8,128)(2,1)S(1)}, bf16[16,72,256]{2,1,0:T(8,128)(2,1)S(1)}, u32[]{:S(2)}, u32[]{:S(2)}) collective-permute-start(bf16[16,72,256]{2,1,0:T(8,128)(2,1)S(1)} %get-tuple-element.35), channel_id=1, source_target_pairs={{0,8},{8,0},{16,24},{24,16},{32,40},{40,32},{48,56},{56,48},{64,72... | collective-permute-start | bytes 1769480 | tf_op jit(solution)/shard_map/ppermute | solution.py:410
  41.3 23.8 %all-to-all-start = ((bf16[16,72,256]{2,1,0:T(8,128)(2,1)}), bf16[16,72,256]{2,1,0:T(8,128)(2,1)S(1)}, u32[]{:S(2)}, u32[]{:S(2)}) async-start(bf16[16,72,256]{2,1,0:T(8,128)(2,1)} %add_convert_fusion), calls=%async_computation | async-start | bytes 1179648 | tf_op jit(solution)/shard_map/all_to_all | solution.py:404
  54.4 4.7 %collective-permute-start.6 = (bf16[8,768]{1,0:T(8,128)(2,1)S(1)}, bf16[8,768]{1,0:T(8,128)(2,1)S(1)}, u32[]{:S(2)}, u32[]{:S(2)}) collective-permute-start(bf16[8,768]{1,0:T(8,128)(2,1)S(1)} %get-tuple-element.68), channel_id=1, source_target_pairs={{1,2},{2,1},{3,4},{4,3},{5,6},{6,5},{9,10},{10,9},{11,12},{12,11},... | collective-permute-start | bytes 36872 | tf_op jit(solution)/shard_map/ppermute | solution.py:361
  55.1 5.7 %collective-permute-start.5 = (bf16[8,768]{1,0:T(8,128)(2,1)S(1)}, bf16[8,768]{1,0:T(8,128)(2,1)S(1)}, u32[]{:S(2)}, u32[]{:S(2)}) collective-permute-start(bf16[8,768]{1,0:T(8,128)(2,1)S(1)} %get-tuple-element.69), channel_id=1, source_target_pairs={{0,1},{1,0},{2,3},{3,2},{4,5},{5,4},{6,7},{7,6},{8,9},{9,8},{10,11... | collective-permute-start | bytes 36872 | tf_op jit(solution)/shard_map/ppermute | solution.py:360
  65.9 19.7 %all-to-all-start.1 = ((bf16[8,72,256]{2,1,0:T(8,128)(2,1)}), bf16[8,72,256]{2,1,0:T(8,128)(2,1)S(1)}, u32[]{:S(2)}, u32[]{:S(2)}) async-start(bf16[8,72,256]{2,1,0:T(8,128)(2,1)} %broadcast_in_dim.4), calls=%async_computation.1 | async-start | bytes 589824 | tf_op jit(solution)/shard_map/all_to_all | solution.py:404
  73.5 6.1 %collective-permute-start.8 = (bf16[3,34304]{1,0:T(4,128)(2,1)S(1)}, bf16[3,34304]{1,0:T(4,128)(2,1)S(1)}, u32[]{:S(2)}, u32[]{:S(2)}) collective-permute-start(bf16[3,34304]{1,0:T(4,128)(2,1)S(1)} %get-tuple-element.60), channel_id=1, source_target_pairs={{0,8},{8,0},{16,24},{24,16},{32,40},{40,32},{48,56},{56,48},{64,72... | collective-permute-start | bytes 617480 | tf_op jit(solution)/shard_map/ppermute | solution.py:370
  76.0 9.6 %collective-permute-start.7 = (bf16[3,34304]{1,0:T(4,128)(2,1)S(1)}, bf16[3,34304]{1,0:T(4,128)(2,1)S(1)}, u32[]{:S(2)}, u32[]{:S(2)}) collective-permute-start(bf16[3,34304]{1,0:T(4,128)(2,1)S(1)} %get-tuple-element.61), channel_id=1, source_target_pairs={{8,16},{16,8},{24,32},{32,24},{40,48},{48,40},{56,64},{64,56},{72,... | collective-permute-start | bytes 617480 | tf_op jit(solution)/shard_map/ppermute | solution.py:369
  87.0 12.9 %all-to-all-start.2 = ((bf16[16,72,256]{2,1,0:T(8,128)(2,1)}), bf16[16,72,256]{2,1,0:T(8,128)(2,1)S(1)}, u32[]{:S(2)}, u32[]{:S(2)}) async-start(bf16[16,72,256]{2,1,0:T(8,128)(2,1)} %broadcast_in_dim.5), calls=%async_computation.2 | async-start | bytes 1179648 | tf_op jit(solution)/shard_map/all_to_all | solution.py:404
  99.9 5.3 %collective-permute-start.9 = (bf16[16,72,256]{2,1,0:T(8,128)(2,1)S(1)}, bf16[16,72,256]{2,1,0:T(8,128)(2,1)S(1)}, u32[]{:S(2)}, u32[]{:S(2)}) collective-permute-start(bf16[16,72,256]{2,1,0:T(8,128)(2,1)S(1)} %all-to-all-done.2.mine), channel_id=1, source_target_pairs={{0,8},{8,0},{16,24},{24,16},{32,40},{40,32},{48,56},{56,48},{64,72... | collective-permute-start | bytes 1769480 | tf_op jit(solution)/shard_map/ppermute | solution.py:422

commit v8 on v7

--- a/solution.py
+++ b/solution.py
@@ -17,12 +17,15 @@
 MIB = 1024 * 1024
 
 
-def shift_rows(own, left, right, rows, tall, shifted):
+def shift_rows(core, own, left, right, rows, tall, shifted):
+    even = core[0] == 0
+
     def place(j, mid, at):
         edge = rows[:, pl.ds(at, C)].astype(F32)
+        crossed, swapped = edge[0:3], edge[3:6]
         tall[j, 8:16, :] = mid.astype(F32)
-        tall[j, 5:8, :] = edge[0:3]
-        tall[j, 16:19, :] = edge[3:6]
+        tall[j, 5:8, :] = jnp.where(even, crossed, swapped)
+        tall[j, 16:19, :] = jnp.where(even, swapped, crossed)
         for a in range(7):
             shifted[a, j] = tall[j, 5 + a : 13 + a, :]
 
@@ -68,7 +71,7 @@
     tall, shifted, spread, conv, normed, inv, lnout, lnout_t, grad_flat, grad_t, pre, dact, act, dpre, dcw, small,
     pay,
 ):
-    shift_rows(own, left, right, rows, tall, shifted)
+    shift_rows(core, own, left, right, rows, tall, shifted)
     spread_weights(dww, spread)
 
     def normalize(n):
@@ -99,7 +102,7 @@
         return carry
 
     convolve(0)
-    lax.fori_loop(1, COLS // JB, forward, 0)
+    lax.fori_loop(1, COLS // JB, forward, 0, unroll=3)
     normalize(COLS // JB - 1)
 
     CH = 256
@@ -162,7 +165,7 @@
                 dconv_out[:, pl.ds(pl.multiple_of((j0 + o) * C, C), C)] = wide[o].astype(BF16)
             return s_gain, s_lnb, s_dwb
 
-        s_gain, s_lnb, s_dwb = lax.fori_loop(0, CH // 64, back, (s_gain, s_lnb, s_dwb), unroll=2)
+        s_gain, s_lnb, s_dwb = lax.fori_loop(0, CH // 64, back, (s_gain, s_lnb, s_dwb), unroll=4)
         return s_gain, s_lnb, s_g, s_dwb
 
     for n in range(PIX // CH):
@@ -200,7 +203,7 @@
 
     for lane in range(2):
         lanes = slice(lane * 128, lane * 128 + 128)
-        for group in ((0, 1), (2, 3), (4, 5), (6,)):
+        for group in ((0, 1, 2), (3, 4), (5, 6)):
 
             def taps(n, acc, group=group, lanes=lanes):
                 first = n * JB
@@ -232,9 +235,9 @@
 
 
 def transposed_kernel(
-    own, left, right, rows, grad, dww, out, tall, shifted, spread
+    core, own, left, right, rows, grad, dww, out, tall, shifted, spread
 ):
-    shift_rows(own, left, right, rows, tall, shifted)
+    shift_rows(core, own, left, right, rows, tall, shifted)
     spread_weights(dww, spread)
 
     def step(n, carry):
@@ -322,6 +325,8 @@
     return pl.pallas_call(
         transposed_kernel,
         out_shape=jax.ShapeDtypeStruct((ROWS, COLS * C), BF16),
+        in_specs=[pl.BlockSpec(memory_space=pltpu.SMEM)]
+        + [pl.BlockSpec(memory_space=pltpu.VMEM)] * (len(operands) - 1),
         scratch_shapes=CONV_SCRATCH,
         compiler_params=pltpu.CompilerParams(vmem_limit_bytes=20 * MIB),
         cost_estimate=pl.CostEstimate(flops=200_000_000, bytes_accessed=40 * MIB, transcendentals=0),
@@ -370,8 +375,7 @@
     swapped = lax.ppermute(jnp.where(even, last, lead), "ha", inner)
     if beside_rows is not None:
         crossed, swapped, _ = lax.optimization_barrier((crossed, swapped, beside_rows))
-    top, bottom = jnp.where(even, crossed, swapped), jnp.where(even, swapped, crossed)
-    return left, right, jnp.concatenate([top, bottom], axis=0)
+    return left, right, jnp.concatenate([crossed, swapped], axis=0)
 
 
 def plane_and_line():
@@ -417,7 +421,7 @@
     total = add_up(sums)
     total, edges = lax.optimization_barrier((total, edges))
     mine = exchange(repeat(total, len(plane[0])), plane)
-    grad_features = run_transposed(dconv, *edges, grad_out, dw_weight[::-1])
+    grad_features = run_transposed(core, dconv, *edges, grad_out, dw_weight[::-1])
     mine, grad_features = lax.optimization_barrier((mine, grad_features))
     other = lax.ppermute(mine, "ha", swap)
     o_dw, o_dwb, o_gain, o_lnb, o_win, o_bin, o_wout, o_bout, o_scale = run_finish(

time: 108 us -> 106 us (0.981)
  Pallas kernels: 30.2 us -> 28.9 us
    pallas_call x1, Pallas kernels: 21.9 us -> 20.3 us  [run_main(): pl.pallas_call(main_kernel, out_shape=(jax.ShapeDtypeStruct((ROWS, COLS *...]
    select_n x2 -> x0, other arithmetic: 1.41 us -> none  [halo(): jnp.where(even, crossed, swapped)]
where the time goes in v8:
time: 106 us; the launch traced here: 105 us
  starting transfers between devices  45.7 us (43%)
  Pallas kernels  28.9 us (27%)
  waiting for transfers between devices  21.6 us (20%)
  other arithmetic  4.03 us (4%)
  local copies, waits for them, and re-layouts  3.89 us (4%)
    all_to_all x3, starting transfers between devices, exchange(): lax.all_to_all(x, ('ha', 'wa'), 0, 0, axis_index_groups=groups, tiled=True)  24 us
    pallas_call x1, Pallas kernels, run_main(): pl.pallas_call(main_kernel, out_shape=(jax.ShapeDtypeStruct((ROWS, COLS *...  20.3 us
    ppermute x2, waiting for transfers between devices, halo(): crossed = lax.ppermute(jnp.where(even, lead, last), 'ha', outer)  9.64 us
    ppermute x2, starting transfers between devices, halo(): crossed = lax.ppermute(jnp.where(even, lead, last), 'ha', outer)  7.94 us
    pallas_call x1, Pallas kernels, run_transposed(): pl.pallas_call(transposed_kernel, out_shape=jax.ShapeDtypeStruct((ROWS, C...  6.75 us
    all_to_all x3, waiting for transfers between devices, exchange(): lax.all_to_all(x, ('ha', 'wa'), 0, 0, axis_index_groups=groups, tiled=True)  6.67 us
    ppermute x2, starting transfers between devices, halo(): near = lax.ppermute(jnp.where(even, last, first), 'wa', inner)  6 us
    ppermute x1, starting transfers between devices, on_device(): other = lax.ppermute(mine, 'ha', swap)  3.67 us
  transfers between devices with their start and end apart: 13, of which 7 were waited for; matrix products, arithmetic and copies ran while one was open for 2% of the time, Pallas kernels for 6%

profile of v8, /device:TPU:1, one launch (start us, length us, event | category | flops | bytes accessed | tf_op | source)
XLA Modules:
  0.0 105.2 jit_solution(4413866168984942245)
XLA Ops:
  0.6 0.7 broadcast_select_fusion.10
  1.4 2.1 %collective-permute-start.1 = (bf16[8,768]{1,0:T(8,128)(2,1)S(1)}, bf16[8,768]{1,0:T(8,128)(2,1)S(1)}, u32[]{:S(2)}, u32[]{:S(2)}) collective-permute-start(bf16[8,768]{1,0:T(8,128)(2,1)S(1)} %get-tuple-element.68), channel_id=1, source_target_pairs={{0,1},{1,0},{2,3},{3,2},{4,5},{5,4},{6,7},{7,6},{8,9},{9,8},{10,11... | collective-permute-start | bytes 36872 | tf_op jit(solution)/shard_map/ppermute | solution.py:365
  3.5 0.8 collective-permute-start
  4.3 1.5 %fusion.1 = (bf16[3,32768]{1,0:T(4,128)(2,1)S(1)}, bf16[3,32768]{1,0:T(4,128)(2,1)S(1)}) fusion(bf16[8,32768]{1,0:T(8,128)(2,1)} %own.1), kind=kLoop, calls=%fused_computation.20 | loop fusion | bytes 786432 | tf_op jit(solution)/shard_map/slice | solution.py:373
  5.8 0.0 collective-permute-done
  5.9 0.0 copy-start.2
  5.9 0.3 broadcast_select_fusion.3
  6.2 4.4 %collective-permute-start.2 = (bf16[3,34304]{1,0:T(4,128)(2,1)S(1)}, bf16[3,34304]{1,0:T(4,128)(2,1)}, u32[]{:S(2)}, u32[]{:S(2)}) collective-permute-start(bf16[3,34304]{1,0:T(4,128)(2,1)S(1)} %get-tuple-element.60), channel_id=1, source_target_pairs={{8,16},{16,8},{24,32},{32,24},{40,48},{48,40},{56,64},{64,56},{72,... | collective-permute-start | bytes 617480 | tf_op jit(solution)/shard_map/ppermute | solution.py:374
  10.6 0.1 collective-permute-start.3
  10.7 0.2 copy.24
  10.9 0.0 copy-start
  10.9 0.0 copy-start.1
  11.0 0.0 copy-start.3
  11.0 0.0 copy-start.4
  11.0 0.0 copy-start.5
  11.0 0.0 copy-start.6
  11.0 0.0 copy-start.7
  11.0 0.0 copy-start.8
  11.0 0.0 copy-start.9
  11.0 0.2 copy.23
  11.2 3.6 %collective-permute-done.2 = bf16[3,34304]{1,0:T(4,128)(2,1)} collective-permute-done((bf16[3,34304]{1,0:T(4,128)(2,1)S(1)}, bf16[3,34304]{1,0:T(4,128)(2,1)}, u32[]{:S(2)}, u32[]{:S(2)}) %collective-permute-start.2) | collective-permute-done | bytes 205856 | tf_op jit(solution)/shard_map/ppermute | solution.py:374
  14.9 1.3 %pad_maximum_fusion.rows = bf16[6,34304]{1,0:T(8,128)(2,1)S(1)} fusion(bf16[3,34304]{1,0:T(4,128)(2,1)} %collective-permute-done.3, bf16[3,34304]{1,0:T(4,128)(2,1)} %collective-permute-done.2), kind=kLoop, calls=%fused_computation.1 | loop fusion | flops 823296 | bytes 823296 | tf_op jit(solution)/shard_map/concatenate | solution.py:378
  16.3 20.3 %block_backward.1 = (bf16[8,32768]{1,0:T(8,128)(2,1)S(1)}, bf16[16,72,256]{2,1,0:T(8,128)(2,1)S(1)}, bf16[16,72,256]{2,1,0:T(8,128)(2,1)S(1)}) custom-call(s32[1]{0:T(128)} %bitcast.core, bf16[8,32768]{1,0:T(8,128)(2,1)S(1)} %copy-done, bf16[8,768]{1,0:T(8,128)(2,1)S(1)} %get-tuple-element.73.left, bf16[8,768]{1,0:T(8,128)(2,1)S(1)} %get-tuple-element.72.right, ...), custom_call_target="tpu_custom_call" | custom-call | tf_op jit(solution)/shard_map/block_backward/pallas_call | solution.py:293
  36.6 0.1 collective-permute-start.4
  36.7 2.0 %collective-permute-done.4 = bf16[16,72,256]{2,1,0:T(8,128)(2,1)S(1)} collective-permute-done((bf16[16,72,256]{2,1,0:T(8,128)(2,1)S(1)}, bf16[16,72,256]{2,1,0:T(8,128)(2,1)S(1)}, u32[]{:S(2)}, u32[]{:S(2)}) %collective-permute-start.4) | collective-permute-done | bytes 589856 | tf_op jit(solution)/shard_map/ppermute | solution.py:414
  38.7 1.0 add_convert_fusion
  39.7 13.1 %all-to-all-start = ((bf16[16,72,256]{2,1,0:T(8,128)(2,1)}), bf16[16,72,256]{2,1,0:T(8,128)(2,1)S(1)}, u32[]{:S(2)}, u32[]{:S(2)}) async-start(bf16[16,72,256]{2,1,0:T(8,128)(2,1)} %add_convert_fusion), calls=%async_computation | async-start | bytes 1179648 | tf_op jit(solution)/shard_map/all_to_all | solution.py:408
  52.8 0.7 collective-permute-start.6
  53.5 3.9 %collective-permute-start.5 = (bf16[8,768]{1,0:T(8,128)(2,1)S(1)}, bf16[8,768]{1,0:T(8,128)(2,1)S(1)}, u32[]{:S(2)}, u32[]{:S(2)}) collective-permute-start(bf16[8,768]{1,0:T(8,128)(2,1)S(1)} %get-tuple-element.65), channel_id=1, source_target_pairs={{0,1},{1,0},{2,3},{3,2},{4,5},{5,4},{6,7},{7,6},{8,9},{9,8},{10,11... | collective-permute-start | bytes 36872 | tf_op jit(solution)/shard_map/ppermute | solution.py:365
  57.4 0.2 fusion
  57.6 1.7 %collective-permute-done.5 = bf16[8,768]{1,0:T(8,128)(2,1)S(1)} collective-permute-done((bf16[8,768]{1,0:T(8,128)(2,1)S(1)}, bf16[8,768]{1,0:T(8,128)(2,1)S(1)}, u32[]{:S(2)}, u32[]{:S(2)}) %collective-permute-start.5) | collective-permute-done | bytes 12320 | tf_op jit(solution)/shard_map/ppermute | solution.py:365
  59.2 4.2 %all-to-all-done = bf16[16,72,256]{2,1,0:T(8,128)(2,1)S(1)} async-done(((bf16[16,72,256]{2,1,0:T(8,128)(2,1)}), bf16[16,72,256]{2,1,0:T(8,128)(2,1)S(1)}, u32[]{:S(2)}, u32[]{:S(2)}) %all-to-all-start) | async-done | bytes 589856 | tf_op jit(solution)/shard_map/all_to_all | solution.py:408
  63.5 0.1 reduce_sum.24
  63.6 0.7 broadcast_in_dim.4
  64.3 7.3 %all-to-all-start.1 = ((bf16[8,72,256]{2,1,0:T(8,128)(2,1)}), bf16[8,72,256]{2,1,0:T(8,128)(2,1)S(1)}, u32[]{:S(2)}, u32[]{:S(2)}) async-start(bf16[8,72,256]{2,1,0:T(8,128)(2,1)} %broadcast_in_dim.4), calls=%async_computation.1 | async-start | bytes 589824 | tf_op jit(solution)/shard_map/all_to_all | solution.py:408
  71.6 0.3 broadcast_select_fusion
  71.9 2.5 %collective-permute-start.8 = (bf16[3,34304]{1,0:T(4,128)(2,1)S(1)}, bf16[3,34304]{1,0:T(4,128)(2,1)S(1)}, u32[]{:S(2)}, u32[]{:S(2)}) collective-permute-start(bf16[3,34304]{1,0:T(4,128)(2,1)S(1)} %get-tuple-element.58), channel_id=1, source_target_pairs={{0,8},{8,0},{16,24},{24,16},{32,40},{40,32},{48,56},{56,48},{64,72... | collective-permute-start | bytes 617480 | tf_op jit(solution)/shard_map/ppermute | solution.py:375
  74.4 3.5 %collective-permute-start.7 = (bf16[3,34304]{1,0:T(4,128)(2,1)S(1)}, bf16[3,34304]{1,0:T(4,128)(2,1)S(1)}, u32[]{:S(2)}, u32[]{:S(2)}) collective-permute-start(bf16[3,34304]{1,0:T(4,128)(2,1)S(1)} %get-tuple-element.59), channel_id=1, source_target_pairs={{8,16},{16,8},{24,32},{32,24},{40,48},{48,40},{56,64},{64,56},{72,... | collective-permute-start | bytes 617480 | tf_op jit(solution)/shard_map/ppermute | solution.py:374
  78.0 6.0 %collective-permute-done.7 = bf16[3,34304]{1,0:T(4,128)(2,1)S(1)} collective-permute-done((bf16[3,34304]{1,0:T(4,128)(2,1)S(1)}, bf16[3,34304]{1,0:T(4,128)(2,1)S(1)}, u32[]{:S(2)}, u32[]{:S(2)}) %collective-permute-start.7) | collective-permute-done | bytes 205856 | tf_op jit(solution)/shard_map/ppermute | solution.py:374
  84.0 0.3 pad_maximum_fusion.1.rows
  84.3 0.9 broadcast_in_dim.5
  85.2 3.6 %all-to-all-start.2 = ((bf16[16,72,256]{2,1,0:T(8,128)(2,1)}), bf16[16,72,256]{2,1,0:T(8,128)(2,1)S(1)}, u32[]{:S(2)}, u32[]{:S(2)}) async-start(bf16[16,72,256]{2,1,0:T(8,128)(2,1)} %broadcast_in_dim.5), calls=%async_computation.2 | async-start | bytes 1179648 | tf_op jit(solution)/shard_map/all_to_all | solution.py:408
  88.8 0.1 rev.3.dww
  88.9 6.8 %transposed_conv.1 = bf16[8,32768]{1,0:T(8,128)(2,1)} custom-call(s32[1]{0:T(128)} %bitcast.core, bf16[8,32768]{1,0:T(8,128)(2,1)S(1)} %get-tuple-element.38.own, bf16[8,768]{1,0:T(8,128)(2,1)S(1)} %get-tuple-element.44.left, bf16[8,768]{1,0:T(8,128)(2,1)S(1)} %get-tuple-element.45.right, bf16[6,34304]{1,0:T(8,128)(2,1)S(1)} %pad_maximum_fusion.1.rows, ...), custom_call_target="tpu_custom_call" | custom-call | flops 200000000 | bytes 41943040 | tf_op jit(solution)/shard_map/transposed_conv/pallas_call | solution.py:325
  95.6 2.4 %all-to-all-done.2.mine = bf16[16,72,256]{2,1,0:T(8,128)(2,1)S(1)} async-done(((bf16[16,72,256]{2,1,0:T(8,128)(2,1)}), bf16[16,72,256]{2,1,0:T(8,128)(2,1)S(1)}, u32[]{:S(2)}, u32[]{:S(2)}) %all-to-all-start.2) | async-done | bytes 589856 | tf_op jit(solution)/shard_map/all_to_all | solution.py:408
  98.1 3.7 %collective-permute-start.9 = (bf16[16,72,256]{2,1,0:T(8,128)(2,1)S(1)}, bf16[16,72,256]{2,1,0:T(8,128)(2,1)S(1)}, u32[]{:S(2)}, u32[]{:S(2)}) collective-permute-start(bf16[16,72,256]{2,1,0:T(8,128)(2,1)S(1)} %all-to-all-done.2.mine), channel_id=1, source_target_pairs={{0,8},{8,0},{16,24},{24,16},{32,40},{40,32},{48,56},{56,48},{64,72... | collective-permute-start | bytes 1769480 | tf_op jit(solution)/shard_map/ppermute | solution.py:426
  101.7 1.6 %collective-permute-done.9.other = bf16[16,72,256]{2,1,0:T(8,128)(2,1)S(1)} collective-permute-done((bf16[16,72,256]{2,1,0:T(8,128)(2,1)S(1)}, bf16[16,72,256]{2,1,0:T(8,128)(2,1)S(1)}, u32[]{:S(2)}, u32[]{:S(2)}) %collective-permute-start.9) | collective-permute-done | bytes 589856 | tf_op jit(solution)/shard_map/ppermute | solution.py:426
  103.4 1.8 %clip.1 = (f32[49,256]{1,0:T(8,128)}, f32[1,256]{1,0:T(1,128)}, f32[1,256]{1,0:T(1,128)}, f32[1,256]{1,0:T(1,128)}, f32[256,1024]{1,0:T(8,128)}, /*index=5*/f32[...) custom-call(s32[1]{0:T(128)} %bitcast.core, bf16[16,72,256]{2,1,0:T(8,128)(2,1)S(1)} %all-to-all-done.2.mine, ...), custom_call_target="tpu_custom_call" | custom-call | tf_op jit(solution)/shard_map/clip/pallas_call | solution.py:340
  (24 shorter events, 0.1 us)
Async XLA Ops:
  1.4 4.5 %collective-permute-start.1 = (bf16[8,768]{1,0:T(8,128)(2,1)S(1)}, bf16[8,768]{1,0:T(8,128)(2,1)S(1)}, u32[]{:S(2)}, u32[]{:S(2)}) collective-permute-start(bf16[8,768]{1,0:T(8,128)(2,1)S(1)} %get-tuple-element.68), channel_id=1, source_target_pairs={{0,1},{1,0},{2,3},{3,2},{4,5},{5,4},{6,7},{7,6},{8,9},{9,8},{10,11... | collective-permute-start | bytes 36872 | tf_op jit(solution)/shard_map/ppermute | solution.py:365
  3.5 7.2 %copy-start.10 = (bf16[1024,256]{1,0:T(8,128)(2,1)S(1)}, bf16[1024,256]{1,0:T(8,128)(2,1)}, u32[]{:S(2)}) copy-start(bf16[1024,256]{1,0:T(8,128)(2,1)} %param.19) | copy-start | bytes 1572868
  3.5 2.3 %collective-permute-start = (bf16[8,768]{1,0:T(8,128)(2,1)S(1)}, bf16[8,768]{1,0:T(8,128)(2,1)S(1)}, u32[]{:S(2)}, u32[]{:S(2)}) collective-permute-start(bf16[8,768]{1,0:T(8,128)(2,1)S(1)} %get-tuple-element.69), channel_id=1, source_target_pairs={{1,2},{2,1},{3,4},{4,3},{5,6},{6,5},{9,10},{10,9},{11,12},{12,11},... | collective-permute-start | bytes 36872 | tf_op jit(solution)/shard_map/ppermute | solution.py:366
  5.9 5.0 %copy-start.2 = (bf16[256,1024]{1,0:T(8,128)(2,1)S(1)}, bf16[256,1024]{1,0:T(8,128)(2,1)}, u32[]{:S(2)}) copy-start(bf16[256,1024]{1,0:T(8,128)(2,1)} %w_in.1) | copy-start | bytes 1572868
  6.2 8.7 %collective-permute-start.2 = (bf16[3,34304]{1,0:T(4,128)(2,1)S(1)}, bf16[3,34304]{1,0:T(4,128)(2,1)}, u32[]{:S(2)}, u32[]{:S(2)}) collective-permute-start(bf16[3,34304]{1,0:T(4,128)(2,1)S(1)} %get-tuple-element.60), channel_id=1, source_target_pairs={{8,16},{16,8},{24,32},{32,24},{40,48},{48,40},{56,64},{64,56},{72,... | collective-permute-start | bytes 617480 | tf_op jit(solution)/shard_map/ppermute | solution.py:374
  10.6 4.3 %collective-permute-start.3 = (bf16[3,34304]{1,0:T(4,128)(2,1)S(1)}, bf16[3,34304]{1,0:T(4,128)(2,1)}, u32[]{:S(2)}, u32[]{:S(2)}) collective-permute-start(bf16[3,34304]{1,0:T(4,128)(2,1)S(1)} %get-tuple-element.61), channel_id=1, source_target_pairs={{0,8},{8,0},{16,24},{24,16},{32,40},{40,32},{48,56},{56,48},{64,72... | collective-permute-start | bytes 617480 | tf_op jit(solution)/shard_map/ppermute | solution.py:375
  10.9 5.3 %copy-start = (bf16[8,32768]{1,0:T(8,128)(2,1)S(1)}, bf16[8,32768]{1,0:T(8,128)(2,1)}, u32[]{:S(2)}) copy-start(bf16[8,32768]{1,0:T(8,128)(2,1)} %own.1) | copy-start | bytes 1572868
  10.9 5.3 %copy-start.1 = (bf16[8,32768]{1,0:T(8,128)(2,1)S(1)}, bf16[8,32768]{1,0:T(8,128)(2,1)}, u32[]{:S(2)}) copy-start(bf16[8,32768]{1,0:T(8,128)(2,1)} %grad.3) | copy-start | bytes 1572868
  11.0 5.3 %copy-start.3 = (f32[49,256]{1,0:T(8,128)S(1)}, f32[49,256]{1,0:T(8,128)}, u32[]{:S(2)}) copy-start(f32[49,256]{1,0:T(8,128)} %dww.1) | copy-start | bytes 150532
  11.0 5.3 %copy-start.4 = (f32[1024]{0:T(1024)S(1)}, f32[1024]{0:T(1024)}, u32[]{:S(2)}) copy-start(f32[1024]{0:T(1024)} %param.18) | copy-start | bytes 12292
  11.0 5.3 %copy-start.5 = (f32[256]{0:T(256)S(1)}, f32[256]{0:T(256)}, u32[]{:S(2)}) copy-start(f32[256]{0:T(256)} %param.14) | copy-start | bytes 3076
  11.0 5.2 %copy-start.6 = (f32[256]{0:T(256)S(1)}, f32[256]{0:T(256)}, u32[]{:S(2)}) copy-start(f32[256]{0:T(256)} %param.15) | copy-start | bytes 3076
  11.0 5.2 %copy-start.7 = (f32[256]{0:T(256)S(1)}, f32[256]{0:T(256)}, u32[]{:S(2)}) copy-start(f32[256]{0:T(256)} %param.16) | copy-start | bytes 3076
  11.0 5.2 %copy-start.8 = (f32[256]{0:T(256)S(1)}, f32[256]{0:T(256)}, u32[]{:S(2)}) copy-start(f32[256]{0:T(256)} %param.20) | copy-start | bytes 3076
  11.0 5.2 %copy-start.9 = (f32[256]{0:T(256)S(1)}, f32[256]{0:T(256)}, u32[]{:S(2)}) copy-start(f32[256]{0:T(256)} %param.21) | copy-start | bytes 3076
  36.6 2.1 %collective-permute-start.4 = (bf16[16,72,256]{2,1,0:T(8,128)(2,1)S(1)}, bf16[16,72,256]{2,1,0:T(8,128)(2,1)S(1)}, u32[]{:S(2)}, u32[]{:S(2)}) collective-permute-start(bf16[16,72,256]{2,1,0:T(8,128)(2,1)S(1)} %get-tuple-element.35), channel_id=1, source_target_pairs={{0,8},{8,0},{16,24},{24,16},{32,40},{40,32},{48,56},{56,48},{64,72... | collective-permute-start | bytes 1769480 | tf_op jit(solution)/shard_map/ppermute | solution.py:414
  39.7 23.8 %all-to-all-start = ((bf16[16,72,256]{2,1,0:T(8,128)(2,1)}), bf16[16,72,256]{2,1,0:T(8,128)(2,1)S(1)}, u32[]{:S(2)}, u32[]{:S(2)}) async-start(bf16[16,72,256]{2,1,0:T(8,128)(2,1)} %add_convert_fusion), calls=%async_computation | async-start | bytes 1179648 | tf_op jit(solution)/shard_map/all_to_all | solution.py:408
  52.8 4.7 %collective-permute-start.6 = (bf16[8,768]{1,0:T(8,128)(2,1)S(1)}, bf16[8,768]{1,0:T(8,128)(2,1)S(1)}, u32[]{:S(2)}, u32[]{:S(2)}) collective-permute-start(bf16[8,768]{1,0:T(8,128)(2,1)S(1)} %get-tuple-element.64), channel_id=1, source_target_pairs={{1,2},{2,1},{3,4},{4,3},{5,6},{6,5},{9,10},{10,9},{11,12},{12,11},... | collective-permute-start | bytes 36872 | tf_op jit(solution)/shard_map/ppermute | solution.py:366
  53.5 5.7 %collective-permute-start.5 = (bf16[8,768]{1,0:T(8,128)(2,1)S(1)}, bf16[8,768]{1,0:T(8,128)(2,1)S(1)}, u32[]{:S(2)}, u32[]{:S(2)}) collective-permute-start(bf16[8,768]{1,0:T(8,128)(2,1)S(1)} %get-tuple-element.65), channel_id=1, source_target_pairs={{0,1},{1,0},{2,3},{3,2},{4,5},{5,4},{6,7},{7,6},{8,9},{9,8},{10,11... | collective-permute-start | bytes 36872 | tf_op jit(solution)/shard_map/ppermute | solution.py:365
  64.3 19.7 %all-to-all-start.1 = ((bf16[8,72,256]{2,1,0:T(8,128)(2,1)}), bf16[8,72,256]{2,1,0:T(8,128)(2,1)S(1)}, u32[]{:S(2)}, u32[]{:S(2)}) async-start(bf16[8,72,256]{2,1,0:T(8,128)(2,1)} %broadcast_in_dim.4), calls=%async_computation.1 | async-start | bytes 589824 | tf_op jit(solution)/shard_map/all_to_all | solution.py:408
  71.9 6.1 %collective-permute-start.8 = (bf16[3,34304]{1,0:T(4,128)(2,1)S(1)}, bf16[3,34304]{1,0:T(4,128)(2,1)S(1)}, u32[]{:S(2)}, u32[]{:S(2)}) collective-permute-start(bf16[3,34304]{1,0:T(4,128)(2,1)S(1)} %get-tuple-element.58), channel_id=1, source_target_pairs={{0,8},{8,0},{16,24},{24,16},{32,40},{40,32},{48,56},{56,48},{64,72... | collective-permute-start | bytes 617480 | tf_op jit(solution)/shard_map/ppermute | solution.py:375
  74.4 9.6 %collective-permute-start.7 = (bf16[3,34304]{1,0:T(4,128)(2,1)S(1)}, bf16[3,34304]{1,0:T(4,128)(2,1)S(1)}, u32[]{:S(2)}, u32[]{:S(2)}) collective-permute-start(bf16[3,34304]{1,0:T(4,128)(2,1)S(1)} %get-tuple-element.59), channel_id=1, source_target_pairs={{8,16},{16,8},{24,32},{32,24},{40,48},{48,40},{56,64},{64,56},{72,... | collective-permute-start | bytes 617480 | tf_op jit(solution)/shard_map/ppermute | solution.py:374
  85.2 12.9 %all-to-all-start.2 = ((bf16[16,72,256]{2,1,0:T(8,128)(2,1)}), bf16[16,72,256]{2,1,0:T(8,128)(2,1)S(1)}, u32[]{:S(2)}, u32[]{:S(2)}) async-start(bf16[16,72,256]{2,1,0:T(8,128)(2,1)} %broadcast_in_dim.5), calls=%async_computation.2 | async-start | bytes 1179648 | tf_op jit(solution)/shard_map/all_to_all | solution.py:408
  98.1 5.3 %collective-permute-start.9 = (bf16[16,72,256]{2,1,0:T(8,128)(2,1)S(1)}, bf16[16,72,256]{2,1,0:T(8,128)(2,1)S(1)}, u32[]{:S(2)}, u32[]{:S(2)}) collective-permute-start(bf16[16,72,256]{2,1,0:T(8,128)(2,1)S(1)} %all-to-all-done.2.mine), channel_id=1, source_target_pairs={{0,8},{8,0},{16,24},{24,16},{32,40},{40,32},{48,56},{56,48},{64,72... | collective-permute-start | bytes 1769480 | tf_op jit(solution)/shard_map/ppermute | solution.py:426

commit v9 on v8

--- a/solution.py
+++ b/solution.py
@@ -66,9 +66,9 @@
 
 
 def main_kernel(
-    core, own, left, right, rows, grad, dww, dwb, gain, lnb, w_in, w_in_t, b_in, w_out_t, b_out, scale,
+    core, own, left, right, rows, grad_t, dact, sum_g8, dww, dwb, gain, lnb, w_in, w_in_t, b_in, w_out_t, b_out, scale,
     dconv_out, keep, send,
-    tall, shifted, spread, conv, normed, inv, lnout, lnout_t, grad_flat, grad_t, pre, dact, act, dpre, dcw, small,
+    tall, shifted, spread, conv, normed, inv, lnout, lnout_t, pre, back_in, act, dpre, dcw, small,
     pay,
 ):
     shift_rows(core, own, left, right, rows, tall, shifted)
@@ -91,10 +91,6 @@
             lanes = slice(lane * 128, lane * 128 + 128)
             for o, acc in enumerate(conv_block(shifted, spread, first, lane)):
                 conv[first + o, :, lanes] = acc
-        for o in range(JB):
-            at = pl.multiple_of((first + o) * C, C)
-            g = grad[:, pl.ds(at, C)].astype(F32)
-            grad_flat[pl.ds(pl.multiple_of((first + o) * 8, 8), 8), :] = g
 
     def forward(n, carry):
         normalize(n - 1)
@@ -108,16 +104,11 @@
     CH = 256
 
     def mlp(n, carry):
-        s_gain, s_lnb, s_g, s_dwb = carry
+        s_gain, s_lnb, s_dwb = carry
         rows = pl.ds(pl.multiple_of(n * CH, CH), CH)
         ln = lnout[rows, :]
         lnout_t[n, 0:C, :] = ln.astype(F32).T.astype(BF16)
-        g = grad_flat[rows, :]
-        grad_t[n] = g.T.astype(BF16)
         pre[...] = jnp.dot(ln, w_in[...], preferred_element_type=F32) + b_in[...]
-        dbr = (g * scale[...]).astype(BF16)
-        dact[...] = jnp.dot(dbr, w_out_t[...], preferred_element_type=F32)
-        s_g = s_g + fold(g)
 
         def gelu(m, c):
             sub = pl.ds(pl.multiple_of(m * 16, 16), 16)
@@ -137,17 +128,17 @@
                 cdf = jnp.where(v < 0.0, tail, 1.0 - tail)
                 act[out, lanes] = (v * cdf).astype(BF16)
                 slope = cdf + v * (e * (1.0 / math.sqrt(2.0 * math.pi)))
-                dpre[out, lanes] = (dact[sub, lanes] * slope).astype(BF16)
+                dpre[out, lanes] = (dact[out, lanes] * slope).astype(BF16)
             return c
 
         lax.fori_loop(0, CH // 16, gelu, 0, unroll=4)
-        dact[:, 0:C] = jnp.dot(dpre[rows, :], w_in_t[...], preferred_element_type=F32)
+        back_in[...] = jnp.dot(dpre[rows, :], w_in_t[...], preferred_element_type=F32)
 
         def back(m, c):
             s_gain, s_lnb, s_dwb = c
             sub = pl.ds(pl.multiple_of(m * 64, 64), 64)
             out = pl.ds(pl.multiple_of(n * CH + m * 64, 64), 64)
-            dln = dact[sub, 0:C]
+            dln = back_in[sub, :]
             norm = normed[out, :]
             prod = dln * norm
             s_gain = s_gain + fold(prod)
@@ -166,16 +157,16 @@
             return s_gain, s_lnb, s_dwb
 
         s_gain, s_lnb, s_dwb = lax.fori_loop(0, CH // 64, back, (s_gain, s_lnb, s_dwb), unroll=4)
-        return s_gain, s_lnb, s_g, s_dwb
+        return s_gain, s_lnb, s_dwb
 
     for n in range(PIX // CH):
         lnout_t[n, C:, :] = jnp.ones((16, CH), BF16)
     zero = jnp.zeros((8, C), F32)
-    s_gain, s_lnb, s_g, s_dwb = lax.fori_loop(0, PIX // CH, mlp, (zero, zero, zero, zero))
+    s_gain, s_lnb, s_dwb = lax.fori_loop(0, PIX // CH, mlp, (zero, zero, zero))
 
     small[...] = jnp.zeros_like(small)
     down = lambda v: jnp.sum(v, axis=0, keepdims=True)
-    sum_g = down(s_g)
+    sum_g = down(sum_g8[...])
     small[49:50, :] = down(s_dwb)
     small[50:51, :] = down(s_gain)
     small[51:52, :] = down(s_lnb)
@@ -232,6 +223,21 @@
         for out, half, first in ((keep, core[0], even), (send, 1 - core[0], jnp.logical_not(even))):
             extra = jnp.where(first, rest, none)
             out[k] = jnp.concatenate([pay[half, k], extra], axis=0).astype(BF16)
+
+
+def prepare_kernel(grad, w_out_t, scale, grad_t, dact, sum_g8, flat):
+    def step(n, total):
+        for o in range(32):
+            at = pl.multiple_of((n * 32 + o) * C, C)
+            flat[o * 8 : o * 8 + 8, :] = grad[:, pl.ds(at, C)].astype(F32)
+        g = flat[...]
+        grad_t[n] = g.T.astype(BF16)
+        branch = (g * scale[...]).astype(BF16)
+        rows = pl.ds(pl.multiple_of(n * 256, 256), 256)
+        dact[rows, :] = jnp.dot(branch, w_out_t[...], preferred_element_type=F32)
+        return total + fold(g)
+
+    sum_g8[...] = lax.fori_loop(0, PIX // 256, step, jnp.zeros((8, C), F32))
 
 
 def transposed_kernel(
@@ -306,18 +312,31 @@
             pltpu.VMEM((PIX, 1), F32),
             pltpu.VMEM((PIX, C), BF16),
             pltpu.VMEM((4, C + 16, 256), BF16),
-            pltpu.VMEM((PIX, C), F32),
-            pltpu.VMEM((4, C, 256), BF16),
             pltpu.VMEM((256, HID), F32),
-            pltpu.VMEM((256, HID), F32),
+            pltpu.VMEM((256, C), F32),
             pltpu.VMEM((PIX, HID), BF16),
             pltpu.VMEM((PIX, HID), BF16),
             pltpu.VMEM((COLS, 8, C), F32),
             pltpu.VMEM((64, C), F32),
             pltpu.VMEM((2, 16, 64, C), F32),
         ),
-        compiler_params=pltpu.CompilerParams(vmem_limit_bytes=40 * MIB),
+        compiler_params=pltpu.CompilerParams(vmem_limit_bytes=30 * MIB),
         name="block_backward",
+    )(*operands)
+
+
+def run_prepare(*operands):
+    return pl.pallas_call(
+        prepare_kernel,
+        out_shape=(
+            jax.ShapeDtypeStruct((PIX // 256, C, 256), BF16),
+            jax.ShapeDtypeStruct((PIX, HID), F32),
+            jax.ShapeDtypeStruct((8, C), F32),
+        ),
+        scratch_shapes=(pltpu.VMEM((256, C), F32),),
+        compiler_params=pltpu.CompilerParams(vmem_limit_bytes=10 * MIB),
+        cost_estimate=pl.CostEstimate(flops=600_000_000, bytes_accessed=8 * MIB, transcendentals=0),
+        name="prepare",
     )(*operands)
 
 
@@ -407,8 +426,9 @@
     def exchange(x, groups):
         return lax.all_to_all(x, ("ha", "wa"), 0, 0, axis_index_groups=groups, tiled=True)
 
+    prepared = run_prepare(grad_out, w_out.T, row(scale))
     dconv, keep, send = run_main(
-        core, features, *halo(features, core), grad_out, dw_weight, row(dw_bias), row(ln_gain),
+        core, features, *halo(features, core), *prepared, dw_weight, row(dw_bias), row(ln_gain),
         row(ln_bias), w_in, w_in.T, row(b_in), w_out.T, row(b_out), row(scale),
     )
     half = (keep.astype(F32) + lax.ppermute(send, "ha", swap).astype(F32)).astype(BF16)

time: 106 us -> 108 us (1.019)
  waiting for transfers between devices: 21.6 us -> 24.9 us
    all_to_all x3, waiting for transfers between devices: 6.67 us -> 12.9 us  [exchange(): lax.all_to_all(x, ('ha', 'wa'), 0, 0, axis_index_groups=groups, tiled=True)]
    ppermute x2, starting transfers between devices: 7.94 us -> 10.9 us  [halo(): crossed = lax.ppermute(jnp.where(even, lead, last), 'ha', outer)]
    ppermute x2, starting transfers between devices: 2.61 us -> 0.19 us  [halo(): swapped = lax.ppermute(jnp.where(even, last, lead), 'ha', inner)]
    all_to_all x3, starting transfers between devices: 24 us -> 22.2 us  [exchange(): lax.all_to_all(x, ('ha', 'wa'), 0, 0, axis_index_groups=groups, tiled=True)]
    ppermute x2, waiting for transfers between devices: 1.67 us -> 0.01 us  [halo(): near = lax.ppermute(jnp.where(even, last, first), 'wa', inner)]
    ppermute x2, waiting for transfers between devices: 9.64 us -> 8.33 us  [halo(): crossed = lax.ppermute(jnp.where(even, lead, last), 'ha', outer)]
    pallas_call x0 -> x1, Pallas kernels: none -> 1.26 us  [run_prepare(): pl.pallas_call(prepare_kernel, out_shape=(jax.ShapeDtypeStruct((PIX // 25...]
  transfers between devices with their start and end apart: 13 -> 13, of which waited for: 7 -> 6; matrix products, arithmetic and copies ran while one was open for 2% -> 2% of each run, Pallas kernels for 6% -> 7%
where the time goes in v9:
time: 108 us; the launch traced here: 107 us
  starting transfers between devices  44.8 us (41%)
  Pallas kernels  29.5 us (27%)
  waiting for transfers between devices  24.9 us (23%)
  local copies, waits for them, and re-layouts  3.84 us (4%)
  other arithmetic  2.99 us (3%)
    all_to_all x3, starting transfers between devices, exchange(): lax.all_to_all(x, ('ha', 'wa'), 0, 0, axis_index_groups=groups, tiled=True)  22.2 us
    pallas_call x1, Pallas kernels, run_main(): pl.pallas_call(main_kernel, out_shape=(jax.ShapeDtypeStruct((ROWS, COLS *...  19.7 us
    all_to_all x3, waiting for transfers between devices, exchange(): lax.all_to_all(x, ('ha', 'wa'), 0, 0, axis_index_groups=groups, tiled=True)  12.9 us
    ppermute x2, starting transfers between devices, halo(): crossed = lax.ppermute(jnp.where(even, lead, last), 'ha', outer)  10.9 us
    ppermute x2, waiting for transfers between devices, halo(): crossed = lax.ppermute(jnp.where(even, lead, last), 'ha', outer)  8.33 us
    pallas_call x1, Pallas kernels, run_transposed(): pl.pallas_call(transposed_kernel, out_shape=jax.ShapeDtypeStruct((ROWS, C...  6.73 us
    ppermute x2, starting transfers between devices, halo(): near = lax.ppermute(jnp.where(even, last, first), 'wa', inner)  6.49 us
    ppermute x1, starting transfers between devices, on_device(): other = lax.ppermute(mine, 'ha', swap)  3.67 us
  transfers between devices with their start and end apart: 13, of which 6 were waited for; matrix products, arithmetic and copies ran while one was open for 2% of the time, Pallas kernels for 7%

profile of v9, /device:TPU:1, one launch (start us, length us, event | category | flops | bytes accessed | tf_op | source)
XLA Modules:
  0.0 107.0 jit_solution(9189969536036912725)
XLA Ops:
  0.6 0.7 broadcast_select_fusion.10
  1.4 0.7 collective-permute-start
  2.0 0.0 copy-start.10
  2.1 4.8 %collective-permute-start.1 = (bf16[8,768]{1,0:T(8,128)(2,1)S(1)}, bf16[8,768]{1,0:T(8,128)(2,1)S(1)}, u32[]{:S(2)}, u32[]{:S(2)}) collective-permute-start(bf16[8,768]{1,0:T(8,128)(2,1)S(1)} %get-tuple-element.74), channel_id=1, source_target_pairs={{0,1},{1,0},{2,3},{3,2},{4,5},{5,4},{6,7},{7,6},{8,9},{9,8},{10,11... | collective-permute-start | bytes 36872 | tf_op jit(solution)/shard_map/ppermute | solution.py:384
  6.8 1.5 %fusion.1 = (bf16[3,32768]{1,0:T(4,128)(2,1)S(1)}, bf16[3,32768]{1,0:T(4,128)(2,1)S(1)}) fusion(bf16[8,32768]{1,0:T(8,128)(2,1)} %own.1), kind=kLoop, calls=%fused_computation.20 | loop fusion | bytes 786432 | tf_op jit(solution)/shard_map/slice | solution.py:392
  8.3 0.0 copy-start.1
  8.4 0.3 broadcast_select_fusion.3
  8.7 0.0 copy-start.2
  8.7 0.0 copy-start.5
  8.7 5.0 %collective-permute-start.2 = (bf16[3,34304]{1,0:T(4,128)(2,1)S(1)}, bf16[3,34304]{1,0:T(4,128)(2,1)S(1)}, u32[]{:S(2)}, u32[]{:S(2)}) collective-permute-start(bf16[3,34304]{1,0:T(4,128)(2,1)S(1)} %get-tuple-element.66), channel_id=1, source_target_pairs={{8,16},{16,8},{24,32},{32,24},{40,48},{48,40},{56,64},{64,56},{72,... | collective-permute-start | bytes 617480 | tf_op jit(solution)/shard_map/ppermute | solution.py:393
  13.6 0.1 collective-permute-start.3
  13.8 0.2 copy.23
  14.0 0.2 copy.24
  14.2 1.3 %prepare.1 = (bf16[4,256,256]{2,1,0:T(8,128)(2,1)S(1)}, f32[1024,1024]{1,0:T(8,128)S(1)}, f32[8,256]{1,0:T(8,128)S(1)}) custom-call(bf16[8,32768]{1,0:T(8,128)(2,1)S(1)} %copy-done.2, bf16[256,1024]{1,0:T(8,128)(2,1)S(1)} %bitcast.15, f32[1,256]{1,0:T(1,128)S(1)} %bitcast.19), custom_call_target="tpu_custom_call" | custom-call | flops 600000000 | bytes 8388608 | tf_op jit(solution)/shard_map/prepare/pallas_call | solution.py:329
  15.5 0.0 copy-start
  15.5 0.0 copy-start.3
  15.5 0.0 copy-start.4
  15.5 0.0 copy-start.6
  15.5 0.0 copy-start.7
  15.5 0.0 copy-start.8
  15.5 0.0 copy-start.9
  15.5 2.3 %collective-permute-done.2 = bf16[3,34304]{1,0:T(4,128)(2,1)S(1)} collective-permute-done((bf16[3,34304]{1,0:T(4,128)(2,1)S(1)}, bf16[3,34304]{1,0:T(4,128)(2,1)S(1)}, u32[]{:S(2)}, u32[]{:S(2)}) %collective-permute-start.2) | collective-permute-done | bytes 205856 | tf_op jit(solution)/shard_map/ppermute | solution.py:393
  17.8 0.3 pad_maximum_fusion.rows
  18.2 19.7 %block_backward.1 = (bf16[8,32768]{1,0:T(8,128)(2,1)S(1)}, bf16[16,72,256]{2,1,0:T(8,128)(2,1)S(1)}, bf16[16,72,256]{2,1,0:T(8,128)(2,1)S(1)}) custom-call(s32[1]{0:T(128)} %bitcast.core, bf16[8,32768]{1,0:T(8,128)(2,1)S(1)} %copy-done, bf16[8,768]{1,0:T(8,128)(2,1)S(1)} %get-tuple-element.79.left, bf16[8,768]{1,0:T(8,128)(2,1)S(1)} %get-tuple-element.78.right, ...), custom_call_target="tpu_custom_call" | custom-call | tf_op jit(solution)/shard_map/block_backward/pallas_call | solution.py:299
  37.8 0.1 collective-permute-start.4
  37.9 2.0 %collective-permute-done.4 = bf16[16,72,256]{2,1,0:T(8,128)(2,1)S(1)} collective-permute-done((bf16[16,72,256]{2,1,0:T(8,128)(2,1)S(1)}, bf16[16,72,256]{2,1,0:T(8,128)(2,1)S(1)}, u32[]{:S(2)}, u32[]{:S(2)}) %collective-permute-start.4) | collective-permute-done | bytes 589856 | tf_op jit(solution)/shard_map/ppermute | solution.py:434
  39.9 1.0 add_convert_fusion
  40.9 1.7 %collective-permute-start.5 = (bf16[8,768]{1,0:T(8,128)(2,1)S(1)}, bf16[8,768]{1,0:T(8,128)(2,1)S(1)}, u32[]{:S(2)}, u32[]{:S(2)}) collective-permute-start(bf16[8,768]{1,0:T(8,128)(2,1)S(1)} %get-tuple-element.71), channel_id=1, source_target_pairs={{0,1},{1,0},{2,3},{3,2},{4,5},{5,4},{6,7},{7,6},{8,9},{9,8},{10,11... | collective-permute-start | bytes 36872 | tf_op jit(solution)/shard_map/ppermute | solution.py:384
  42.6 0.7 collective-permute-start.6
  43.3 11.6 %all-to-all-start = ((bf16[16,72,256]{2,1,0:T(8,128)(2,1)}), bf16[16,72,256]{2,1,0:T(8,128)(2,1)S(1)}, u32[]{:S(2)}, u32[]{:S(2)}) async-start(bf16[16,72,256]{2,1,0:T(8,128)(2,1)} %add_convert_fusion), calls=%async_computation | async-start | bytes 1179648 | tf_op jit(solution)/shard_map/all_to_all | solution.py:427
  54.9 0.2 fusion
  55.1 10.5 %all-to-all-done = bf16[16,72,256]{2,1,0:T(8,128)(2,1)S(1)} async-done(((bf16[16,72,256]{2,1,0:T(8,128)(2,1)}), bf16[16,72,256]{2,1,0:T(8,128)(2,1)S(1)}, u32[]{:S(2)}, u32[]{:S(2)}) %all-to-all-start) | async-done | bytes 589856 | tf_op jit(solution)/shard_map/all_to_all | solution.py:427
  65.6 0.1 reduce_sum.24
  65.7 0.7 broadcast_in_dim.4
  66.4 7.0 %all-to-all-start.1 = ((bf16[8,72,256]{2,1,0:T(8,128)(2,1)}), bf16[8,72,256]{2,1,0:T(8,128)(2,1)S(1)}, u32[]{:S(2)}, u32[]{:S(2)}) async-start(bf16[8,72,256]{2,1,0:T(8,128)(2,1)} %broadcast_in_dim.4), calls=%async_computation.1 | async-start | bytes 589824 | tf_op jit(solution)/shard_map/all_to_all | solution.py:427
  73.4 0.3 broadcast_select_fusion
  73.7 5.9 %collective-permute-start.7 = (bf16[3,34304]{1,0:T(4,128)(2,1)S(1)}, bf16[3,34304]{1,0:T(4,128)(2,1)S(1)}, u32[]{:S(2)}, u32[]{:S(2)}) collective-permute-start(bf16[3,34304]{1,0:T(4,128)(2,1)S(1)} %get-tuple-element.65), channel_id=1, source_target_pairs={{8,16},{16,8},{24,32},{32,24},{40,48},{48,40},{56,64},{64,56},{72,... | collective-permute-start | bytes 617480 | tf_op jit(solution)/shard_map/ppermute | solution.py:393
  79.7 0.1 collective-permute-start.8
  79.8 6.1 %collective-permute-done.7 = bf16[3,34304]{1,0:T(4,128)(2,1)S(1)} collective-permute-done((bf16[3,34304]{1,0:T(4,128)(2,1)S(1)}, bf16[3,34304]{1,0:T(4,128)(2,1)S(1)}, u32[]{:S(2)}, u32[]{:S(2)}) %collective-permute-start.7) | collective-permute-done | bytes 205856 | tf_op jit(solution)/shard_map/ppermute | solution.py:393
  85.8 0.3 pad_maximum_fusion.1.rows
  86.2 0.9 broadcast_in_dim.5
  87.0 3.6 %all-to-all-start.2 = ((bf16[16,72,256]{2,1,0:T(8,128)(2,1)}), bf16[16,72,256]{2,1,0:T(8,128)(2,1)S(1)}, u32[]{:S(2)}, u32[]{:S(2)}) async-start(bf16[16,72,256]{2,1,0:T(8,128)(2,1)} %broadcast_in_dim.5), calls=%async_computation.2 | async-start | bytes 1179648 | tf_op jit(solution)/shard_map/all_to_all | solution.py:427
  90.6 0.1 rev.3.dww
  90.7 6.7 %transposed_conv.1 = bf16[8,32768]{1,0:T(8,128)(2,1)} custom-call(s32[1]{0:T(128)} %bitcast.core, bf16[8,32768]{1,0:T(8,128)(2,1)S(1)} %get-tuple-element.44.own, bf16[8,768]{1,0:T(8,128)(2,1)S(1)} %get-tuple-element.50.left, bf16[8,768]{1,0:T(8,128)(2,1)S(1)} %get-tuple-element.51.right, bf16[6,34304]{1,0:T(8,128)(2,1)S(1)} %pad_maximum_fusion.1.rows, ...), custom_call_target="tpu_custom_call" | custom-call | flops 200000000 | bytes 41943040 | tf_op jit(solution)/shard_map/transposed_conv/pallas_call | solution.py:344
  97.4 2.5 %all-to-all-done.2.mine = bf16[16,72,256]{2,1,0:T(8,128)(2,1)S(1)} async-done(((bf16[16,72,256]{2,1,0:T(8,128)(2,1)}), bf16[16,72,256]{2,1,0:T(8,128)(2,1)S(1)}, u32[]{:S(2)}, u32[]{:S(2)}) %all-to-all-start.2) | async-done | bytes 589856 | tf_op jit(solution)/shard_map/all_to_all | solution.py:427
  99.9 3.7 %collective-permute-start.9 = (bf16[16,72,256]{2,1,0:T(8,128)(2,1)S(1)}, bf16[16,72,256]{2,1,0:T(8,128)(2,1)S(1)}, u32[]{:S(2)}, u32[]{:S(2)}) collective-permute-start(bf16[16,72,256]{2,1,0:T(8,128)(2,1)S(1)} %all-to-all-done.2.mine), channel_id=1, source_target_pairs={{0,8},{8,0},{16,24},{24,16},{32,40},{40,32},{48,56},{56,48},{64,72... | collective-permute-start | bytes 1769480 | tf_op jit(solution)/shard_map/ppermute | solution.py:446
  103.6 1.6 %collective-permute-done.9.other = bf16[16,72,256]{2,1,0:T(8,128)(2,1)S(1)} collective-permute-done((bf16[16,72,256]{2,1,0:T(8,128)(2,1)S(1)}, bf16[16,72,256]{2,1,0:T(8,128)(2,1)S(1)}, u32[]{:S(2)}, u32[]{:S(2)}) %collective-permute-start.9) | collective-permute-done | bytes 589856 | tf_op jit(solution)/shard_map/ppermute | solution.py:446
  105.2 1.8 %clip.1 = (f32[49,256]{1,0:T(8,128)}, f32[1,256]{1,0:T(1,128)}, f32[1,256]{1,0:T(1,128)}, f32[1,256]{1,0:T(1,128)}, f32[256,1024]{1,0:T(8,128)}, /*index=5*/f32[...) custom-call(s32[1]{0:T(128)} %bitcast.core, bf16[16,72,256]{2,1,0:T(8,128)(2,1)S(1)} %all-to-all-done.2.mine, ...), custom_call_target="tpu_custom_call" | custom-call | tf_op jit(solution)/shard_map/clip/pallas_call | solution.py:359
  (25 shorter events, 0.1 us)
Async XLA Ops:
  1.4 6.9 %collective-permute-start = (bf16[8,768]{1,0:T(8,128)(2,1)S(1)}, bf16[8,768]{1,0:T(8,128)(2,1)S(1)}, u32[]{:S(2)}, u32[]{:S(2)}) collective-permute-start(bf16[8,768]{1,0:T(8,128)(2,1)S(1)} %get-tuple-element.75), channel_id=1, source_target_pairs={{1,2},{2,1},{3,4},{4,3},{5,6},{6,5},{9,10},{10,9},{11,12},{12,11},... | collective-permute-start | bytes 36872 | tf_op jit(solution)/shard_map/ppermute | solution.py:385
  2.0 11.7 %copy-start.10 = (bf16[1024,256]{1,0:T(8,128)(2,1)S(1)}, bf16[1024,256]{1,0:T(8,128)(2,1)}, u32[]{:S(2)}) copy-start(bf16[1024,256]{1,0:T(8,128)(2,1)} %param.19) | copy-start | bytes 1572868
  2.1 6.2 %collective-permute-start.1 = (bf16[8,768]{1,0:T(8,128)(2,1)S(1)}, bf16[8,768]{1,0:T(8,128)(2,1)S(1)}, u32[]{:S(2)}, u32[]{:S(2)}) collective-permute-start(bf16[8,768]{1,0:T(8,128)(2,1)S(1)} %get-tuple-element.74), channel_id=1, source_target_pairs={{0,1},{1,0},{2,3},{3,2},{4,5},{5,4},{6,7},{7,6},{8,9},{9,8},{10,11... | collective-permute-start | bytes 36872 | tf_op jit(solution)/shard_map/ppermute | solution.py:384
  8.3 5.6 %copy-start.1 = (bf16[256,1024]{1,0:T(8,128)(2,1)S(1)}, bf16[256,1024]{1,0:T(8,128)(2,1)}, u32[]{:S(2)}) copy-start(bf16[256,1024]{1,0:T(8,128)(2,1)} %w_in.1) | copy-start | bytes 1572868
  8.7 5.5 %copy-start.2 = (bf16[8,32768]{1,0:T(8,128)(2,1)S(1)}, bf16[8,32768]{1,0:T(8,128)(2,1)}, u32[]{:S(2)}) copy-start(bf16[8,32768]{1,0:T(8,128)(2,1)} %grad.3) | copy-start | bytes 1572868
  8.7 5.5 %copy-start.5 = (f32[256]{0:T(256)S(1)}, f32[256]{0:T(256)}, u32[]{:S(2)}) copy-start(f32[256]{0:T(256)} %param.21) | copy-start | bytes 3076
  8.7 9.1 %collective-permute-start.2 = (bf16[3,34304]{1,0:T(4,128)(2,1)S(1)}, bf16[3,34304]{1,0:T(4,128)(2,1)S(1)}, u32[]{:S(2)}, u32[]{:S(2)}) collective-permute-start(bf16[3,34304]{1,0:T(4,128)(2,1)S(1)} %get-tuple-element.66), channel_id=1, source_target_pairs={{8,16},{16,8},{24,32},{32,24},{40,48},{48,40},{56,64},{64,56},{72,... | collective-permute-start | bytes 617480 | tf_op jit(solution)/shard_map/ppermute | solution.py:393
  13.6 4.2 %collective-permute-start.3 = (bf16[3,34304]{1,0:T(4,128)(2,1)S(1)}, bf16[3,34304]{1,0:T(4,128)(2,1)S(1)}, u32[]{:S(2)}, u32[]{:S(2)}) collective-permute-start(bf16[3,34304]{1,0:T(4,128)(2,1)S(1)} %get-tuple-element.67), channel_id=1, source_target_pairs={{0,8},{8,0},{16,24},{24,16},{32,40},{40,32},{48,56},{56,48},{64,72... | collective-permute-start | bytes 617480 | tf_op jit(solution)/shard_map/ppermute | solution.py:394
  15.5 2.6 %copy-start = (bf16[8,32768]{1,0:T(8,128)(2,1)S(1)}, bf16[8,32768]{1,0:T(8,128)(2,1)}, u32[]{:S(2)}) copy-start(bf16[8,32768]{1,0:T(8,128)(2,1)} %own.1) | copy-start | bytes 1572868
  15.5 2.6 %copy-start.3 = (f32[49,256]{1,0:T(8,128)S(1)}, f32[49,256]{1,0:T(8,128)}, u32[]{:S(2)}) copy-start(f32[49,256]{1,0:T(8,128)} %dww.1) | copy-start | bytes 150532
  15.5 2.6 %copy-start.4 = (f32[1024]{0:T(1024)S(1)}, f32[1024]{0:T(1024)}, u32[]{:S(2)}) copy-start(f32[1024]{0:T(1024)} %param.18) | copy-start | bytes 12292
  15.5 2.6 %copy-start.6 = (f32[256]{0:T(256)S(1)}, f32[256]{0:T(256)}, u32[]{:S(2)}) copy-start(f32[256]{0:T(256)} %param.14) | copy-start | bytes 3076
  15.5 2.6 %copy-start.7 = (f32[256]{0:T(256)S(1)}, f32[256]{0:T(256)}, u32[]{:S(2)}) copy-start(f32[256]{0:T(256)} %param.15) | copy-start | bytes 3076
  15.5 2.6 %copy-start.8 = (f32[256]{0:T(256)S(1)}, f32[256]{0:T(256)}, u32[]{:S(2)}) copy-start(f32[256]{0:T(256)} %param.16) | copy-start | bytes 3076
  15.5 2.6 %copy-start.9 = (f32[256]{0:T(256)S(1)}, f32[256]{0:T(256)}, u32[]{:S(2)}) copy-start(f32[256]{0:T(256)} %param.20) | copy-start | bytes 3076
  37.8 2.1 %collective-permute-start.4 = (bf16[16,72,256]{2,1,0:T(8,128)(2,1)S(1)}, bf16[16,72,256]{2,1,0:T(8,128)(2,1)S(1)}, u32[]{:S(2)}, u32[]{:S(2)}) collective-permute-start(bf16[16,72,256]{2,1,0:T(8,128)(2,1)S(1)} %get-tuple-element.41), channel_id=1, source_target_pairs={{0,8},{8,0},{16,24},{24,16},{32,40},{40,32},{48,56},{56,48},{64,72... | collective-permute-start | bytes 1769480 | tf_op jit(solution)/shard_map/ppermute | solution.py:434
  40.9 14.2 %collective-permute-start.5 = (bf16[8,768]{1,0:T(8,128)(2,1)S(1)}, bf16[8,768]{1,0:T(8,128)(2,1)S(1)}, u32[]{:S(2)}, u32[]{:S(2)}) collective-permute-start(bf16[8,768]{1,0:T(8,128)(2,1)S(1)} %get-tuple-element.71), channel_id=1, source_target_pairs={{0,1},{1,0},{2,3},{3,2},{4,5},{5,4},{6,7},{7,6},{8,9},{9,8},{10,11... | collective-permute-start | bytes 36872 | tf_op jit(solution)/shard_map/ppermute | solution.py:384
  42.6 12.4 %collective-permute-start.6 = (bf16[8,768]{1,0:T(8,128)(2,1)S(1)}, bf16[8,768]{1,0:T(8,128)(2,1)S(1)}, u32[]{:S(2)}, u32[]{:S(2)}) collective-permute-start(bf16[8,768]{1,0:T(8,128)(2,1)S(1)} %get-tuple-element.70), channel_id=1, source_target_pairs={{1,2},{2,1},{3,4},{4,3},{5,6},{6,5},{9,10},{10,9},{11,12},{12,11},... | collective-permute-start | bytes 36872 | tf_op jit(solution)/shard_map/ppermute | solution.py:385
  43.3 22.3 %all-to-all-start = ((bf16[16,72,256]{2,1,0:T(8,128)(2,1)}), bf16[16,72,256]{2,1,0:T(8,128)(2,1)S(1)}, u32[]{:S(2)}, u32[]{:S(2)}) async-start(bf16[16,72,256]{2,1,0:T(8,128)(2,1)} %add_convert_fusion), calls=%async_computation | async-start | bytes 1179648 | tf_op jit(solution)/shard_map/all_to_all | solution.py:427
  66.4 19.4 %all-to-all-start.1 = ((bf16[8,72,256]{2,1,0:T(8,128)(2,1)}), bf16[8,72,256]{2,1,0:T(8,128)(2,1)S(1)}, u32[]{:S(2)}, u32[]{:S(2)}) async-start(bf16[8,72,256]{2,1,0:T(8,128)(2,1)} %broadcast_in_dim.4), calls=%async_computation.1 | async-start | bytes 589824 | tf_op jit(solution)/shard_map/all_to_all | solution.py:427
  73.7 12.1 %collective-permute-start.7 = (bf16[3,34304]{1,0:T(4,128)(2,1)S(1)}, bf16[3,34304]{1,0:T(4,128)(2,1)S(1)}, u32[]{:S(2)}, u32[]{:S(2)}) collective-permute-start(bf16[3,34304]{1,0:T(4,128)(2,1)S(1)} %get-tuple-element.65), channel_id=1, source_target_pairs={{8,16},{16,8},{24,32},{32,24},{40,48},{48,40},{56,64},{64,56},{72,... | collective-permute-start | bytes 617480 | tf_op jit(solution)/shard_map/ppermute | solution.py:393
  79.7 6.2 %collective-permute-start.8 = (bf16[3,34304]{1,0:T(4,128)(2,1)S(1)}, bf16[3,34304]{1,0:T(4,128)(2,1)S(1)}, u32[]{:S(2)}, u32[]{:S(2)}) collective-permute-start(bf16[3,34304]{1,0:T(4,128)(2,1)S(1)} %get-tuple-element.64), channel_id=1, source_target_pairs={{0,8},{8,0},{16,24},{24,16},{32,40},{40,32},{48,56},{56,48},{64,72... | collective-permute-start | bytes 617480 | tf_op jit(solution)/shard_map/ppermute | solution.py:394
  87.0 12.9 %all-to-all-start.2 = ((bf16[16,72,256]{2,1,0:T(8,128)(2,1)}), bf16[16,72,256]{2,1,0:T(8,128)(2,1)S(1)}, u32[]{:S(2)}, u32[]{:S(2)}) async-start(bf16[16,72,256]{2,1,0:T(8,128)(2,1)} %broadcast_in_dim.5), calls=%async_computation.2 | async-start | bytes 1179648 | tf_op jit(solution)/shard_map/all_to_all | solution.py:427
  99.9 5.3 %collective-permute-start.9 = (bf16[16,72,256]{2,1,0:T(8,128)(2,1)S(1)}, bf16[16,72,256]{2,1,0:T(8,128)(2,1)S(1)}, u32[]{:S(2)}, u32[]{:S(2)}) collective-permute-start(bf16[16,72,256]{2,1,0:T(8,128)(2,1)S(1)} %all-to-all-done.2.mine), channel_id=1, source_target_pairs={{0,8},{8,0},{16,24},{24,16},{32,40},{40,32},{48,56},{56,48},{64,72... | collective-permute-start | bytes 1769480 | tf_op jit(solution)/shard_map/ppermute | solution.py:446

commit v10 on v8

--- a/solution.py
+++ b/solution.py
@@ -102,7 +102,7 @@
         return carry
 
     convolve(0)
-    lax.fori_loop(1, COLS // JB, forward, 0, unroll=3)
+    lax.fori_loop(1, COLS // JB, forward, 0, unroll=5)
     normalize(COLS // JB - 1)
 
     CH = 256
@@ -140,7 +140,7 @@
                 dpre[out, lanes] = (dact[sub, lanes] * slope).astype(BF16)
             return c
 
-        lax.fori_loop(0, CH // 16, gelu, 0, unroll=4)
+        lax.fori_loop(0, CH // 16, gelu, 0, unroll=16)
         dact[:, 0:C] = jnp.dot(dpre[rows, :], w_in_t[...], preferred_element_type=F32)
 
         def back(m, c):
@@ -171,7 +171,7 @@
     for n in range(PIX // CH):
         lnout_t[n, C:, :] = jnp.ones((16, CH), BF16)
     zero = jnp.zeros((8, C), F32)
-    s_gain, s_lnb, s_g, s_dwb = lax.fori_loop(0, PIX // CH, mlp, (zero, zero, zero, zero))
+    s_gain, s_lnb, s_g, s_dwb = lax.fori_loop(0, PIX // CH, mlp, (zero, zero, zero, zero), unroll=2)
 
     small[...] = jnp.zeros_like(small)
     down = lambda v: jnp.sum(v, axis=0, keepdims=True)
@@ -219,7 +219,7 @@
                 return tuple(acc)
 
             none = jnp.zeros((8, 128), F32)
-            acc = lax.fori_loop(0, COLS // JB, taps, (none,) * (7 * len(group)))
+            acc = lax.fori_loop(0, COLS // JB, taps, (none,) * (7 * len(group)), unroll=4)
             for p, a in enumerate(group):
                 for b in range(7):
                     k = a * 7 + b

time: 106 us -> 103 us (0.972)
  Pallas kernels: 28.9 us -> 26.3 us
    pallas_call x1, Pallas kernels: 20.3 us -> 17.7 us  [run_main(): pl.pallas_call(main_kernel, out_shape=(jax.ShapeDtypeStruct((ROWS, COLS *...]
  transfers between devices with their start and end apart: 13 -> 13, of which waited for: 7 -> 7; matrix products, arithmetic and copies ran while one was open for 2% -> 2% of each run, Pallas kernels for 6% -> 7%
where the time goes in v10:
time: 103 us
  starting transfers between devices  45.9 us (45%)
  Pallas kernels  26.3 us (26%)
  waiting for transfers between devices  21.6 us (21%)
  other arithmetic  4.03 us (4%)
  local copies, waits for them, and re-layouts  3.77 us (4%)
    all_to_all x3, starting transfers between devices, exchange(): lax.all_to_all(x, ('ha', 'wa'), 0, 0, axis_index_groups=groups, tiled=True)  24.1 us
    pallas_call x1, Pallas kernels, run_main(): pl.pallas_call(main_kernel, out_shape=(jax.ShapeDtypeStruct((ROWS, COLS *...  17.7 us
    ppermute x2, waiting for transfers between devices, halo(): crossed = lax.ppermute(jnp.where(even, lead, last), 'ha', outer)  9.64 us
    ppermute x2, starting transfers between devices, halo(): crossed = lax.ppermute(jnp.where(even, lead, last), 'ha', outer)  7.94 us
    pallas_call x1, Pallas kernels, run_transposed(): pl.pallas_call(transposed_kernel, out_shape=jax.ShapeDtypeStruct((ROWS, C...  6.75 us
    all_to_all x3, waiting for transfers between devices, exchange(): lax.all_to_all(x, ('ha', 'wa'), 0, 0, axis_index_groups=groups, tiled=True)  6.67 us
    ppermute x2, starting transfers between devices, halo(): near = lax.ppermute(jnp.where(even, last, first), 'wa', inner)  6 us
    ppermute x1, starting transfers between devices, on_device(): other = lax.ppermute(mine, 'ha', swap)  3.67 us
  transfers between devices with their start and end apart: 13, of which 7 were waited for; matrix products, arithmetic and copies ran while one was open for 2% of the time, Pallas kernels for 7%

profile of v10, /device:TPU:1, one launch (start us, length us, event | category | flops | bytes accessed | tf_op | source)
XLA Modules:
  0.0 102.6 jit_solution(10518206925838898117)
XLA Ops:
  0.6 0.7 broadcast_select_fusion.10
  1.4 2.1 %collective-permute-start.1 = (bf16[8,768]{1,0:T(8,128)(2,1)S(1)}, bf16[8,768]{1,0:T(8,128)(2,1)S(1)}, u32[]{:S(2)}, u32[]{:S(2)}) collective-permute-start(bf16[8,768]{1,0:T(8,128)(2,1)S(1)} %get-tuple-element.68), channel_id=1, source_target_pairs={{0,1},{1,0},{2,3},{3,2},{4,5},{5,4},{6,7},{7,6},{8,9},{9,8},{10,11... | collective-permute-start | bytes 36872 | tf_op jit(solution)/shard_map/ppermute | solution.py:365
  3.5 0.8 collective-permute-start
  4.3 1.4 %fusion.1 = (bf16[3,32768]{1,0:T(4,128)(2,1)S(1)}, bf16[3,32768]{1,0:T(4,128)(2,1)S(1)}) fusion(bf16[8,32768]{1,0:T(8,128)(2,1)} %own.1), kind=kLoop, calls=%fused_computation.20 | loop fusion | bytes 786432 | tf_op jit(solution)/shard_map/slice | solution.py:373
  5.7 0.0 collective-permute-done.1
  5.8 0.0 copy-start.2
  5.8 0.3 broadcast_select_fusion.3
  6.1 4.4 %collective-permute-start.2 = (bf16[3,34304]{1,0:T(4,128)(2,1)S(1)}, bf16[3,34304]{1,0:T(4,128)(2,1)}, u32[]{:S(2)}, u32[]{:S(2)}) collective-permute-start(bf16[3,34304]{1,0:T(4,128)(2,1)S(1)} %get-tuple-element.60), channel_id=1, source_target_pairs={{8,16},{16,8},{24,32},{32,24},{40,48},{48,40},{56,64},{64,56},{72,... | collective-permute-start | bytes 617480 | tf_op jit(solution)/shard_map/ppermute | solution.py:374
  10.5 0.1 collective-permute-start.3
  10.6 0.2 copy.24
  10.8 0.0 copy-start
  10.8 0.0 copy-start.1
  10.8 0.0 copy-start.3
  10.8 0.0 copy-start.4
  10.9 0.0 copy-start.5
  10.9 0.0 copy-start.6
  10.9 0.0 copy-start.7
  10.9 0.0 copy-start.8
  10.9 0.0 copy-start.9
  10.9 0.2 copy.23
  11.1 3.6 %collective-permute-done.2 = bf16[3,34304]{1,0:T(4,128)(2,1)} collective-permute-done((bf16[3,34304]{1,0:T(4,128)(2,1)S(1)}, bf16[3,34304]{1,0:T(4,128)(2,1)}, u32[]{:S(2)}, u32[]{:S(2)}) %collective-permute-start.2) | collective-permute-done | bytes 205856 | tf_op jit(solution)/shard_map/ppermute | solution.py:374
  14.8 1.3 %pad_maximum_fusion.rows = bf16[6,34304]{1,0:T(8,128)(2,1)S(1)} fusion(bf16[3,34304]{1,0:T(4,128)(2,1)} %collective-permute-done.3, bf16[3,34304]{1,0:T(4,128)(2,1)} %collective-permute-done.2), kind=kLoop, calls=%fused_computation.1 | loop fusion | flops 823296 | bytes 823296 | tf_op jit(solution)/shard_map/concatenate | solution.py:378
  16.2 17.7 %block_backward.1 = (bf16[8,32768]{1,0:T(8,128)(2,1)S(1)}, bf16[16,72,256]{2,1,0:T(8,128)(2,1)S(1)}, bf16[16,72,256]{2,1,0:T(8,128)(2,1)S(1)}) custom-call(s32[1]{0:T(128)} %bitcast.core, bf16[8,32768]{1,0:T(8,128)(2,1)S(1)} %copy-done, bf16[8,768]{1,0:T(8,128)(2,1)S(1)} %get-tuple-element.73.left, bf16[8,768]{1,0:T(8,128)(2,1)S(1)} %get-tuple-element.72.right, ...), custom_call_target="tpu_custom_call" | custom-call | tf_op jit(solution)/shard_map/block_backward/pallas_call | solution.py:293
  33.9 0.1 collective-permute-start.4
  34.0 2.0 %collective-permute-done.4 = bf16[16,72,256]{2,1,0:T(8,128)(2,1)S(1)} collective-permute-done((bf16[16,72,256]{2,1,0:T(8,128)(2,1)S(1)}, bf16[16,72,256]{2,1,0:T(8,128)(2,1)S(1)}, u32[]{:S(2)}, u32[]{:S(2)}) %collective-permute-start.4) | collective-permute-done | bytes 589856 | tf_op jit(solution)/shard_map/ppermute | solution.py:414
  36.0 1.0 add_convert_fusion
  37.0 13.2 %all-to-all-start = ((bf16[16,72,256]{2,1,0:T(8,128)(2,1)}), bf16[16,72,256]{2,1,0:T(8,128)(2,1)S(1)}, u32[]{:S(2)}, u32[]{:S(2)}) async-start(bf16[16,72,256]{2,1,0:T(8,128)(2,1)} %add_convert_fusion), calls=%async_computation | async-start | bytes 1179648 | tf_op jit(solution)/shard_map/all_to_all | solution.py:408
  50.2 0.7 collective-permute-start.6
  50.9 3.9 %collective-permute-start.5 = (bf16[8,768]{1,0:T(8,128)(2,1)S(1)}, bf16[8,768]{1,0:T(8,128)(2,1)S(1)}, u32[]{:S(2)}, u32[]{:S(2)}) collective-permute-start(bf16[8,768]{1,0:T(8,128)(2,1)S(1)} %get-tuple-element.65), channel_id=1, source_target_pairs={{0,1},{1,0},{2,3},{3,2},{4,5},{5,4},{6,7},{7,6},{8,9},{9,8},{10,11... | collective-permute-start | bytes 36872 | tf_op jit(solution)/shard_map/ppermute | solution.py:365
  54.8 0.2 fusion
  55.0 1.7 %collective-permute-done.5 = bf16[8,768]{1,0:T(8,128)(2,1)S(1)} collective-permute-done((bf16[8,768]{1,0:T(8,128)(2,1)S(1)}, bf16[8,768]{1,0:T(8,128)(2,1)S(1)}, u32[]{:S(2)}, u32[]{:S(2)}) %collective-permute-start.5) | collective-permute-done | bytes 12320 | tf_op jit(solution)/shard_map/ppermute | solution.py:365
  56.6 4.2 %all-to-all-done = bf16[16,72,256]{2,1,0:T(8,128)(2,1)S(1)} async-done(((bf16[16,72,256]{2,1,0:T(8,128)(2,1)}), bf16[16,72,256]{2,1,0:T(8,128)(2,1)S(1)}, u32[]{:S(2)}, u32[]{:S(2)}) %all-to-all-start) | async-done | bytes 589856 | tf_op jit(solution)/shard_map/all_to_all | solution.py:408
  60.9 0.1 reduce_sum.24
  61.0 0.7 broadcast_in_dim.4
  61.7 7.3 %all-to-all-start.1 = ((bf16[8,72,256]{2,1,0:T(8,128)(2,1)}), bf16[8,72,256]{2,1,0:T(8,128)(2,1)S(1)}, u32[]{:S(2)}, u32[]{:S(2)}) async-start(bf16[8,72,256]{2,1,0:T(8,128)(2,1)} %broadcast_in_dim.4), calls=%async_computation.1 | async-start | bytes 589824 | tf_op jit(solution)/shard_map/all_to_all | solution.py:408
  69.0 0.3 broadcast_select_fusion
  69.3 2.5 %collective-permute-start.8 = (bf16[3,34304]{1,0:T(4,128)(2,1)S(1)}, bf16[3,34304]{1,0:T(4,128)(2,1)S(1)}, u32[]{:S(2)}, u32[]{:S(2)}) collective-permute-start(bf16[3,34304]{1,0:T(4,128)(2,1)S(1)} %get-tuple-element.58), channel_id=1, source_target_pairs={{0,8},{8,0},{16,24},{24,16},{32,40},{40,32},{48,56},{56,48},{64,72... | collective-permute-start | bytes 617480 | tf_op jit(solution)/shard_map/ppermute | solution.py:375
  71.8 3.5 %collective-permute-start.7 = (bf16[3,34304]{1,0:T(4,128)(2,1)S(1)}, bf16[3,34304]{1,0:T(4,128)(2,1)S(1)}, u32[]{:S(2)}, u32[]{:S(2)}) collective-permute-start(bf16[3,34304]{1,0:T(4,128)(2,1)S(1)} %get-tuple-element.59), channel_id=1, source_target_pairs={{8,16},{16,8},{24,32},{32,24},{40,48},{48,40},{56,64},{64,56},{72,... | collective-permute-start | bytes 617480 | tf_op jit(solution)/shard_map/ppermute | solution.py:374
  75.4 6.0 %collective-permute-done.7 = bf16[3,34304]{1,0:T(4,128)(2,1)S(1)} collective-permute-done((bf16[3,34304]{1,0:T(4,128)(2,1)S(1)}, bf16[3,34304]{1,0:T(4,128)(2,1)S(1)}, u32[]{:S(2)}, u32[]{:S(2)}) %collective-permute-start.7) | collective-permute-done | bytes 205856 | tf_op jit(solution)/shard_map/ppermute | solution.py:374
  81.4 0.3 pad_maximum_fusion.1.rows
  81.8 0.9 broadcast_in_dim.5
  82.6 3.6 %all-to-all-start.2 = ((bf16[16,72,256]{2,1,0:T(8,128)(2,1)}), bf16[16,72,256]{2,1,0:T(8,128)(2,1)S(1)}, u32[]{:S(2)}, u32[]{:S(2)}) async-start(bf16[16,72,256]{2,1,0:T(8,128)(2,1)} %broadcast_in_dim.5), calls=%async_computation.2 | async-start | bytes 1179648 | tf_op jit(solution)/shard_map/all_to_all | solution.py:408
  86.2 0.1 rev.3.dww
  86.3 6.8 %transposed_conv.1 = bf16[8,32768]{1,0:T(8,128)(2,1)} custom-call(s32[1]{0:T(128)} %bitcast.core, bf16[8,32768]{1,0:T(8,128)(2,1)S(1)} %get-tuple-element.38.own, bf16[8,768]{1,0:T(8,128)(2,1)S(1)} %get-tuple-element.44.left, bf16[8,768]{1,0:T(8,128)(2,1)S(1)} %get-tuple-element.45.right, bf16[6,34304]{1,0:T(8,128)(2,1)S(1)} %pad_maximum_fusion.1.rows, ...), custom_call_target="tpu_custom_call" | custom-call | flops 200000000 | bytes 41943040 | tf_op jit(solution)/shard_map/transposed_conv/pallas_call | solution.py:325
  93.1 2.4 %all-to-all-done.2.mine = bf16[16,72,256]{2,1,0:T(8,128)(2,1)S(1)} async-done(((bf16[16,72,256]{2,1,0:T(8,128)(2,1)}), bf16[16,72,256]{2,1,0:T(8,128)(2,1)S(1)}, u32[]{:S(2)}, u32[]{:S(2)}) %all-to-all-start.2) | async-done | bytes 589856 | tf_op jit(solution)/shard_map/all_to_all | solution.py:408
  95.5 3.7 %collective-permute-start.9 = (bf16[16,72,256]{2,1,0:T(8,128)(2,1)S(1)}, bf16[16,72,256]{2,1,0:T(8,128)(2,1)S(1)}, u32[]{:S(2)}, u32[]{:S(2)}) collective-permute-start(bf16[16,72,256]{2,1,0:T(8,128)(2,1)S(1)} %all-to-all-done.2.mine), channel_id=1, source_target_pairs={{0,8},{8,0},{16,24},{24,16},{32,40},{40,32},{48,56},{56,48},{64,72... | collective-permute-start | bytes 1769480 | tf_op jit(solution)/shard_map/ppermute | solution.py:426
  99.2 1.6 %collective-permute-done.9.other = bf16[16,72,256]{2,1,0:T(8,128)(2,1)S(1)} collective-permute-done((bf16[16,72,256]{2,1,0:T(8,128)(2,1)S(1)}, bf16[16,72,256]{2,1,0:T(8,128)(2,1)S(1)}, u32[]{:S(2)}, u32[]{:S(2)}) %collective-permute-start.9) | collective-permute-done | bytes 589856 | tf_op jit(solution)/shard_map/ppermute | solution.py:426
  100.8 1.8 %clip.1 = (f32[49,256]{1,0:T(8,128)}, f32[1,256]{1,0:T(1,128)}, f32[1,256]{1,0:T(1,128)}, f32[1,256]{1,0:T(1,128)}, f32[256,1024]{1,0:T(8,128)}, /*index=5*/f32[...) custom-call(s32[1]{0:T(128)} %bitcast.core, bf16[16,72,256]{2,1,0:T(8,128)(2,1)S(1)} %all-to-all-done.2.mine, ...), custom_call_target="tpu_custom_call" | custom-call | tf_op jit(solution)/shard_map/clip/pallas_call | solution.py:340
  (24 shorter events, 0.1 us)
Async XLA Ops:
  1.4 4.3 %collective-permute-start.1 = (bf16[8,768]{1,0:T(8,128)(2,1)S(1)}, bf16[8,768]{1,0:T(8,128)(2,1)S(1)}, u32[]{:S(2)}, u32[]{:S(2)}) collective-permute-start(bf16[8,768]{1,0:T(8,128)(2,1)S(1)} %get-tuple-element.68), channel_id=1, source_target_pairs={{0,1},{1,0},{2,3},{3,2},{4,5},{5,4},{6,7},{7,6},{8,9},{9,8},{10,11... | collective-permute-start | bytes 36872 | tf_op jit(solution)/shard_map/ppermute | solution.py:365
  3.5 7.1 %copy-start.10 = (bf16[1024,256]{1,0:T(8,128)(2,1)S(1)}, bf16[1024,256]{1,0:T(8,128)(2,1)}, u32[]{:S(2)}) copy-start(bf16[1024,256]{1,0:T(8,128)(2,1)} %param.19) | copy-start | bytes 1572868
  3.5 2.2 %collective-permute-start = (bf16[8,768]{1,0:T(8,128)(2,1)S(1)}, bf16[8,768]{1,0:T(8,128)(2,1)S(1)}, u32[]{:S(2)}, u32[]{:S(2)}) collective-permute-start(bf16[8,768]{1,0:T(8,128)(2,1)S(1)} %get-tuple-element.69), channel_id=1, source_target_pairs={{1,2},{2,1},{3,4},{4,3},{5,6},{6,5},{9,10},{10,9},{11,12},{12,11},... | collective-permute-start | bytes 36872 | tf_op jit(solution)/shard_map/ppermute | solution.py:366
  5.8 5.0 %copy-start.2 = (bf16[256,1024]{1,0:T(8,128)(2,1)S(1)}, bf16[256,1024]{1,0:T(8,128)(2,1)}, u32[]{:S(2)}) copy-start(bf16[256,1024]{1,0:T(8,128)(2,1)} %w_in.1) | copy-start | bytes 1572868
  6.1 8.7 %collective-permute-start.2 = (bf16[3,34304]{1,0:T(4,128)(2,1)S(1)}, bf16[3,34304]{1,0:T(4,128)(2,1)}, u32[]{:S(2)}, u32[]{:S(2)}) collective-permute-start(bf16[3,34304]{1,0:T(4,128)(2,1)S(1)} %get-tuple-element.60), channel_id=1, source_target_pairs={{8,16},{16,8},{24,32},{32,24},{40,48},{48,40},{56,64},{64,56},{72,... | collective-permute-start | bytes 617480 | tf_op jit(solution)/shard_map/ppermute | solution.py:374
  10.5 4.3 %collective-permute-start.3 = (bf16[3,34304]{1,0:T(4,128)(2,1)S(1)}, bf16[3,34304]{1,0:T(4,128)(2,1)}, u32[]{:S(2)}, u32[]{:S(2)}) collective-permute-start(bf16[3,34304]{1,0:T(4,128)(2,1)S(1)} %get-tuple-element.61), channel_id=1, source_target_pairs={{0,8},{8,0},{16,24},{24,16},{32,40},{40,32},{48,56},{56,48},{64,72... | collective-permute-start | bytes 617480 | tf_op jit(solution)/shard_map/ppermute | solution.py:375
  10.8 5.3 %copy-start = (bf16[8,32768]{1,0:T(8,128)(2,1)S(1)}, bf16[8,32768]{1,0:T(8,128)(2,1)}, u32[]{:S(2)}) copy-start(bf16[8,32768]{1,0:T(8,128)(2,1)} %own.1) | copy-start | bytes 1572868
  10.8 5.3 %copy-start.1 = (bf16[8,32768]{1,0:T(8,128)(2,1)S(1)}, bf16[8,32768]{1,0:T(8,128)(2,1)}, u32[]{:S(2)}) copy-start(bf16[8,32768]{1,0:T(8,128)(2,1)} %grad.3) | copy-start | bytes 1572868
  10.8 5.3 %copy-start.3 = (f32[49,256]{1,0:T(8,128)S(1)}, f32[49,256]{1,0:T(8,128)}, u32[]{:S(2)}) copy-start(f32[49,256]{1,0:T(8,128)} %dww.1) | copy-start | bytes 150532
  10.8 5.3 %copy-start.4 = (f32[1024]{0:T(1024)S(1)}, f32[1024]{0:T(1024)}, u32[]{:S(2)}) copy-start(f32[1024]{0:T(1024)} %param.18) | copy-start | bytes 12292
  10.9 5.3 %copy-start.5 = (f32[256]{0:T(256)S(1)}, f32[256]{0:T(256)}, u32[]{:S(2)}) copy-start(f32[256]{0:T(256)} %param.14) | copy-start | bytes 3076
  10.9 5.2 %copy-start.6 = (f32[256]{0:T(256)S(1)}, f32[256]{0:T(256)}, u32[]{:S(2)}) copy-start(f32[256]{0:T(256)} %param.15) | copy-start | bytes 3076
  10.9 5.2 %copy-start.7 = (f32[256]{0:T(256)S(1)}, f32[256]{0:T(256)}, u32[]{:S(2)}) copy-start(f32[256]{0:T(256)} %param.16) | copy-start | bytes 3076
  10.9 5.2 %copy-start.8 = (f32[256]{0:T(256)S(1)}, f32[256]{0:T(256)}, u32[]{:S(2)}) copy-start(f32[256]{0:T(256)} %param.20) | copy-start | bytes 3076
  10.9 5.2 %copy-start.9 = (f32[256]{0:T(256)S(1)}, f32[256]{0:T(256)}, u32[]{:S(2)}) copy-start(f32[256]{0:T(256)} %param.21) | copy-start | bytes 3076
  33.9 2.1 %collective-permute-start.4 = (bf16[16,72,256]{2,1,0:T(8,128)(2,1)S(1)}, bf16[16,72,256]{2,1,0:T(8,128)(2,1)S(1)}, u32[]{:S(2)}, u32[]{:S(2)}) collective-permute-start(bf16[16,72,256]{2,1,0:T(8,128)(2,1)S(1)} %get-tuple-element.35), channel_id=1, source_target_pairs={{0,8},{8,0},{16,24},{24,16},{32,40},{40,32},{48,56},{56,48},{64,72... | collective-permute-start | bytes 1769480 | tf_op jit(solution)/shard_map/ppermute | solution.py:414
  37.0 23.9 %all-to-all-start = ((bf16[16,72,256]{2,1,0:T(8,128)(2,1)}), bf16[16,72,256]{2,1,0:T(8,128)(2,1)S(1)}, u32[]{:S(2)}, u32[]{:S(2)}) async-start(bf16[16,72,256]{2,1,0:T(8,128)(2,1)} %add_convert_fusion), calls=%async_computation | async-start | bytes 1179648 | tf_op jit(solution)/shard_map/all_to_all | solution.py:408
  50.2 4.7 %collective-permute-start.6 = (bf16[8,768]{1,0:T(8,128)(2,1)S(1)}, bf16[8,768]{1,0:T(8,128)(2,1)S(1)}, u32[]{:S(2)}, u32[]{:S(2)}) collective-permute-start(bf16[8,768]{1,0:T(8,128)(2,1)S(1)} %get-tuple-element.64), channel_id=1, source_target_pairs={{1,2},{2,1},{3,4},{4,3},{5,6},{6,5},{9,10},{10,9},{11,12},{12,11},... | collective-permute-start | bytes 36872 | tf_op jit(solution)/shard_map/ppermute | solution.py:366
  50.9 5.7 %collective-permute-start.5 = (bf16[8,768]{1,0:T(8,128)(2,1)S(1)}, bf16[8,768]{1,0:T(8,128)(2,1)S(1)}, u32[]{:S(2)}, u32[]{:S(2)}) collective-permute-start(bf16[8,768]{1,0:T(8,128)(2,1)S(1)} %get-tuple-element.65), channel_id=1, source_target_pairs={{0,1},{1,0},{2,3},{3,2},{4,5},{5,4},{6,7},{7,6},{8,9},{9,8},{10,11... | collective-permute-start | bytes 36872 | tf_op jit(solution)/shard_map/ppermute | solution.py:365
  61.7 19.7 %all-to-all-start.1 = ((bf16[8,72,256]{2,1,0:T(8,128)(2,1)}), bf16[8,72,256]{2,1,0:T(8,128)(2,1)S(1)}, u32[]{:S(2)}, u32[]{:S(2)}) async-start(bf16[8,72,256]{2,1,0:T(8,128)(2,1)} %broadcast_in_dim.4), calls=%async_computation.1 | async-start | bytes 589824 | tf_op jit(solution)/shard_map/all_to_all | solution.py:408
  69.3 6.1 %collective-permute-start.8 = (bf16[3,34304]{1,0:T(4,128)(2,1)S(1)}, bf16[3,34304]{1,0:T(4,128)(2,1)S(1)}, u32[]{:S(2)}, u32[]{:S(2)}) collective-permute-start(bf16[3,34304]{1,0:T(4,128)(2,1)S(1)} %get-tuple-element.58), channel_id=1, source_target_pairs={{0,8},{8,0},{16,24},{24,16},{32,40},{40,32},{48,56},{56,48},{64,72... | collective-permute-start | bytes 617480 | tf_op jit(solution)/shard_map/ppermute | solution.py:375
  71.8 9.6 %collective-permute-start.7 = (bf16[3,34304]{1,0:T(4,128)(2,1)S(1)}, bf16[3,34304]{1,0:T(4,128)(2,1)S(1)}, u32[]{:S(2)}, u32[]{:S(2)}) collective-permute-start(bf16[3,34304]{1,0:T(4,128)(2,1)S(1)} %get-tuple-element.59), channel_id=1, source_target_pairs={{8,16},{16,8},{24,32},{32,24},{40,48},{48,40},{56,64},{64,56},{72,... | collective-permute-start | bytes 617480 | tf_op jit(solution)/shard_map/ppermute | solution.py:374
  82.6 12.9 %all-to-all-start.2 = ((bf16[16,72,256]{2,1,0:T(8,128)(2,1)}), bf16[16,72,256]{2,1,0:T(8,128)(2,1)S(1)}, u32[]{:S(2)}, u32[]{:S(2)}) async-start(bf16[16,72,256]{2,1,0:T(8,128)(2,1)} %broadcast_in_dim.5), calls=%async_computation.2 | async-start | bytes 1179648 | tf_op jit(solution)/shard_map/all_to_all | solution.py:408
  95.5 5.3 %collective-permute-start.9 = (bf16[16,72,256]{2,1,0:T(8,128)(2,1)S(1)}, bf16[16,72,256]{2,1,0:T(8,128)(2,1)S(1)}, u32[]{:S(2)}, u32[]{:S(2)}) collective-permute-start(bf16[16,72,256]{2,1,0:T(8,128)(2,1)S(1)} %all-to-all-done.2.mine), channel_id=1, source_target_pairs={{0,8},{8,0},{16,24},{24,16},{32,40},{40,32},{48,56},{56,48},{64,72... | collective-permute-start | bytes 1769480 | tf_op jit(solution)/shard_map/ppermute | solution.py:426
